TPU v7x, 32 devices: a whole 2x2x4 slice. The times are simulated.
32 devices in a mesh: seq: 8 (over z, x), dp: 4 (over y, core).
Axes of the slice: x: 2, y: 2, z: 4, core: 2. Of those that a mesh axis runs over, the one named last changes fastest.
Arguments:
- tokens: bfloat16 [4, 2048, 1024], P('dp', 'seq'), may hold values from -6 to 6
- attn_gain: bfloat16 [1024], P(('seq', 'dp')), may hold values from 0.5 to 1.5
- q_weight: bfloat16 [1024, 1024], P(('seq', 'dp')), may hold values from -0.1875 to 0.1875
- k_weight: bfloat16 [1024, 512], P(('seq', 'dp')), may hold values from -0.1875 to 0.1875
- v_weight: bfloat16 [1024, 512], P(('seq', 'dp')), may hold values from -0.1875 to 0.1875
- q_norm_gain: bfloat16 [64], replicated, may hold values from 0.25 to 1.75
- k_norm_gain: bfloat16 [64], replicated, may hold values from 0.25 to 1.75
- o_weight: bfloat16 [1024, 1024], P(('seq', 'dp')), may hold values from -1 to 1
- ffn_gain: bfloat16 [1024], P(('seq', 'dp')), may hold values from 0.5 to 1.5
- gate_weight: bfloat16 [1024, 4608], P(('seq', 'dp')), may hold values from -0.1875 to 0.1875
- up_weight: bfloat16 [1024, 4608], P(('seq', 'dp')), may hold values from -0.1875 to 0.1875
- down_weight: bfloat16 [4608, 1024], P(('seq', 'dp')), may hold values from -0.09375 to 0.09375
- doc_lengths: int32 [4, 4], P('dp'), may hold values from 1 to 2048, as said below
- cotangent: bfloat16 [4, 2048, 1024], P('dp', 'seq'), may hold values from -6 to 6
Outputs:
- output: bfloat16 [4, 2048, 1024], P('dp', 'seq')
- input_grad: float32 [4, 2048, 1024], P('dp', 'seq')
- attn_gain_grad: float32 [1024], P(('seq', 'dp'))
- q_weight_grad: float32 [1024, 1024], P(('seq', 'dp'))
- k_weight_grad: float32 [1024, 512], P(('seq', 'dp'))
- v_weight_grad: float32 [1024, 512], P(('seq', 'dp'))
- q_norm_gain_grad: float32 [64], replicated
- k_norm_gain_grad: float32 [64], replicated
- o_weight_grad: float32 [1024, 1024], P(('seq', 'dp'))
- ffn_gain_grad: float32 [1024], P(('seq', 'dp'))
- gate_weight_grad: float32 [1024, 4608], P(('seq', 'dp'))
- up_weight_grad: float32 [1024, 4608], P(('seq', 'dp'))
- down_weight_grad: float32 [4608, 1024], P(('seq', 'dp'))
Inputs may be any that keep to these rules, and one draw needn't show every extreme that they name: `doc_lengths`: in each pack the 4 lengths sum to 2048; all of them but one are at most 64, and that value is reached in every pack.
All inputs are finite; a program needn't handle non-finite values.
Results may differ from a plain program's by a relative error of at most 0.018.
Values may be sent and summed in bfloat16 or wider, within the bound.
No kernel may reach another device: no remote copies, remote signals or barrier semaphores. Data moves between devices by JAX's collectives and lax.ppermute only.
A program may use at most 384 MiB of HBM per device.

v0:
```python
import jax
import jax.numpy as jnp
from jax import lax
from jax.sharding import PartitionSpec as P

EPS = 1e-05
THETA = 1000000.0
NEG = -1e30


def passed_along(array, axis, by):
    count = lax.axis_size(axis)
    pairs = [(i, i + by) for i in range(count) if 0 <= i + by < count]
    return lax.ppermute(array, axis, pairs)


def shifted(array, axis, by):
    count = lax.axis_size(axis)
    return lax.ppermute(array, axis, [(i, (i + by) % count) for i in range(count)])


def product(left, right):
    return jnp.dot(left, right, preferred_element_type=jnp.float32)


def rms_scale(values, gain):
    return values * lax.rsqrt(jnp.mean(values * values, axis=-1, keepdims=True) + EPS) * gain


def rotate(values, cosine, sine):
    half = values.shape[-1] // 2
    first = values[..., :half]
    second = values[..., half:]
    return jnp.concatenate(
        [first * cosine - second * sine, second * cosine + first * sine], axis=-1
    )


def prepare(pre, gain, cosine, sine):
    heads = pre.reshape(pre.shape[0], -1, gain.shape[0])
    return rotate(rms_scale(heads, gain), cosine[:, None, :], sine[:, None, :])


def on_device(
    tokens,
    attn_gain,
    q_weight,
    k_weight,
    v_weight,
    q_norm_gain,
    k_norm_gain,
    o_weight,
    ffn_gain,
    gate_weight,
    up_weight,
    down_weight,
    doc_lengths,
    cotangent,
):
    rows = tokens.shape[1]
    head_dim = q_norm_gain.shape[0]
    scale = head_dim ** (-0.5)
    cycle_size = lax.axis_size("seq")
    here = lax.axis_index("seq")
    lengths = doc_lengths[0]
    ends = jnp.cumsum(lengths)
    starts = ends - lengths
    place = here * rows + jnp.arange(rows, dtype=jnp.int32)

    def doc_of(positions):
        return jnp.sum((positions[:, None] >= ends[None, :]).astype(jnp.int32), axis=1)

    query_doc = doc_of(place)
    labels = jnp.arange(lengths.shape[0], dtype=jnp.int32)
    begin = jnp.sum(jnp.where(query_doc[:, None] == labels[None, :], starts[None, :], 0), axis=1)
    offset = (place - begin).astype(jnp.float32)
    freqs = THETA ** (-jnp.arange(head_dim // 2, dtype=jnp.float32) * 2.0 / head_dim)
    angles = offset[:, None] * freqs[None, :]
    cosine = jnp.cos(angles)
    sine = jnp.sin(angles)
    g_attn, w_query, w_key, w_value, w_out, g_ffn, w_gate, w_up, w_down = (
        lax.all_gather(attn_gain, ("seq", "dp"), axis=0, tiled=True),
        lax.all_gather(q_weight, ("seq", "dp"), axis=0, tiled=True),
        lax.all_gather(k_weight, ("seq", "dp"), axis=0, tiled=True),
        lax.all_gather(v_weight, ("seq", "dp"), axis=0, tiled=True),
        lax.all_gather(o_weight, ("seq", "dp"), axis=0, tiled=True),
        lax.all_gather(ffn_gain, ("seq", "dp"), axis=0, tiled=True),
        lax.all_gather(gate_weight, ("seq", "dp"), axis=0, tiled=True),
        lax.all_gather(up_weight, ("seq", "dp"), axis=0, tiled=True),
        lax.all_gather(down_weight, ("seq", "dp"), axis=0, tiled=True),
    )
    heads = w_query.shape[1] // head_dim
    kv_heads = w_key.shape[1] // head_dim
    groups = heads // kv_heads
    q_gain = q_norm_gain.astype(jnp.float32)
    k_gain = k_norm_gain.astype(jnp.float32)
    inputs = tokens[0].astype(jnp.float32)
    normed = rms_scale(inputs, g_attn.astype(jnp.float32)).astype(jnp.bfloat16)
    q_pre = product(normed, w_query)
    k_pre = product(normed, w_key)
    values = product(normed, w_value).astype(jnp.bfloat16)
    queries = prepare(q_pre, q_gain, cosine, sine).astype(jnp.bfloat16)
    keys = (
        prepare(k_pre, k_gain, cosine, sine).astype(jnp.bfloat16).reshape(rows, kv_heads * head_dim)
    )
    query_heads = queries.reshape(rows, kv_heads, groups, head_dim)

    def masked_scores(key_rows, start):
        count = key_rows.shape[0]
        key_heads = key_rows.reshape(count, kv_heads, head_dim)
        key_place = start + jnp.arange(count, dtype=jnp.int32)
        allowed = (query_doc[:, None] == doc_of(key_place)[None, :]) & (
            place[:, None] >= key_place[None, :]
        )
        raw = (
            jnp.einsum("tkgd,ukd->kgtu", query_heads, key_heads, preferred_element_type=jnp.float32)
            * scale
        )
        return (jnp.where(allowed, raw, NEG), allowed, key_heads)

    row_max = jnp.full((kv_heads, groups, rows), NEG, jnp.float32)
    key_rows = lax.all_gather(keys, "seq", axis=0, tiled=True)
    value_rows = lax.all_gather(values, "seq", axis=0, tiled=True)
    scores, allowed, key_heads = masked_scores(key_rows, jnp.int32(0))
    value_heads = value_rows.reshape(value_rows.shape[0], kv_heads, head_dim)
    new_max = jnp.maximum(row_max, jnp.max(scores, axis=-1))
    weights = jnp.exp(scores - new_max[..., None]) * allowed
    row_sum = jnp.sum(weights, axis=-1)
    weighted = jnp.einsum(
        "kgtu,ukd->kgtd",
        weights.astype(jnp.bfloat16),
        value_heads,
        preferred_element_type=jnp.float32,
    )
    row_max, row_sum, weighted = (new_max, row_sum, weighted)
    attn_heads = jnp.transpose(weighted / row_sum[..., None], (2, 0, 1, 3))
    attn = attn_heads.reshape(rows, heads * head_dim)
    attn_b = attn.astype(jnp.bfloat16)
    hidden = inputs + product(attn_b, w_out)
    ffn_gain32 = g_ffn.astype(jnp.float32)
    normed_two = rms_scale(hidden, ffn_gain32).astype(jnp.bfloat16)
    gate_proj = product(normed_two, w_gate)
    up_proj = product(normed_two, w_up)
    activated = (jax.nn.silu(gate_proj) * up_proj).astype(jnp.bfloat16)
    result = hidden + product(activated, w_down)
    output = result.astype(jnp.bfloat16)[None]
    g_attn, w_query, w_key, w_value, w_out, g_ffn, w_gate, w_up, w_down = (
        lax.all_gather(attn_gain, ("seq", "dp"), axis=0, tiled=True),
        lax.all_gather(q_weight, ("seq", "dp"), axis=0, tiled=True),
        lax.all_gather(k_weight, ("seq", "dp"), axis=0, tiled=True),
        lax.all_gather(v_weight, ("seq", "dp"), axis=0, tiled=True),
        lax.all_gather(o_weight, ("seq", "dp"), axis=0, tiled=True),
        lax.all_gather(ffn_gain, ("seq", "dp"), axis=0, tiled=True),
        lax.all_gather(gate_weight, ("seq", "dp"), axis=0, tiled=True),
        lax.all_gather(up_weight, ("seq", "dp"), axis=0, tiled=True),
        lax.all_gather(down_weight, ("seq", "dp"), axis=0, tiled=True),
    )
    grad_out = cotangent[0]
    d_act = product(grad_out, w_down.T)
    down_grad = product(activated.T, grad_out)
    _, act_pull = jax.vjp(lambda left, right: jax.nn.silu(left) * right, gate_proj, up_proj)
    d_gate, d_up = act_pull(d_act)
    d_gate = d_gate.astype(jnp.bfloat16)
    d_up = d_up.astype(jnp.bfloat16)
    gate_grad = product(normed_two.T, d_gate)
    up_grad = product(normed_two.T, d_up)
    d_normed_two = product(d_gate, w_gate.T) + product(d_up, w_up.T)
    _, norm_pull = jax.vjp(rms_scale, hidden, g_ffn.astype(jnp.float32))
    d_hidden_part, ffn_gain_grad = norm_pull(d_normed_two)
    d_hidden = grad_out.astype(jnp.float32) + d_hidden_part
    d_branch = d_hidden.astype(jnp.bfloat16)
    out_grad = product(attn_b.T, d_branch)
    d_attn = product(d_branch, w_out.T).astype(jnp.bfloat16)
    d_attn_heads = d_attn.reshape(rows, kv_heads, groups, head_dim)
    delta = jnp.einsum("tkgd,tkgd->kgt", d_attn_heads.astype(jnp.float32), attn_heads)
    log_total = row_max + jnp.log(row_sum)

    def visit(step, state):
        key_block, value_block, key_grad, value_grad, query_grad = state
        source = (here - step) % cycle_size
        scores, allowed, key_heads = masked_scores(key_block, source * rows)
        value_heads = value_block.reshape(rows, kv_heads, head_dim)
        probs = jnp.exp(scores - log_total[..., None]) * allowed
        d_probs = jnp.einsum(
            "tkgd,ukd->kgtu", d_attn_heads, value_heads, preferred_element_type=jnp.float32
        )
        d_scores = (probs * (d_probs - delta[..., None])).astype(jnp.bfloat16)
        query_grad = query_grad + jnp.einsum(
            "kgtu,ukd->tkgd", d_scores, key_heads, preferred_element_type=jnp.float32
        )
        key_grad = key_grad + jnp.einsum(
            "kgtu,tkgd->ukd", d_scores, query_heads, preferred_element_type=jnp.float32
        ).reshape(rows, -1)
        value_grad = value_grad + jnp.einsum(
            "kgtu,tkgd->ukd",
            probs.astype(jnp.bfloat16),
            d_attn_heads,
            preferred_element_type=jnp.float32,
        ).reshape(rows, -1)
        key_block, value_block = passed_along((key_block, value_block), "seq", 1)
        key_grad, value_grad = (
            shifted(key_grad.astype(jnp.bfloat16), "seq", 1).astype(key_grad.dtype),
            shifted(value_grad.astype(jnp.bfloat16), "seq", 1).astype(value_grad.dtype),
        )
        return (key_block, value_block, key_grad, value_grad, query_grad)

    zero_kv = jnp.zeros((rows, kv_heads * head_dim), jnp.float32)
    state = (
        keys,
        values,
        zero_kv,
        zero_kv,
        jnp.zeros((rows, kv_heads, groups, head_dim), jnp.float32),
    )
    _, _, key_grad, value_grad, query_grad = lax.fori_loop(0, cycle_size, visit, state)
    _, query_pull = jax.vjp(lambda pre, gain: prepare(pre, gain, cosine, sine), q_pre, q_gain)
    d_q_pre, q_gain_grad = query_pull((query_grad * scale).reshape(rows, heads, head_dim))
    _, key_pull = jax.vjp(lambda pre, gain: prepare(pre, gain, cosine, sine), k_pre, k_gain)
    d_k_pre, k_gain_grad = key_pull((key_grad * scale).reshape(rows, kv_heads, head_dim))
    d_q_pre = d_q_pre.astype(jnp.bfloat16)
    d_k_pre = d_k_pre.astype(jnp.bfloat16)
    d_v_pre = value_grad.astype(jnp.bfloat16)
    query_weight_grad = product(normed.T, d_q_pre)
    key_weight_grad = product(normed.T, d_k_pre)
    value_weight_grad = product(normed.T, d_v_pre)
    d_normed = product(d_q_pre, w_query.T) + product(d_k_pre, w_key.T) + product(d_v_pre, w_value.T)
    _, first_pull = jax.vjp(rms_scale, inputs, g_attn.astype(jnp.float32))
    d_input_part, attn_gain_grad = first_pull(d_normed)
    input_grad = (d_hidden + d_input_part)[None]
    q_gain_sum, k_gain_sum = lax.psum((q_gain_grad, k_gain_grad), ("seq", "dp"))
    shares = (
        lax.psum_scatter(attn_gain_grad, ("seq", "dp"), scatter_dimension=0, tiled=True),
        lax.psum_scatter(query_weight_grad, ("seq", "dp"), scatter_dimension=0, tiled=True),
        lax.psum_scatter(key_weight_grad, ("seq", "dp"), scatter_dimension=0, tiled=True),
        lax.psum_scatter(value_weight_grad, ("seq", "dp"), scatter_dimension=0, tiled=True),
        lax.psum_scatter(out_grad, ("seq", "dp"), scatter_dimension=0, tiled=True),
        lax.psum_scatter(ffn_gain_grad, ("seq", "dp"), scatter_dimension=0, tiled=True),
        lax.psum_scatter(gate_grad, ("seq", "dp"), scatter_dimension=0, tiled=True),
        lax.psum_scatter(up_grad, ("seq", "dp"), scatter_dimension=0, tiled=True),
        lax.psum_scatter(down_grad, ("seq", "dp"), scatter_dimension=0, tiled=True),
    )
    return (
        output,
        input_grad,
        shares[0],
        shares[1],
        shares[2],
        shares[3],
        q_gain_sum,
        k_gain_sum,
        shares[4],
        shares[5],
        shares[6],
        shares[7],
        shares[8],
    )


def solution(mesh):
    placed = (
        P("dp", "seq", None),
        P(("seq", "dp")),
        P(("seq", "dp"), None),
        P(("seq", "dp"), None),
        P(("seq", "dp"), None),
        P(),
        P(),
        P(("seq", "dp"), None),
        P(("seq", "dp")),
        P(("seq", "dp"), None),
        P(("seq", "dp"), None),
        P(("seq", "dp"), None),
        P("dp", None),
        P("dp", "seq", None),
    )
    return jax.shard_map(
        on_device,
        mesh=mesh,
        in_specs=placed,
        out_specs=(
            P("dp", "seq", None),
            P("dp", "seq", None),
            P(("seq", "dp")),
            P(("seq", "dp"), None),
            P(("seq", "dp"), None),
            P(("seq", "dp"), None),
            P(),
            P(),
            P(("seq", "dp"), None),
            P(("seq", "dp")),
            P(("seq", "dp"), None),
            P(("seq", "dp"), None),
            P(("seq", "dp"), None),
        ),
        check_vma=False,
    )
```

profile of v0, /device:TPU:0, one launch (start us, length us, event | category | flops | bytes accessed | tf_op | source)
XLA Modules:
  0.0 2049.5 jit_solution(17003371261047998453)
XLA Ops:
  11.2 42.0 %all-reduce.9 = (bf16[1024]{0:T(1024)(128)(2,1)S(1)}, bf16[1024]{0:T(1024)(128)(2,1)S(1)}) all-reduce(bf16[1024]{0:T(1024)(128)(2,1)S(1)} %dynamic-update-slice, bf16[1024]{0:T(1024)(128)(2,1)S(1)} %dynamic-update-slice.1), channel_id=1, replica_groups=mesh['seq'=8,'dp'=4] {'seq','dp'}, use_global_device_ids=true, to_apply=%add.4 | all-reduce | flops 2048 | bytes 8192
  54.6 12.9 all-gather.16.cloned.1.call-done
  72.7 50.3 %all-gather.10.cloned.1.call-done = bf16[1024,512]{1,0:T(8,128)(2,1)} async-done(((bf16[32,512]{1,0:T(8,128)(2,1)}), bf16[1024,512]{1,0:T(8,128)(2,1)}) %all-gather.10.cloned.1.call-update) | async-done | bytes 1048592 | tf_op jit(solution)/shard_map/all_gather | solution.py:84
  132.9 48.3 %all-gather.14.cloned.1.call-done = bf16[1024,1024]{1,0:T(8,128)(2,1)} async-done(((bf16[32,1024]{1,0:T(8,128)(2,1)}), bf16[1024,1024]{1,0:T(8,128)(2,1)}) %all-gather.14.cloned.1.call-update) | async-done | bytes 2097168 | tf_op jit(solution)/shard_map/all_gather | solution.py:83
  181.2 3.9 copy.58
  188.7 43.2 %all-gather.18.cloned.1.call-done = bf16[2048,512]{1,0:T(8,128)(2,1)} async-done(((bf16[256,512]{1,0:T(8,128)(2,1)}), bf16[2048,512]{1,0:T(8,128)(2,1)}) %all-gather.18.cloned.1.call-update) | async-done | bytes 2097168 | tf_op jit(solution)/shard_map/all_gather | solution.py:123
  231.9 3.9 copy.59
  235.8 47.6 %all-gather.12.cloned.1.call-done = bf16[2048,512]{0,1:T(8,128)(2,1)} async-done(((bf16[256,512]{0,1:T(8,128)(2,1)}), bf16[2048,512]{0,1:T(8,128)(2,1)}) %all-gather.12.cloned.1.call-update) | async-done | bytes 2097168 | tf_op jit(solution)/shard_map/all_gather | solution.py:122
  283.4 14.8 fusion.17
  298.3 14.8 fusion.18
  313.1 16.7 fusion.87
  329.8 10.9 all-gather.20.cloned.1.call-done
  344.0 80.6 %all-gather.22.cloned.1.call-done = bf16[1024,4608]{1,0:T(8,128)(2,1)} async-done(((bf16[32,4608]{1,0:T(8,128)(2,1)}), bf16[1024,4608]{1,0:T(8,128)(2,1)}) %all-gather.22.cloned.1.call-update) | async-done | bytes 9437200 | tf_op jit(solution)/shard_map/all_gather | solution.py:88
  424.6 8.1 fusion.90
  432.7 75.5 %all-gather.24.cloned.1.call-done = bf16[1024,4608]{1,0:T(8,128)(2,1)} async-done(((bf16[32,4608]{1,0:T(8,128)(2,1)}), bf16[1024,4608]{1,0:T(8,128)(2,1)}) %all-gather.24.cloned.1.call-update) | async-done | bytes 9437200 | tf_op jit(solution)/shard_map/all_gather | solution.py:89
  508.2 8.0 fusion.91
  516.2 75.6 %all-gather.26.cloned.1.call-done = bf16[4608,1024]{1,0:T(8,128)(2,1)} async-done(((bf16[144,1024]{1,0:T(8,128)(2,1)}), bf16[4608,1024]{1,0:T(8,128)(2,1)}) %all-gather.26.cloned.1.call-update) | async-done | bytes 9437200 | tf_op jit(solution)/shard_map/all_gather | solution.py:90
  591.8 13.7 multiply_convert_fusion
  605.5 6.9 fusion.92
  613.6 3.4 multiply_reduce_fusion
  621.3 230.3 %while.24 = (s32[]{:T(128)}, bf16[256,512]{0,1:T(8,128)(2,1)}, bf16[256,512]{0,1:T(8,128)(2,1)}, f32[256,512]{0,1:T(8,128)}, f32[256,512]{0,1:T(8,128)S(1)}, /*i...) while((s32[]{:T(128)}, bf16[256,512]{0,1:T(8,128)(2,1)}, ...), condition=%wide.region_13.14_spmd.clone, body=%wide.region_11.13_spmd.clone.sunk | while | flops 685509888 | bytes 37610052 | solution.py:215
  622.5 4.0 collective-permute-start
  628.2 3.4 collective-permute-start.1
  643.2 5.9 collective-permute-done.2
  674.6 4.7 collective-permute-done.2
  688.0 3.0 collective-permute-start.1
  704.0 3.9 collective-permute-done.2
  716.3 3.3 collective-permute-start.1
  732.5 3.4 collective-permute-done.2
  744.4 3.3 collective-permute-start.1
  760.6 3.2 collective-permute-done.2
  772.3 3.5 collective-permute-start.1
  788.7 3.1 collective-permute-done.2
  800.2 3.7 collective-permute-start.1
  828.1 3.8 collective-permute-start.1
  844.9 2.9 collective-permute-done.2
  867.5 9.6 fusion.94
  877.2 9.7 fusion.95
  887.9 9.9 fusion.54
  903.5 37.9 %all-reduce.8 = (f32[1024]{0:T(1024)S(1)}, f32[64]{0:T(128)}, f32[64]{0:T(128)}, f32[1024]{0:T(1024)S(1)}) all-reduce(f32[1024]{0:T(1024)S(1)} %get-tuple-element.457, f32[64]{0:T(128)S(1)} %get-tuple-element.455, f32[64]{0:T(128)S(1)} %copy-done.40, f32[1024]{0:T(1024)S(1)} %copy-done.39), channel_id=2, replica_groups=mesh['seq'=8,'dp'=4] {'seq','dp'}, use_global_device_ids=true, to_apply=%region_18.19.clone | all-reduce | flops 2176 | bytes 17408
  945.0 7.8 fusion.38
  952.8 39.9 %reduce-scatter.10.cloned.1.call-done = f32[32,512]{1,0:T(8,128)} async-done(((f32[1024,512]{1,0:T(8,128)}), f32[32,512]{1,0:T(8,128)}) %reduce-scatter.10.cloned.1.call-update) | async-done | bytes 65552 | tf_op jit(solution)/shard_map/reduce_scatter | solution.py:234
  992.7 135.6 %reduce-scatter.12.cloned.1.call-done = f32[32,512]{1,0:T(8,128)} async-done(((f32[1024,512]{1,0:T(8,128)}), f32[32,512]{1,0:T(8,128)}) %reduce-scatter.12.cloned.1.call-update) | async-done | bytes 65552 | tf_op jit(solution)/shard_map/reduce_scatter | solution.py:235
  1128.3 140.0 %reduce-scatter.8.cloned.1.call-done = f32[32,1024]{1,0:T(8,128)} async-done(((f32[1024,1024]{1,0:T(8,128)}), f32[32,1024]{1,0:T(8,128)}) %reduce-scatter.8.cloned.1.call-update) | async-done | bytes 131088 | tf_op jit(solution)/shard_map/reduce_scatter | solution.py:233
  1268.3 140.2 %reduce-scatter.14.cloned.1.call-done = f32[32,1024]{1,0:T(8,128)} async-done(((f32[1024,1024]{1,0:T(8,128)}), f32[32,1024]{1,0:T(8,128)}) %reduce-scatter.14.cloned.1.call-update) | async-done | bytes 131088 | tf_op jit(solution)/shard_map/reduce_scatter | solution.py:236
  1408.5 209.4 %reduce-scatter.16.cloned.1.call-done = f32[32,4608]{1,0:T(8,128)} async-done(((f32[1024,4608]{1,0:T(8,128)}), f32[32,4608]{1,0:T(8,128)}) %reduce-scatter.16.cloned.1.call-update) | async-done | bytes 589840 | tf_op jit(solution)/shard_map/reduce_scatter | solution.py:238
  1617.9 212.4 %reduce-scatter.18.cloned.1.call-done = f32[32,4608]{1,0:T(8,128)} async-done(((f32[1024,4608]{1,0:T(8,128)}), f32[32,4608]{1,0:T(8,128)}) %reduce-scatter.18.cloned.1.call-update) | async-done | bytes 589840 | tf_op jit(solution)/shard_map/reduce_scatter | solution.py:239
  1830.3 212.4 %reduce-scatter.20.cloned.1.call-done = f32[144,1024]{1,0:T(8,128)} async-done(((f32[4608,1024]{1,0:T(8,128)}), f32[144,1024]{1,0:T(8,128)}) %reduce-scatter.20.cloned.1.call-update) | async-done | bytes 589840 | tf_op jit(solution)/shard_map/reduce_scatter | solution.py:240
  (394 shorter events, 232.6 us)
Async XLA Ops:
  7.2 60.3 %all-gather.16.cloned.1.call-start = ((), (), s32[]{:S(2)}) async-start(), calls=%async_computation.10 | async-start | bytes 1081344 | tf_op jit(solution)/shard_map/all_gather | solution.py:85
  7.9 115.1 %all-gather.10.cloned.1.call-start = ((), (), s32[]{:S(2)}) async-start(), calls=%async_computation.7 | async-start | bytes 1081344 | tf_op jit(solution)/shard_map/all_gather | solution.py:84
  8.7 172.5 %all-gather.14.cloned.1.call-start = ((), (), s32[]{:S(2)}) async-start(), calls=%async_computation.9 | async-start | bytes 2162688 | tf_op jit(solution)/shard_map/all_gather | solution.py:83
  9.4 222.5 %all-gather.18.cloned.1.call-start = ((), (), s32[]{:S(2)}) async-start(), calls=%async_computation.11 | async-start | bytes 2359296 | tf_op jit(solution)/shard_map/all_gather | solution.py:123
  70.1 213.3 %all-gather.12.cloned.1.call-start = ((), (), s32[]{:S(2)}) async-start(), calls=%async_computation.8 | async-start | bytes 2359296 | tf_op jit(solution)/shard_map/all_gather | solution.py:122
  126.9 213.9 %all-gather.20.cloned.1.call-start = ((), (), s32[]{:S(2)}) async-start(), calls=%async_computation.12 | async-start | bytes 2162688 | tf_op jit(solution)/shard_map/all_gather | solution.py:86
  127.4 297.2 %all-gather.22.cloned.1.call-start = ((), (), s32[]{:S(2)}) async-start(), calls=%async_computation.13 | async-start | bytes 9732096 | tf_op jit(solution)/shard_map/all_gather | solution.py:88
  128.2 380.0 %all-gather.24.cloned.1.call-start = ((), (), s32[]{:S(2)}) async-start(), calls=%async_computation.14 | async-start | bytes 9732096 | tf_op jit(solution)/shard_map/all_gather | solution.py:89
  128.9 462.9 %all-gather.26.cloned.1.call-start = ((), (), s32[]{:S(2)}) async-start(), calls=%async_computation.15 | async-start | bytes 9732096 | tf_op jit(solution)/shard_map/all_gather | solution.py:90
  129.7 863.0 %reduce-scatter.10.cloned.1.call-start = ((), (), s32[]{:S(2)}) async-start(), calls=%async_computation.17 | async-start | bytes 2162688 | tf_op jit(solution)/shard_map/reduce_scatter | solution.py:234
  622.5 31.9 %collective-permute-start = (bf16[256,512]{0,1:T(8,128)(2,1)S(1)}, bf16[256,512]{0,1:T(8,128)(2,1)}, u32[]{:S(2)}, u32[]{:S(2)}) collective-permute-start(bf16[256,512]{0,1:T(8,128)(2,1)S(1)} %copy.91), channel_id=1, source_target_pairs={{0,4},{4,8},{8,12},{12,16},{16,20},{20,24},{24,28},{1,5},{5,9},{9,... | collective-permute-start | bytes 786440 | tf_op jit(solution)/shard_map/while/body/eval_jaxpr/ppermute | solution.py:14
  628.2 26.2 %collective-permute-start.1 = (bf16[256,512]{0,1:T(8,128)(2,1)}, bf16[256,512]{0,1:T(8,128)(2,1)}, u32[]{:S(2)}, u32[]{:S(2)}) collective-permute-start(bf16[256,512]{0,1:T(8,128)(2,1)} %copy.92), channel_id=1, source_target_pairs={{0,4},{4,8},{8,12},{12,16},{16,20},{20,24},{24,28},{1,5},{5,9},{9,... | collective-permute-start | bytes 786440 | tf_op jit(solution)/shard_map/while/body/eval_jaxpr/ppermute | solution.py:14
  636.8 12.2 collective-permute-start.2
  640.6 12.7 collective-permute-start.3
  655.4 28.0 %collective-permute-start = (bf16[256,512]{0,1:T(8,128)(2,1)S(1)}, bf16[256,512]{0,1:T(8,128)(2,1)}, u32[]{:S(2)}, u32[]{:S(2)}) collective-permute-start(bf16[256,512]{0,1:T(8,128)(2,1)S(1)} %copy.91), channel_id=1, source_target_pairs={{0,4},{4,8},{8,12},{12,16},{16,20},{20,24},{24,28},{1,5},{5,9},{9,... | collective-permute-start | bytes 786440 | tf_op jit(solution)/shard_map/while/body/eval_jaxpr/ppermute | solution.py:14
  659.0 24.3 %collective-permute-start.1 = (bf16[256,512]{0,1:T(8,128)(2,1)}, bf16[256,512]{0,1:T(8,128)(2,1)}, u32[]{:S(2)}, u32[]{:S(2)}) collective-permute-start(bf16[256,512]{0,1:T(8,128)(2,1)} %copy.92), channel_id=1, source_target_pairs={{0,4},{4,8},{8,12},{12,16},{16,20},{20,24},{24,28},{1,5},{5,9},{9,... | collective-permute-start | bytes 786440 | tf_op jit(solution)/shard_map/while/body/eval_jaxpr/ppermute | solution.py:14
  667.0 12.3 collective-permute-start.2
  670.0 12.3 collective-permute-start.3
  684.3 27.3 %collective-permute-start = (bf16[256,512]{0,1:T(8,128)(2,1)S(1)}, bf16[256,512]{0,1:T(8,128)(2,1)}, u32[]{:S(2)}, u32[]{:S(2)}) collective-permute-start(bf16[256,512]{0,1:T(8,128)(2,1)S(1)} %copy.91), channel_id=1, source_target_pairs={{0,4},{4,8},{8,12},{12,16},{16,20},{20,24},{24,28},{1,5},{5,9},{9,... | collective-permute-start | bytes 786440 | tf_op jit(solution)/shard_map/while/body/eval_jaxpr/ppermute | solution.py:14
  688.0 23.7 %collective-permute-start.1 = (bf16[256,512]{0,1:T(8,128)(2,1)}, bf16[256,512]{0,1:T(8,128)(2,1)}, u32[]{:S(2)}, u32[]{:S(2)}) collective-permute-start(bf16[256,512]{0,1:T(8,128)(2,1)} %copy.92), channel_id=1, source_target_pairs={{0,4},{4,8},{8,12},{12,16},{16,20},{20,24},{24,28},{1,5},{5,9},{9,... | collective-permute-start | bytes 786440 | tf_op jit(solution)/shard_map/while/body/eval_jaxpr/ppermute | solution.py:14
  696.2 11.7 collective-permute-start.2
  699.2 11.5 collective-permute-start.3
  712.6 27.1 %collective-permute-start = (bf16[256,512]{0,1:T(8,128)(2,1)S(1)}, bf16[256,512]{0,1:T(8,128)(2,1)}, u32[]{:S(2)}, u32[]{:S(2)}) collective-permute-start(bf16[256,512]{0,1:T(8,128)(2,1)S(1)} %copy.91), channel_id=1, source_target_pairs={{0,4},{4,8},{8,12},{12,16},{16,20},{20,24},{24,28},{1,5},{5,9},{9,... | collective-permute-start | bytes 786440 | tf_op jit(solution)/shard_map/while/body/eval_jaxpr/ppermute | solution.py:14
  716.3 23.5 %collective-permute-start.1 = (bf16[256,512]{0,1:T(8,128)(2,1)}, bf16[256,512]{0,1:T(8,128)(2,1)}, u32[]{:S(2)}, u32[]{:S(2)}) collective-permute-start(bf16[256,512]{0,1:T(8,128)(2,1)} %copy.92), channel_id=1, source_target_pairs={{0,4},{4,8},{8,12},{12,16},{16,20},{20,24},{24,28},{1,5},{5,9},{9,... | collective-permute-start | bytes 786440 | tf_op jit(solution)/shard_map/while/body/eval_jaxpr/ppermute | solution.py:14
  724.8 11.1 collective-permute-start.2
  727.9 10.9 collective-permute-start.3
  740.8 26.9 %collective-permute-start = (bf16[256,512]{0,1:T(8,128)(2,1)S(1)}, bf16[256,512]{0,1:T(8,128)(2,1)}, u32[]{:S(2)}, u32[]{:S(2)}) collective-permute-start(bf16[256,512]{0,1:T(8,128)(2,1)S(1)} %copy.91), channel_id=1, source_target_pairs={{0,4},{4,8},{8,12},{12,16},{16,20},{20,24},{24,28},{1,5},{5,9},{9,... | collective-permute-start | bytes 786440 | tf_op jit(solution)/shard_map/while/body/eval_jaxpr/ppermute | solution.py:14
  744.4 23.3 %collective-permute-start.1 = (bf16[256,512]{0,1:T(8,128)(2,1)}, bf16[256,512]{0,1:T(8,128)(2,1)}, u32[]{:S(2)}, u32[]{:S(2)}) collective-permute-start(bf16[256,512]{0,1:T(8,128)(2,1)} %copy.92), channel_id=1, source_target_pairs={{0,4},{4,8},{8,12},{12,16},{16,20},{20,24},{24,28},{1,5},{5,9},{9,... | collective-permute-start | bytes 786440 | tf_op jit(solution)/shard_map/while/body/eval_jaxpr/ppermute | solution.py:14
  752.9 10.9 collective-permute-start.2
  755.9 10.7 collective-permute-start.3
  768.7 26.9 %collective-permute-start = (bf16[256,512]{0,1:T(8,128)(2,1)S(1)}, bf16[256,512]{0,1:T(8,128)(2,1)}, u32[]{:S(2)}, u32[]{:S(2)}) collective-permute-start(bf16[256,512]{0,1:T(8,128)(2,1)S(1)} %copy.91), channel_id=1, source_target_pairs={{0,4},{4,8},{8,12},{12,16},{16,20},{20,24},{24,28},{1,5},{5,9},{9,... | collective-permute-start | bytes 786440 | tf_op jit(solution)/shard_map/while/body/eval_jaxpr/ppermute | solution.py:14
  772.3 23.3 %collective-permute-start.1 = (bf16[256,512]{0,1:T(8,128)(2,1)}, bf16[256,512]{0,1:T(8,128)(2,1)}, u32[]{:S(2)}, u32[]{:S(2)}) collective-permute-start(bf16[256,512]{0,1:T(8,128)(2,1)} %copy.92), channel_id=1, source_target_pairs={{0,4},{4,8},{8,12},{12,16},{16,20},{20,24},{24,28},{1,5},{5,9},{9,... | collective-permute-start | bytes 786440 | tf_op jit(solution)/shard_map/while/body/eval_jaxpr/ppermute | solution.py:14
  781.0 10.8 collective-permute-start.2
  784.0 10.6 collective-permute-start.3
  796.6 26.9 %collective-permute-start = (bf16[256,512]{0,1:T(8,128)(2,1)S(1)}, bf16[256,512]{0,1:T(8,128)(2,1)}, u32[]{:S(2)}, u32[]{:S(2)}) collective-permute-start(bf16[256,512]{0,1:T(8,128)(2,1)S(1)} %copy.91), channel_id=1, source_target_pairs={{0,4},{4,8},{8,12},{12,16},{16,20},{20,24},{24,28},{1,5},{5,9},{9,... | collective-permute-start | bytes 786440 | tf_op jit(solution)/shard_map/while/body/eval_jaxpr/ppermute | solution.py:14
  800.2 23.3 %collective-permute-start.1 = (bf16[256,512]{0,1:T(8,128)(2,1)}, bf16[256,512]{0,1:T(8,128)(2,1)}, u32[]{:S(2)}, u32[]{:S(2)}) collective-permute-start(bf16[256,512]{0,1:T(8,128)(2,1)} %copy.92), channel_id=1, source_target_pairs={{0,4},{4,8},{8,12},{12,16},{16,20},{20,24},{24,28},{1,5},{5,9},{9,... | collective-permute-start | bytes 786440 | tf_op jit(solution)/shard_map/while/body/eval_jaxpr/ppermute | solution.py:14
  809.1 10.6 collective-permute-start.2
  812.1 10.4 collective-permute-start.3
  824.5 27.1 %collective-permute-start = (bf16[256,512]{0,1:T(8,128)(2,1)S(1)}, bf16[256,512]{0,1:T(8,128)(2,1)}, u32[]{:S(2)}, u32[]{:S(2)}) collective-permute-start(bf16[256,512]{0,1:T(8,128)(2,1)S(1)} %copy.91), channel_id=1, source_target_pairs={{0,4},{4,8},{8,12},{12,16},{16,20},{20,24},{24,28},{1,5},{5,9},{9,... | collective-permute-start | bytes 786440 | tf_op jit(solution)/shard_map/while/body/eval_jaxpr/ppermute | solution.py:14
  828.1 23.5 %collective-permute-start.1 = (bf16[256,512]{0,1:T(8,128)(2,1)}, bf16[256,512]{0,1:T(8,128)(2,1)}, u32[]{:S(2)}, u32[]{:S(2)}) collective-permute-start(bf16[256,512]{0,1:T(8,128)(2,1)} %copy.92), channel_id=1, source_target_pairs={{0,4},{4,8},{8,12},{12,16},{16,20},{20,24},{24,28},{1,5},{5,9},{9,... | collective-permute-start | bytes 786440 | tf_op jit(solution)/shard_map/while/body/eval_jaxpr/ppermute | solution.py:14
  837.2 10.6 collective-permute-start.2
  840.2 10.4 collective-permute-start.3
  857.9 270.4 %reduce-scatter.12.cloned.1.call-start = ((), (), s32[]{:S(2)}) async-start(), calls=%async_computation.18 | async-start | bytes 2162688 | tf_op jit(solution)/shard_map/reduce_scatter | solution.py:235
  859.9 408.4 %reduce-scatter.8.cloned.1.call-start = ((), (), s32[]{:S(2)}) async-start(), calls=%async_computation.16 | async-start | bytes 4325376 | tf_op jit(solution)/shard_map/reduce_scatter | solution.py:233
  864.7 543.8 %reduce-scatter.14.cloned.1.call-start = ((), (), s32[]{:S(2)}) async-start(), calls=%async_computation.19 | async-start | bytes 4325376 | tf_op jit(solution)/shard_map/reduce_scatter | solution.py:236
  867.5 750.4 %reduce-scatter.16.cloned.1.call-start = ((), (), s32[]{:S(2)}) async-start(), calls=%async_computation.20 | async-start | bytes 19464192 | tf_op jit(solution)/shard_map/reduce_scatter | solution.py:238
  877.1 953.1 %reduce-scatter.18.cloned.1.call-start = ((), (), s32[]{:S(2)}) async-start(), calls=%async_computation.21 | async-start | bytes 19464192 | tf_op jit(solution)/shard_map/reduce_scatter | solution.py:239
  886.9 1155.8 %reduce-scatter.20.cloned.1.call-start = ((), (), s32[]{:S(2)}) async-start(), calls=%async_computation.22 | async-start | bytes 19464192 | tf_op jit(solution)/shard_map/reduce_scatter | solution.py:240
  (63 other events, 1618.6 us)
Sparse Core Ops, SparseCore 0:
  10.9 56.5 all-gather.15
  70.3 52.6 all-gather.9
  125.9 55.2 all-gather.13
  183.7 48.1 all-gather.17
  233.8 49.5 all-gather.11
  286.1 54.5 all-gather.19
  343.6 80.8 all-gather.21
  427.5 80.6 all-gather.23
  511.1 80.6 all-gather.25
  858.0 134.5 reduce-scatter.9
  995.6 132.6 reduce-scatter.11
  1131.0 137.2 reduce-scatter.7
  1271.2 137.2 reduce-scatter.13
  1415.3 202.5 reduce-scatter.15
  1624.7 205.5 reduce-scatter.17
  1837.1 205.5 reduce-scatter.19
where the time goes:
time: 2060 us; the launch traced here: 2050 us
  waiting for transfers between devices  1580 us (77%)
  matrix products  203 us (10%)
  blocking collectives  79.9 us (4%)
  other arithmetic  69.2 us (3%)
  starting transfers between devices  61.6 us (3%)
  local copies, waits for them, and re-layouts  40.7 us (2%)
    reduce_scatter x1, waiting for transfers between devices, on_device(): lax.psum_scatter(up_grad, ('seq', 'dp'), scatter_dimension=0, tiled=True)  212 us
    reduce_scatter x1, waiting for transfers between devices, on_device(): lax.psum_scatter(down_grad, ('seq', 'dp'), scatter_dimension=0, tiled=True)  212 us
    reduce_scatter x1, waiting for transfers between devices, on_device(): lax.psum_scatter(gate_grad, ('seq', 'dp'), scatter_dimension=0, tiled=True)  209 us
    reduce_scatter x1, waiting for transfers between devices, on_device(): lax.psum_scatter(out_grad, ('seq', 'dp'), scatter_dimension=0, tiled=True)  140 us
    reduce_scatter x1, waiting for transfers between devices, on_device(): lax.psum_scatter(query_weight_grad, ('seq', 'dp'), scatter_dimension=0, t...  140 us
    reduce_scatter x1, waiting for transfers between devices, on_device(): lax.psum_scatter(value_weight_grad, ('seq', 'dp'), scatter_dimension=0, t...  136 us
    dot_general x21, matrix products, product(): return jnp.dot(left, right, preferred_element_type=jnp.float32)  99.8 us
    all_gather x1, waiting for transfers between devices, on_device(): lax.all_gather(gate_weight, ('seq', 'dp'), axis=0, tiled=True)  80.6 us
  transfers between devices with their start and end apart: 48, of which 32 were waited for; matrix products, arithmetic and copies ran while one was open for 13% of the time, Pallas kernels for 0%

commit v1 on v0

v1 whole, which is shorter than its diff:
```python
import functools
import math

import jax
import jax.numpy as jnp
from jax import lax
from jax.experimental import pallas as pl
from jax.experimental.pallas import tpu as pltpu
from jax.sharding import Mesh
from jax.sharding import PartitionSpec as P

EPS = 1e-05
THETA = 1000000.0
LOG2E = math.log2(math.e)
BF = jnp.bfloat16
F32 = jnp.float32

ZAXES = ("t", "z")
SEQ = ("t", "z", "x")
HEADS = ("z", "x")


def dot(left, right, contract):
    return lax.dot_general(left, right, ((contract[:1], contract[1:]), ((), ())), preferred_element_type=F32)


def swap(array, axis):
    return lax.ppermute(array, axis, [(0, 1), (1, 0)])


def pick(array, index, axis):
    return lax.dynamic_index_in_dim(array, index, axis, keepdims=False)


def gather_two(array, axis, place):
    other = swap(array, axis)
    first = lax.axis_index(axis) == 0
    return jnp.where(first, jnp.stack([array, other], place), jnp.stack([other, array], place))


def shift(array, axes, by):
    count = lax.axis_size(axes)
    return lax.ppermute(array, axes, [(i, (i + by) % count) for i in range(count)])


def gather_line(array):
    count, here = lax.axis_size(ZAXES), lax.axis_index(ZAXES)
    out = jnp.zeros((count,) + array.shape, array.dtype)
    out = lax.dynamic_update_index_in_dim(out, array, here, 0)
    for by in range(1, count):
        out = lax.dynamic_update_index_in_dim(out, shift(array, ZAXES, by), (here - by) % count, 0)
    return out


def scatter_line(array):
    count, here = lax.axis_size(ZAXES), lax.axis_index(ZAXES)
    sent = array.astype(BF)
    total = pick(array, here, 0)
    for by in range(1, count):
        total = total + shift(pick(sent, (here + by) % count, 0), ZAXES, by).astype(F32)
    return total


def scatter_two(array, axis, place):
    here = lax.axis_index(axis)
    other = swap(pick(array, 1 - here, place).astype(BF), axis)
    return pick(array, here, place) + other.astype(F32)


def rms_factor(values):
    return lax.rsqrt(jnp.mean(values * values, axis=-1, keepdims=True) + EPS)


def rms_back(values, factor, gain, grad):
    scaled = grad * gain
    mean = jnp.mean(scaled * values, axis=-1, keepdims=True)
    return factor * scaled - values * (factor * factor * factor * mean)


def prepare(pre, gain, cosine, sine):
    half = pre.shape[1] // 2
    factor = lax.rsqrt(jnp.mean(pre * pre, axis=1, keepdims=True) + EPS)
    normed = pre * factor * gain[None, :, None]
    first, second = normed[:, :half], normed[:, half:]
    return jnp.concatenate([first * cosine - second * sine, second * cosine + first * sine], axis=1)


def attend_kernel(rate, base_ref, start_ref, q_ref, kv_ref, out_ref, exact_ref, mass_ref, key_ref):
    blocks, width, rows = q_ref.shape
    dim = width // 2
    base = base_ref[0]

    def turn(j, _):
        key_ref[j] = kv_ref[j, :dim, :].astype(F32).T.astype(BF)
        return 0

    lax.fori_loop(0, kv_ref.shape[0], turn, 0)
    place = lax.broadcasted_iota(jnp.int32, (rows, 2 * rows), 0)
    lane = lax.broadcasted_iota(jnp.int32, (rows, 2 * rows), 1) % rows

    def row(i, _):
        queries = jnp.concatenate([q_ref[i, :dim, :], q_ref[i, dim:, :]], axis=1)
        begin = jnp.concatenate([start_ref[i], start_ref[i]], axis=1)

        def tile(j, state, last):
            mass, total = state
            scores = dot(key_ref[j], queries, (1, 0))
            allowed = place >= begin - j * rows
            if last:
                allowed = allowed & (place <= lane)
            weights = jnp.where(allowed, jnp.exp2(scores * rate), 0.0)
            mass = mass + jnp.sum(weights, axis=0, keepdims=True)
            return mass, total + dot(kv_ref[j, dim:, :], weights.astype(BF), (1, 0))

        state = (jnp.zeros((1, 2 * rows), F32), jnp.zeros((dim, 2 * rows), F32))
        state = lax.fori_loop(0, base + i, functools.partial(tile, last=False), state)
        mass, total = tile(base + i, state, True)
        total = total / mass
        exact = jnp.concatenate([total[:, :rows], total[:, rows:]], axis=0)
        exact_ref[i] = exact
        out_ref[i] = exact.astype(BF)
        mass_ref[i] = mass
        return 0

    lax.fori_loop(0, blocks, row, 0)


def attend_back_kernel(
    rate, scale, base_ref, start_ref, q_ref, kv_ref, exact_ref, mass_ref, grad_ref,
    dq_ref, dkv_ref, key_ref, value_ref, qrow_ref, grow_ref, dk_ref, dv_ref,
):
    blocks, width, rows = q_ref.shape
    dim = width // 2
    base = base_ref[0]

    def turn(j, _):
        key_ref[j] = kv_ref[j, :dim, :].astype(F32).T.astype(BF)
        value_ref[j] = kv_ref[j, dim:, :].astype(F32).T.astype(BF)
        dk_ref[j] = jnp.zeros((rows, dim), F32)
        dv_ref[j] = jnp.zeros((rows, dim), F32)
        return 0

    lax.fori_loop(0, kv_ref.shape[0], turn, 0)

    def turn_rows(i, _):
        for g in range(2):
            part = slice(g * dim, (g + 1) * dim)
            qrow_ref[i, g * rows:(g + 1) * rows, :] = q_ref[i, part, :].astype(F32).T.astype(BF)
            grow_ref[i, g * rows:(g + 1) * rows, :] = grad_ref[i, part, :].astype(F32).T.astype(BF)
        return 0

    lax.fori_loop(0, blocks, turn_rows, 0)
    place = lax.broadcasted_iota(jnp.int32, (rows, 2 * rows), 0)
    lane = lax.broadcasted_iota(jnp.int32, (rows, 2 * rows), 1) % rows

    def row(i, _):
        queries = jnp.concatenate([q_ref[i, :dim, :], q_ref[i, dim:, :]], axis=1)
        grads = jnp.concatenate([grad_ref[i, :dim, :], grad_ref[i, dim:, :]], axis=1)
        exact = jnp.concatenate([exact_ref[i, :dim, :], exact_ref[i, dim:, :]], axis=1)
        begin = jnp.concatenate([start_ref[i], start_ref[i]], axis=1)
        delta = jnp.sum(grads.astype(F32) * exact, axis=0, keepdims=True)
        level = jnp.log(mass_ref[i]) * LOG2E

        def tile(j, dq, last):
            scores = dot(key_ref[j], queries, (1, 0))
            allowed = place >= begin - j * rows
            if last:
                allowed = allowed & (place <= lane)
            probs = jnp.where(allowed, jnp.exp2(scores * rate - level), 0.0)
            d_probs = dot(value_ref[j], grads, (1, 0))
            d_scores = (probs * (d_probs - delta)).astype(BF)
            dv_ref[j] += dot(probs.astype(BF), grow_ref[i], (1, 0))
            dk_ref[j] += dot(d_scores, qrow_ref[i], (1, 0))
            return dq + dot(kv_ref[j, :dim, :], d_scores, (1, 0))

        dq = lax.fori_loop(0, base + i, functools.partial(tile, last=False), jnp.zeros((dim, 2 * rows), F32))
        dq = tile(base + i, dq, True) * scale
        dq_ref[i] = jnp.concatenate([dq[:, :rows], dq[:, rows:]], axis=0).astype(BF)
        return 0

    lax.fori_loop(0, blocks, row, 0)

    def turn_back(j, _):
        dkv_ref[j, :dim, :] = (dk_ref[j] * scale).T.astype(BF)
        dkv_ref[j, dim:, :] = dv_ref[j].T.astype(BF)
        return 0

    lax.fori_loop(0, kv_ref.shape[0], turn_back, 0)


VMEM = pl.BlockSpec(memory_space=pltpu.VMEM)
SMEM = pl.BlockSpec(memory_space=pltpu.SMEM)
PARAMS = pltpu.CompilerParams(vmem_limit_bytes=48 * 1024 * 1024)


def attend(base, start, queries, kv, dim):
    blocks, width, rows = queries.shape
    tiles = kv.shape[0]
    pairs = blocks * (blocks + 1) // 2
    return pl.pallas_call(
        functools.partial(attend_kernel, dim ** -0.5 * LOG2E),
        out_shape=(
            jax.ShapeDtypeStruct(queries.shape, BF),
            jax.ShapeDtypeStruct(queries.shape, F32),
            jax.ShapeDtypeStruct((blocks, 1, 2 * rows), F32),
        ),
        in_specs=[SMEM, VMEM, VMEM, VMEM],
        out_specs=(VMEM, VMEM, VMEM),
        scratch_shapes=[pltpu.VMEM((tiles, rows, dim), BF)],
        compiler_params=PARAMS,
        cost_estimate=pl.CostEstimate(
            flops=pairs * 8 * rows * rows * dim, bytes_accessed=4 * 1024 * 1024, transcendentals=pairs * 2 * rows * rows
        ),
        name="attend",
    )(base, start, queries, kv)


def attend_back(base, start, queries, kv, exact, mass, grads, dim):
    blocks, width, rows = queries.shape
    tiles = kv.shape[0]
    pairs = blocks * (blocks + 1) // 2
    return pl.pallas_call(
        functools.partial(attend_back_kernel, dim ** -0.5 * LOG2E, dim ** -0.5),
        out_shape=(jax.ShapeDtypeStruct(queries.shape, BF), jax.ShapeDtypeStruct(kv.shape, BF)),
        in_specs=[SMEM] + [VMEM] * 6,
        out_specs=(VMEM, VMEM),
        scratch_shapes=[
            pltpu.VMEM((tiles, rows, dim), BF),
            pltpu.VMEM((tiles, rows, dim), BF),
            pltpu.VMEM((blocks, 2 * rows, dim), BF),
            pltpu.VMEM((blocks, 2 * rows, dim), BF),
            pltpu.VMEM((tiles, rows, dim), F32),
            pltpu.VMEM((tiles, rows, dim), F32),
        ],
        compiler_params=PARAMS,
        cost_estimate=pl.CostEstimate(
            flops=pairs * 20 * rows * rows * dim, bytes_accessed=4 * 1024 * 1024, transcendentals=pairs * 2 * rows * rows
        ),
        name="attend_back",
    )(base, start, queries, kv, exact, mass, grads)


def exchange(blocks):
    return lax.all_to_all(blocks, HEADS, 0, 0, tiled=True)


def on_device(
    tokens,
    attn_gain,
    q_weight,
    k_weight,
    v_weight,
    q_norm_gain,
    k_norm_gain,
    o_weight,
    ffn_gain,
    gate_weight,
    up_weight,
    down_weight,
    doc_lengths,
    cotangent,
):
    rows, width = tokens.shape[1:]
    dim = q_norm_gain.shape[0]
    line = lax.axis_size(ZAXES)
    groups = lax.axis_size("t")
    seq, pairs = lax.axis_size(SEQ), lax.axis_size(("y", "c"))
    half_pairs = pairs // 2
    here = lax.axis_index(SEQ)
    own = lax.axis_index(("y", "c"))
    side_x, side_y, side_c = lax.axis_index("x"), lax.axis_index("y"), lax.axis_index("c")
    piece = q_weight.shape[0]
    q_cols, k_cols = q_weight.shape[1], k_weight.shape[1]
    heads, kv_heads = q_cols // dim, k_cols // dim
    blocks = kv_heads
    strip = down_weight.shape[0]
    hidden_local = seq * strip
    pad = 128

    lengths = doc_lengths[0]
    ends = jnp.cumsum(lengths)
    starts = ends - lengths

    def begin_of(positions):
        doc = jnp.sum((positions[:, None] >= ends[None, :]).astype(jnp.int32), axis=1)
        labels = jnp.arange(lengths.shape[0], dtype=jnp.int32)
        return jnp.sum(jnp.where(doc[:, None] == labels[None, :], starts[None, :], 0), axis=1)

    place = here * rows + jnp.arange(rows, dtype=jnp.int32)
    offset = (place - begin_of(place)).astype(F32)
    freqs = THETA ** (-jnp.arange(dim // 2, dtype=F32) * 2.0 / dim)
    angles = freqs[:, None] * offset[None, :]
    cosine, sine = jnp.cos(angles), jnp.sin(angles)
    base = lax.axis_index("t") * blocks
    span = base * rows + jnp.arange(blocks * rows, dtype=jnp.int32)
    start_rows = begin_of(span).reshape(blocks, 1, rows)
    base = base.astype(jnp.int32).reshape(1)

    gains = jnp.pad(jnp.stack([attn_gain, ffn_gain], axis=1), ((0, 0), (0, pad - 2)))

    def gather_all(array, first, second):
        places = {"x": 1, "y": 2}
        array = gather_two(array, first, 1)
        array = gather_two(array, second, places[second])
        return gather_two(array, "c", 3)

    first_line = gather_line(jnp.concatenate([q_weight, k_weight, v_weight, gains], axis=1))
    w_query = gather_all(first_line[..., :q_cols], "x", "y").reshape(width, q_cols)
    w_rest = gather_all(first_line[..., q_cols:], "y", "x").reshape(width, -1)
    w_key, w_value = w_rest[:, :k_cols], w_rest[:, k_cols : 2 * k_cols]
    gain_rows = w_rest[:, 2 * k_cols : 2 * k_cols + 2].astype(F32).T
    attn_gain_all, ffn_gain_all = gain_rows[0], gain_rows[1]

    wide = jnp.stack([gate_weight, up_weight], axis=1).reshape(piece, 2, seq, pairs, strip)
    wide = jnp.transpose(wide, (3, 0, 1, 2, 4)).reshape(pairs, piece, 2 * hidden_local)
    mixed = jnp.zeros_like(wide)
    mixed = lax.dynamic_update_index_in_dim(mixed, pick(wide, own, 0), own, 0)
    for by in range(1, pairs):
        moved = lax.ppermute(pick(wide, own ^ by, 0), ("y", "c"), [(i, i ^ by) for i in range(pairs)])
        mixed = lax.dynamic_update_index_in_dim(mixed, moved, own ^ by, 0)
    mixed = mixed.reshape(pairs * piece, 2 * hidden_local)

    def gather_seq(array):
        return gather_two(gather_line(array), "x", 1).reshape((-1,) + array.shape[1:])

    w_out = gather_all(gather_line(o_weight), "x", "y").reshape(heads * dim, width)
    w_gate = gather_seq(mixed[:, :hidden_local])
    w_up = gather_seq(mixed[:, hidden_local:])
    w_down = gather_seq(down_weight)

    def gather_pairs(array):
        return gather_two(gather_two(array, "y", 0), "c", 1).reshape(pairs * rows, -1)

    grad_out = cotangent[0]
    grad_all = gather_pairs(grad_out)

    inputs = tokens[0].astype(F32)
    in_factor = rms_factor(inputs)
    normed = (inputs * in_factor * attn_gain_all).astype(BF)
    q_pre = dot(w_query, normed, (0, 1)).reshape(heads, dim, rows)
    k_pre = dot(w_key, normed, (0, 1)).reshape(kv_heads, dim, rows)
    values = dot(w_value, normed, (0, 1)).astype(BF).reshape(kv_heads, dim, rows)
    q_gain, k_gain = q_norm_gain.astype(F32), k_norm_gain.astype(F32)
    queries = prepare(q_pre, q_gain, cosine, sine).astype(BF).reshape(kv_heads, 2 * dim, rows)
    keys = prepare(k_pre, k_gain, cosine, sine).astype(BF)
    unit = exchange(jnp.concatenate([queries, keys, values], axis=1))
    unit_q, unit_kv = unit[:, : 2 * dim], unit[:, 2 * dim :]
    if groups > 1:
        unit_kv = lax.all_gather(unit_kv, "t", axis=0, tiled=True)
    unit_out, exact, mass = attend(base, start_rows, unit_q, unit_kv, dim)
    attn_b = exchange(unit_out).reshape(heads * dim, rows)
    hidden = inputs + dot(attn_b, w_out, (0, 0))

    ffn_factor = rms_factor(hidden)
    hn = (hidden * ffn_factor * ffn_gain_all).astype(BF)
    hn_all = gather_pairs(hn)
    gate = dot(hn_all, w_gate, (1, 0))
    up = dot(hn_all, w_up, (1, 0))
    sig = jax.nn.sigmoid(gate)
    silu = gate * sig
    act = (silu * up).astype(BF)
    d_act = dot(grad_all, w_down, (1, 1))
    d_gate = (d_act * up * (sig * (1.0 + gate * (1.0 - sig)))).astype(BF)
    d_up = (d_act * silu).astype(BF)

    def split_rows(array, side):
        return pick(array.reshape(half_pairs, 2, rows, -1), side, 1).reshape(half_pairs * rows, -1)

    def scatter_pairs(product):
        sent = swap(product(1 - side_c).astype(BF), "c")
        kept = (product(side_c) + sent.astype(F32)).reshape(half_pairs, rows, -1)
        return scatter_two(kept, "y", 0)

    d_hn = scatter_pairs(
        lambda side: dot(split_rows(d_gate, side), w_gate, (1, 1)) + dot(split_rows(d_up, side), w_up, (1, 1))
    )
    result = hidden + scatter_pairs(lambda side: dot(split_rows(act, side), w_down, (1, 0)))
    output = result.astype(BF)[None]

    def scatter_seq(left, right):
        part = left.shape[1] // (line * 2)
        cut = left.reshape(left.shape[0], line, 2, part)

        def product(side):
            return dot(pick(cut, side, 2).reshape(left.shape[0], line * part), right, (0, 0))

        sent = swap(product(1 - side_x).astype(BF), "x")
        kept = product(side_x) + sent.astype(F32)
        return scatter_line(kept.reshape(line, part, -1))

    down_grad = scatter_seq(act, grad_all)
    gate_part = scatter_seq(hn_all, d_gate)
    up_part = scatter_seq(hn_all, d_up)
    parts = jnp.concatenate([gate_part, up_part], axis=1).astype(BF).reshape(pairs, piece, 2, seq, strip)
    wide_grad = jnp.zeros_like(parts)
    wide_grad = lax.dynamic_update_index_in_dim(wide_grad, pick(parts, own, 0), own, 0)
    for by in range(1, pairs):
        moved = lax.ppermute(pick(parts, own ^ by, 0), ("y", "c"), [(i, i ^ by) for i in range(pairs)])
        wide_grad = lax.dynamic_update_index_in_dim(wide_grad, moved, own ^ by, 0)
    wide_grad = jnp.transpose(wide_grad, (2, 1, 3, 0, 4)).astype(F32).reshape(2, piece, -1)

    d_hidden = grad_out.astype(F32) + rms_back(hidden, ffn_factor, ffn_gain_all, d_hn)
    ffn_gain_part = jnp.sum(d_hn * hidden * ffn_factor, axis=0)
    d_branch = d_hidden.astype(BF)
    d_attn = dot(w_out, d_branch, (1, 1)).astype(BF).reshape(kv_heads, 2 * dim, rows)
    unit_grad = exchange(d_attn)

    def scatter_rest(array, first, second):
        places = {"x": 1, "y": 2}
        array = scatter_two(array, first, places[first])
        return scatter_two(array, second, 1)

    def cut_core(array, side):
        return pick(array.reshape(line * 2 * half_pairs, 2, piece, -1), side, 1).reshape(line * 2 * half_pairs * piece, -1)

    def out_product(side):
        return dot(cut_core(attn_b, side), d_branch, (1, 0))

    out_kept = out_product(side_c) + swap(out_product(1 - side_c).astype(BF), "c").astype(F32)
    out_kept = out_kept.reshape(line, 2, half_pairs, piece, width)
    out_grad = scatter_line(
        jnp.concatenate(
            [
                scatter_rest(out_kept[..., : width // 2], "x", "y"),
                scatter_rest(out_kept[..., width // 2 :], "y", "x"),
            ],
            axis=-1,
        )
    )

    unit_dq, unit_dkv = attend_back(base, start_rows, unit_q, unit_kv, exact, mass, unit_grad, dim)
    if groups > 1:
        unit_dkv = lax.psum_scatter(unit_dkv.astype(F32), "t", scatter_dimension=0, tiled=True).astype(BF)
    back = exchange(jnp.concatenate([unit_dq, unit_dkv], axis=1)).astype(F32)
    d_queries = back[:, : 2 * dim].reshape(heads, dim, rows)
    d_keys = back[:, 2 * dim : 3 * dim]
    d_values = back[:, 3 * dim :]
    _, query_pull = jax.vjp(lambda pre, gain: prepare(pre, gain, cosine, sine), q_pre, q_gain)
    _, key_pull = jax.vjp(lambda pre, gain: prepare(pre, gain, cosine, sine), k_pre, k_gain)
    d_q_pre, q_gain_grad = query_pull(d_queries)
    d_k_pre, k_gain_grad = key_pull(d_keys)
    d_pre = jnp.concatenate(
        [d_q_pre.reshape(q_cols, rows), d_k_pre.reshape(k_cols, rows), d_values.reshape(k_cols, rows)], axis=0
    ).astype(BF)

    small = jnp.stack([q_gain_grad, k_gain_grad])
    for axis in ("c", "y", "x"):
        small = small + swap(small, axis)
    small = sum((shift(small, ZAXES, by) for by in range(1, line)), small)

    d_normed = (
        dot(d_pre[:q_cols], w_query, (0, 1))
        + dot(d_pre[q_cols : q_cols + k_cols], w_key, (0, 1))
        + dot(d_pre[q_cols + k_cols :], w_value, (0, 1))
    )
    attn_gain_part = jnp.sum(d_normed * inputs * in_factor, axis=0)
    input_grad = (d_hidden + rms_back(inputs, in_factor, attn_gain_all, d_normed))[None]

    gain_parts = jnp.pad(jnp.stack([attn_gain_part, ffn_gain_part], axis=1), ((0, 0), (0, pad - 2)))
    normed_cut = normed.reshape(rows, line * 2 * half_pairs, 2, piece)

    def pre_product(side):
        left = pick(normed_cut, side, 2).reshape(rows, -1)
        return jnp.concatenate([dot(left, d_pre, (0, 1)), cut_core(gain_parts, side)], axis=1)

    kept = pre_product(side_c) + swap(pre_product(1 - side_c).astype(BF), "c").astype(F32)
    kept = kept.reshape(line, 2, half_pairs, piece, -1)
    shares = scatter_line(
        jnp.concatenate(
            [scatter_rest(kept[..., :q_cols], "x", "y"), scatter_rest(kept[..., q_cols:], "y", "x")], axis=-1
        )
    )
    rest = shares[:, q_cols:]
    return (
        output,
        input_grad,
        rest[:, 2 * k_cols],
        shares[:, :q_cols],
        rest[:, :k_cols],
        rest[:, k_cols : 2 * k_cols],
        small[0],
        small[1],
        out_grad,
        rest[:, 2 * k_cols + 1],
        wide_grad[0],
        wide_grad[1],
        down_grad,
    )


def solution(mesh):
    seq, pairs = mesh.shape["seq"], mesh.shape["dp"]

    def run(*arrays):
        kv_heads = arrays[3].shape[1] // arrays[5].shape[0]
        groups = seq // kv_heads
        fine = Mesh(mesh.devices.reshape(groups, kv_heads // 2, 2, pairs // 2, 2), ("t", "z", "x", "y", "c"))
        everywhere = ("t", "z", "x", "y", "c")
        packs = P(("y", "c"), SEQ, None)
        split, split_one = P(everywhere, None), P(everywhere)
        return jax.shard_map(
            on_device,
            mesh=fine,
            in_specs=(
                packs, split_one, split, split, split, P(), P(), split, split_one, split, split, split,
                P(("y", "c"), None), packs,
            ),
            out_specs=(
                packs, packs, split_one, split, split, split, P(), P(), split, split_one, split, split, split,
            ),
            check_vma=False,
        )(*arrays)

    return run
```

time: 2060 us -> 607 us (0.29)
  waiting for transfers between devices: 1580 us -> 152 us
  matrix products: 203 us -> 64.9 us
  local copies, waits for them, and re-layouts: 40.7 us -> 146 us
  blocking collectives: 79.9 us -> 0 us
  starting transfers between devices: 61.6 us -> 128 us
  Pallas kernels: 0 us -> 34.4 us
    reduce_scatter x7 -> x0, waiting for transfers between devices: 1090 us -> none  [the longest x1 212 us: on_device(): lax.psum_scatter(up_grad, ('seq', 'dp'), scatter_dimension=0, tiled=True)]
    all_gather x9 -> x0, waiting for transfers between devices: 445 us -> none  [the longest x1 80.6 us: on_device(): lax.all_gather(gate_weight, ('seq', 'dp'), axis=0, tiled=True)]
    dot_general x63 -> x27, matrix products: 203 us -> 64.9 us  [dot(): lax.dot_general(left, right, ((contract[:1], contract[1:]), ((), ())), pr...]
    ppermute x32 -> x75, waiting for transfers between devices: 40.1 us -> 126 us  [the longest x36 76.2 us: swap(): return lax.ppermute(array, axis, [(0, 1), (1, 0)])]
    unnamed x2 -> x0, blocking collectives: 79.9 us -> none
    dynamic_update_slice x0 -> x26, local copies, waits for them, and re-layouts: none -> 56.5 us  [the longest x3 33.6 us: on_device(): wide_grad = lax.dynamic_update_index_in_dim(wide_grad, moved, own ^ by, 0)]
    ppermute x32 -> x75, starting transfers between devices: 60.4 us -> 103 us  [the longest x33 65.6 us: shift(): lax.ppermute(array, axes, [(i, (i + by) % count) for i in range(count)])]
    pallas_call x0 -> x2, Pallas kernels: none -> 34.4 us  [the longest x1 19.3 us: attend_back(): pl.pallas_call(functools.partial(attend_back_kernel, dim ** (-0.5) * LOG2...]
  transfers between devices with their start and end apart: 48 -> 79, of which waited for: 32 -> 28; matrix products, arithmetic and copies ran while one was open for 13% -> 39% of each run, Pallas kernels for 0% -> 6%
where the time goes in v1:
time: 607 us; the launch traced here: 595 us
  waiting for transfers between devices  152 us (25%)
  local copies, waits for them, and re-layouts  146 us (24%)
  starting transfers between devices  128 us (21%)
  other arithmetic  66.4 us (11%)
  matrix products  64.9 us (11%)
  Pallas kernels  34.4 us (6%)
    ppermute x36, waiting for transfers between devices, swap(): return lax.ppermute(array, axis, [(0, 1), (1, 0)])  76.2 us
    ppermute x33, starting transfers between devices, shift(): lax.ppermute(array, axes, [(i, (i + by) % count) for i in range(count)])  65.6 us
    dot_general x27, matrix products, dot(): lax.dot_general(left, right, ((contract[:1], contract[1:]), ((), ())), pr...  64.9 us
    ppermute x33, waiting for transfers between devices, shift(): lax.ppermute(array, axes, [(i, (i + by) % count) for i in range(count)])  39.1 us
    dynamic_update_slice x3, local copies, waits for them, and re-layouts, on_device(): wide_grad = lax.dynamic_update_index_in_dim(wide_grad, moved, own ^ by, 0)  33.6 us
    ppermute x36, starting transfers between devices, swap(): return lax.ppermute(array, axis, [(0, 1), (1, 0)])  32.7 us
    select_n x24, other arithmetic, gather_two(): jnp.where(first, jnp.stack([array, other], place), jnp.stack([other, arra...  32.5 us
    all_to_all x4, waiting for transfers between devices, exchange(): return lax.all_to_all(blocks, HEADS, 0, 0, tiled=True)  25.7 us
  transfers between devices with their start and end apart: 79, of which 28 were waited for; matrix products, arithmetic and copies ran while one was open for 39% of the time, Pallas kernels for 6%

profile of v1, /device:TPU:0, one launch (start us, length us, event | category | flops | bytes accessed | tf_op | source)
XLA Modules:
  0.0 594.7 jit_solution(12830071332772103136)
XLA Ops:
  0.7 3.1 collective-permute-start.9
  33.6 4.1 collective-permute-done.18
  50.0 8.2 %collective-permute-start.20 = (bf16[128,1152]{1,0:T(8,128)(2,1)S(1)}, bf16[128,1152]{1,0:T(8,128)(2,1)S(1)}, u32[]{:S(2)}, u32[]{:S(2)}) collective-permute-start(bf16[128,1152]{1,0:T(8,128)(2,1)S(1)} %get-tuple-element.77), channel_id=1, source_target_pairs={{0,8},{8,16},{16,24},{24,0},{1,9},{9,17},{17,25},{25,1},{2,10},{10... | collective-permute-start | bytes 884744 | tf_op jit(solution)/shard_map/ppermute | solution.py:43
  61.2 3.5 collective-permute-start.22
  64.9 3.6 collective-permute-start.24
  71.3 4.0 collective-permute-done.21
  78.3 3.2 collective-permute-done.4
  82.5 8.5 %collective-permute-done.7 = bf16[4,2,32,1152]{3,2,0,1:T(8,128)(2,1)S(1)} collective-permute-done((bf16[4,2,32,1152]{3,2,0,1:T(8,128)(2,1)S(1)}, bf16[4,2,32,1152]{3,2,0,1:T(8,128)(2,1)S(1)}, u32[]{:S(2)}, u32[]{:S(2)}) %collective-permute-start.7) | collective-permute-done | bytes 589856 | tf_op jit(solution)/shard_map/ppermute | solution.py:28
  94.5 11.1 %collective-permute-start.26 = (bf16[128,1152]{1,0:T(8,128)(2,1)}, bf16[128,1152]{1,0:T(8,128)(2,1)}, u32[]{:S(2)}, u32[]{:S(2)}) collective-permute-start(bf16[128,1152]{1,0:T(8,128)(2,1)} %get-tuple-element.78), channel_id=1, source_target_pairs={{0,24},{8,0},{16,8},{24,16},{1,25},{9,1},{17,9},{25,17},{2,26},{10... | collective-permute-start | bytes 884744 | tf_op jit(solution)/shard_map/ppermute | solution.py:43
  122.0 3.6 all-to-all-start
  142.3 3.4 collective-permute-done.31
  145.7 3.5 maximum_select_fusion.3
  151.7 15.1 %attend.1 = (bf16[8,128,256]{2,1,0:T(8,128)(2,1)}, f32[8,128,256]{2,1,0:T(8,128)S(1)}, f32[8,1,512]{2,1,0:T(1,128)S(1)}) custom-call(s32[1]{0:T(128)} %constant.392.clone.1.base_ref, s32[8,1,256]{2,1,0:T(1,128)S(1)} %bitcast.408, bf16[8,128,256]{2,1,0:T(8,128)(2,1)S(1)} %get-tuple-element.74.q_ref, bf16[8,128,256]{2,1,0:T(8,128)(2,1)S(1)} %get-tuple-element.73.kv_ref), custom_call_target="tpu_custom_call" | custom-call | flops 1207959552 | bytes 4194304 | tf_op jit(solution)/shard_map/attend/pallas_call | solution.py:200
  166.8 4.0 all-to-all-start.1
  175.8 4.6 fusion.87
  183.9 20.2 %all-to-all-done.1 = bf16[8,128,256]{2,1,0:T(8,128)(2,1)S(1)} async-done(((bf16[8,128,256]{2,1,0:T(8,128)(2,1)}), bf16[8,128,256]{2,1,0:T(8,128)(2,1)S(1)}, u32[]{:S(2)}, u32[]{:S(2)}) %all-to-all-start.1) | async-done | bytes 524320 | tf_op jit(solution)/shard_map/all_to_all | solution.py:244
  207.6 4.3 maximum_select_fusion.1
  212.1 8.1 %collective-permute-done.15 = bf16[256,1024]{1,0:T(8,128)(2,1)S(1)} collective-permute-done((bf16[256,1024]{1,0:T(8,128)(2,1)S(1)}, bf16[256,1024]{1,0:T(8,128)(2,1)S(1)}, u32[]{:S(2)}, u32[]{:S(2)}) %collective-permute-start.15) | collective-permute-done | bytes 524320 | tf_op jit(solution)/shard_map/ppermute | solution.py:28
  233.1 4.5 select_n.635
  237.5 5.3 fusion.86
  242.9 8.3 %multiply_convert_fusion.1 = (bf16[1024,1152]{1,0:T(8,128)(2,1)}, bf16[1024,1152]{1,0:T(8,128)(2,1)}, bf16[1024,1152]{1,0:T(8,128)(2,1)}) fusion(f32[1024,1152]{1,0:T(8,128)} %fusion.87, f32[1024,1152]{1,0:T(8,128)S(1)} %fusion.86, bf16[1024,1024]{1,0:T(8,128)(2,1)S(1)} %bitcast.427, bf16[1024,1152]{1,0:T(8,128)(2,1)S(1)} %bitcast.460), kind=kOutput, calls=%fused_computation.1 | convolution fusion | flops 2433613824 | bytes 20971520 | tf_op jit(solution)/shard_map/dot_general | solution.py:24
  251.2 4.7 copy.139
  262.9 6.4 %constant_dynamic-slice_fusion.3 = (bf16[1024,4,1,128]{3,2,1,0:T(2,128)(2,1)}, bf16[1024,4,1,128]{3,2,1,0:T(2,128)(2,1)}) fusion(bf16[1024,4,2,128]{3,2,1,0:T(2,128)(2,1)S(1)} %copy-done.5, s32[]{:T(128)S(6)} %select_n.628, s32[]{:T(128)S(6)} %select_n.627), kind=kLoop, calls=%fused_computation.246 | loop fusion | bytes 4194312 | tf_op jit(solution)/shard_map/jit(dynamic_index_in_dim)/dynamic_slice | solution.py:32
  269.3 5.8 copy.134
  275.1 4.5 convolution_convert_fusion.2
  280.2 6.0 %copy.133 = bf16[1024,4,1,128]{0,3,1,2:T(8,128)(2,1)} copy(bf16[1024,4,1,128]{3,2,1,0:T(2,128)(2,1)} %get-tuple-element.51) | data formatting | bytes 2097152 | tf_op jit(solution)/shard_map/jit(dynamic_index_in_dim)/dynamic_slice | solution.py:32
  286.2 3.6 convolution_convert_fusion.1
  312.5 3.2 collective-permute-done.60
  319.9 20.6 %collective-permute-done.64 = bf16[512,1152]{1,0:T(8,128)(2,1)S(1)} collective-permute-done((bf16[512,1152]{1,0:T(8,128)(2,1)S(1)}, bf16[512,1152]{1,0:T(8,128)(2,1)S(1)}, u32[]{:S(2)}, u32[]{:S(2)}) %collective-permute-start.64) | collective-permute-done | bytes 1179680 | tf_op jit(solution)/shard_map/ppermute | solution.py:28
  345.5 11.4 %collective-permute-done.63 = bf16[128,1152]{1,0:T(8,128)(2,1)S(1)} collective-permute-done((bf16[128,1152]{1,0:T(8,128)(2,1)S(1)}, bf16[128,1152]{1,0:T(8,128)(2,1)S(1)}, u32[]{:S(2)}, u32[]{:S(2)}) %collective-permute-start.63) | collective-permute-done | bytes 294944 | tf_op jit(solution)/shard_map/ppermute | solution.py:43
  359.2 9.4 %collective-permute-done.66 = bf16[128,1152]{1,0:T(8,128)(2,1)S(1)} collective-permute-done((bf16[128,1152]{1,0:T(8,128)(2,1)S(1)}, bf16[128,1152]{1,0:T(8,128)(2,1)S(1)}, u32[]{:S(2)}, u32[]{:S(2)}) %collective-permute-start.66) | collective-permute-done | bytes 294944 | tf_op jit(solution)/shard_map/ppermute | solution.py:43
  368.6 7.1 %collective-permute-done.67 = bf16[128,1152]{1,0:T(8,128)(2,1)S(1)} collective-permute-done((bf16[128,1152]{1,0:T(8,128)(2,1)S(1)}, bf16[128,1152]{1,0:T(8,128)(2,1)S(1)}, u32[]{:S(2)}, u32[]{:S(2)}) %collective-permute-start.67) | collective-permute-done | bytes 294944 | tf_op jit(solution)/shard_map/ppermute | solution.py:43
  384.4 11.7 %all-to-all-start.2 = ((bf16[8,128,256]{2,1,0:T(8,128)(2,1)}), bf16[8,128,256]{2,1,0:T(8,128)(2,1)S(1)}, u32[]{:S(2)}, u32[]{:S(2)}) async-start(bf16[8,128,256]{2,1,0:T(8,128)(2,1)} %bitcast.511), calls=%async_computation.2 | async-start | bytes 1048576 | tf_op jit(solution)/shard_map/all_to_all | solution.py:244
  399.7 3.5 convert_element_type.372
  408.4 11.2 %dynamic_update_slice.114 = bf16[4,32,2,8,144]{4,0,3,1,2:T(4,128)(2,1)} dynamic-update-slice(bf16[4,32,2,8,144]{4,0,3,1,2:T(4,128)(2,1)} %broadcast_in_dim.215, bf16[1,32,2,8,144]{4,0,3,1,2:T(2,128)(2,1)} %copy.135, s32[]{:T(128)S(6)} %select_n.608, s32[]{:T(128)} %constant.393.clone.1, s32[]{:T(128)} %constant.393.clone.1, s32[]{:T(128)} %constant.393.clone.1, s32[]{:T(128)} %constant.393.clone.1) | dynamic-update-slice | bytes 294916 | tf_op jit(solution)/shard_map/jit(dynamic_update_index_in_dim)/dynamic_update_slice | solution.py:396
  425.4 3.5 collective-permute-done.69
  433.9 11.2 %dynamic_update_slice.115 = bf16[4,32,2,8,144]{4,0,3,1,2:T(4,128)(2,1)} dynamic-update-slice(bf16[4,32,2,8,144]{4,0,3,1,2:T(4,128)(2,1)} %dynamic_update_slice.114, bf16[1,32,2,8,144]{4,0,3,1,2:T(2,128)(2,1)} %copy.136, s32[]{:T(128)S(6)} %select_n.609, s32[]{:T(128)} %constant.393.clone.1, s32[]{:T(128)} %constant.393.clone.1, s32[]{:T(128)} %constant.393.clone.1, s32[]{:T(128)} %constant.393.clone.1) | dynamic-update-slice | bytes 294916 | tf_op jit(solution)/shard_map/jit(dynamic_update_index_in_dim)/dynamic_update_slice | solution.py:399
  445.1 11.2 %dynamic_update_slice.116 = bf16[4,32,2,8,144]{4,0,3,1,2:T(4,128)(2,1)} dynamic-update-slice(bf16[4,32,2,8,144]{4,0,3,1,2:T(4,128)(2,1)} %dynamic_update_slice.115, bf16[1,32,2,8,144]{4,0,3,1,2:T(2,128)(2,1)} %copy.137, s32[]{:T(128)S(6)} %select_n.610, s32[]{:T(128)} %constant.393.clone.1, s32[]{:T(128)} %constant.393.clone.1, s32[]{:T(128)} %constant.393.clone.1, s32[]{:T(128)} %constant.393.clone.1) | dynamic-update-slice | bytes 294916 | tf_op jit(solution)/shard_map/jit(dynamic_update_index_in_dim)/dynamic_update_slice | solution.py:399
  456.3 11.2 %dynamic_update_slice.117 = bf16[4,32,2,8,144]{4,0,3,1,2:T(4,128)(2,1)} dynamic-update-slice(bf16[4,32,2,8,144]{4,0,3,1,2:T(4,128)(2,1)} %dynamic_update_slice.116, bf16[1,32,2,8,144]{4,0,3,1,2:T(2,128)(2,1)} %copy.138, s32[]{:T(128)S(6)} %select_n.611, s32[]{:T(128)} %constant.393.clone.1, s32[]{:T(128)} %constant.393.clone.1, s32[]{:T(128)} %constant.393.clone.1, s32[]{:T(128)} %constant.393.clone.1) | dynamic-update-slice | bytes 294916 | tf_op jit(solution)/shard_map/jit(dynamic_update_index_in_dim)/dynamic_update_slice | solution.py:399
  467.5 19.3 %attend_back.1 = (bf16[8,128,256]{2,1,0:T(8,128)(2,1)S(1)}, bf16[8,128,256]{2,1,0:T(8,128)(2,1)S(1)}) custom-call(s32[1]{0:T(128)} %constant.392.clone.1.base_ref, s32[8,1,256]{2,1,0:T(1,128)S(1)} %bitcast.409, bf16[8,128,256]{2,1,0:T(8,128)(2,1)S(1)} %get-tuple-element.74.q_ref, bf16[8,128,256]{2,1,0:T(8,128)(2,1)S(1)} %get-tuple-element.73.kv_ref, ...), custom_call_target="tpu_custom_call" | custom-call | flops 3019898880 | bytes 4194304 | tf_op jit(solution)/shard_map/attend_back/pallas_call | solution.py:222
  487.9 6.3 %all-to-all-start.3 = ((bf16[8,256,256]{2,1,0:T(8,128)(2,1)}), bf16[8,256,256]{2,1,0:T(8,128)(2,1)S(1)}, u32[]{:S(2)}, u32[]{:S(2)}) async-start(bf16[8,256,256]{2,1,0:T(8,128)(2,1)} %pad_maximum_fusion.5), calls=%async_computation.3 | async-start | bytes 2097152 | tf_op jit(solution)/shard_map/all_to_all | solution.py:244
  500.9 4.0 collective-permute-done.55
  506.9 8.3 %collective-permute-done.53 = bf16[4,2,32,512]{3,2,0,1:T(8,128)(2,1)S(1)} collective-permute-done((bf16[4,2,32,512]{3,2,0,1:T(8,128)(2,1)S(1)}, bf16[4,2,32,512]{3,2,0,1:T(8,128)(2,1)S(1)}, u32[]{:S(2)}, u32[]{:S(2)}) %collective-permute-start.53) | collective-permute-done | bytes 262176 | tf_op jit(solution)/shard_map/ppermute | solution.py:28
  517.8 3.1 all-to-all-done.3
  531.7 3.3 pad_maximum_fusion
  550.8 3.3 collective-permute-done.47
  565.8 5.6 collective-permute-done.39
  588.6 3.6 collective-permute-done.44
  (521 shorter events, 254.3 us)
Async XLA Ops:
  0.7 19.5 %collective-permute-start.9 = (bf16[32,1024]{1,0:T(8,128)(2,1)}, bf16[32,1024]{1,0:T(8,128)(2,1)}, u32[]{:S(2)}, u32[]{:S(2)}) collective-permute-start(bf16[32,1024]{1,0:T(8,128)(2,1)} %param.21), channel_id=1, source_target_pairs={{0,8},{8,16},{16,24},{24,0},{1,9},{9,17},{17,25},{25,1},{2,10},{10... | collective-permute-start | bytes 196616 | tf_op jit(solution)/shard_map/ppermute | solution.py:43
  3.7 20.2 %collective-permute-start.10 = (bf16[32,1024]{1,0:T(8,128)(2,1)}, bf16[32,1024]{1,0:T(8,128)(2,1)S(1)}, u32[]{:S(2)}, u32[]{:S(2)}) collective-permute-start(bf16[32,1024]{1,0:T(8,128)(2,1)} %param.21), channel_id=1, source_target_pairs={{0,16},{8,24},{16,0},{24,8},{1,17},{9,25},{17,1},{25,9},{2,18},{10... | collective-permute-start | bytes 196616 | tf_op jit(solution)/shard_map/ppermute | solution.py:43
  6.3 18.2 %collective-permute-start.11 = (bf16[32,1024]{1,0:T(8,128)(2,1)}, bf16[32,1024]{1,0:T(8,128)(2,1)}, u32[]{:S(2)}, u32[]{:S(2)}) collective-permute-start(bf16[32,1024]{1,0:T(8,128)(2,1)} %param.21), channel_id=1, source_target_pairs={{0,24},{8,0},{16,8},{24,16},{1,25},{9,1},{17,9},{25,17},{2,26},{10... | collective-permute-start | bytes 196616 | tf_op jit(solution)/shard_map/ppermute | solution.py:43
  9.3 17.6 %collective-permute-start = (bf16[32,2176]{1,0:T(8,128)(2,1)S(1)}, bf16[32,2176]{1,0:T(8,128)(2,1)}, u32[]{:S(2)}, u32[]{:S(2)}) collective-permute-start(bf16[32,2176]{1,0:T(8,128)(2,1)S(1)} %fusion.59), channel_id=1, source_target_pairs={{0,8},{8,16},{16,24},{24,0},{1,9},{9,17},{17,25},{25,1},{2,10},{10... | collective-permute-start | bytes 417800 | tf_op jit(solution)/shard_map/ppermute | solution.py:43
  10.1 20.7 %collective-permute-start.1 = (bf16[32,2176]{1,0:T(8,128)(2,1)S(1)}, bf16[32,2176]{1,0:T(8,128)(2,1)S(1)}, u32[]{:S(2)}, u32[]{:S(2)}) collective-permute-start(bf16[32,2176]{1,0:T(8,128)(2,1)S(1)} %fusion.59), channel_id=1, source_target_pairs={{0,16},{8,24},{16,0},{24,8},{1,17},{9,25},{17,1},{25,9},{2,18},{10... | collective-permute-start | bytes 417800 | tf_op jit(solution)/shard_map/ppermute | solution.py:43
  23.9 22.1 %collective-permute-start.28 = (bf16[144,1024]{1,0:T(8,128)(2,1)S(1)}, bf16[144,1024]{1,0:T(8,128)(2,1)S(1)}, u32[]{:S(2)}, u32[]{:S(2)}) collective-permute-start(bf16[144,1024]{1,0:T(8,128)(2,1)S(1)} %copy-done.54), channel_id=1, source_target_pairs={{0,8},{8,16},{16,24},{24,0},{1,9},{9,17},{17,25},{25,1},{2,10},{10... | collective-permute-start | bytes 884744 | tf_op jit(solution)/shard_map/ppermute | solution.py:43
  24.6 23.9 %collective-permute-start.29 = (bf16[144,1024]{1,0:T(8,128)(2,1)S(1)}, bf16[144,1024]{1,0:T(8,128)(2,1)S(1)}, u32[]{:S(2)}, u32[]{:S(2)}) collective-permute-start(bf16[144,1024]{1,0:T(8,128)(2,1)S(1)} %copy-done.54), channel_id=1, source_target_pairs={{0,16},{8,24},{16,0},{24,8},{1,17},{9,25},{17,1},{25,9},{2,18},{10... | collective-permute-start | bytes 884744 | tf_op jit(solution)/shard_map/ppermute | solution.py:43
  26.9 23.1 %collective-permute-start.30 = (bf16[144,1024]{1,0:T(8,128)(2,1)S(1)}, bf16[144,1024]{1,0:T(8,128)(2,1)S(1)}, u32[]{:S(2)}, u32[]{:S(2)}) collective-permute-start(bf16[144,1024]{1,0:T(8,128)(2,1)S(1)} %copy-done.54), channel_id=1, source_target_pairs={{0,24},{8,0},{16,8},{24,16},{1,25},{9,1},{17,9},{25,17},{2,26},{10... | collective-permute-start | bytes 884744 | tf_op jit(solution)/shard_map/ppermute | solution.py:43
  37.7 94.5 %collective-permute-start.34 = (bf16[256,1024]{1,0:T(8,128)(2,1)}, bf16[256,1024]{1,0:T(8,128)(2,1)}, u32[]{:S(2)}, u32[]{:S(2)}) collective-permute-start(bf16[256,1024]{1,0:T(8,128)(2,1)} %bitcast.98), channel_id=1, source_target_pairs={{0,2},{2,0},{1,3},{3,1},{4,6},{6,4},{5,7},{7,5},{8,10},{10,8},{9,1... | collective-permute-start | bytes 1572872 | tf_op jit(solution)/shard_map/ppermute | solution.py:28
  40.0 18.3 %collective-permute-start.12 = (bf16[4,32,1024]{2,1,0:T(8,128)(2,1)S(1)}, bf16[4,32,1024]{2,1,0:T(8,128)(2,1)S(1)}, u32[]{:S(2)}, u32[]{:S(2)}) collective-permute-start(bf16[4,32,1024]{2,1,0:T(8,128)(2,1)S(1)} %bitcast_dynamic-update-slice_fusion.19), channel_id=1, source_target_pairs={{0,4},{4,0},{1,5},{5,1},{2,6},{6,2},{3,7},{7,3},{8,12},{12,8},{9,1... | collective-permute-start | bytes 786440 | tf_op jit(solution)/shard_map/ppermute | solution.py:28
  46.0 15.2 %collective-permute-start.3 = (bf16[4,32,1024]{2,1,0:T(8,128)(2,1)S(1)}, bf16[4,32,1024]{2,1,0:T(8,128)(2,1)S(1)}, u32[]{:S(2)}, u32[]{:S(2)}) collective-permute-start(bf16[4,32,1024]{2,1,0:T(8,128)(2,1)S(1)} %get-tuple-element.90), channel_id=1, source_target_pairs={{0,4},{4,0},{1,5},{5,1},{2,6},{6,2},{3,7},{7,3},{8,12},{12,8},{9,1... | collective-permute-start | bytes 786440 | tf_op jit(solution)/shard_map/ppermute | solution.py:28
  48.5 16.4 %collective-permute-start.6 = (bf16[4,32,1152]{2,1,0:T(8,128)(2,1)S(1)}, bf16[4,32,1152]{2,1,0:T(8,128)(2,1)S(1)}, u32[]{:S(2)}, u32[]{:S(2)}) collective-permute-start(bf16[4,32,1152]{2,1,0:T(8,128)(2,1)S(1)} %get-tuple-element.93), channel_id=1, source_target_pairs={{0,2},{2,0},{1,3},{3,1},{4,6},{6,4},{5,7},{7,5},{8,10},{10,8},{9,1... | collective-permute-start | bytes 884744 | tf_op jit(solution)/shard_map/ppermute | solution.py:28
  50.0 18.9 %collective-permute-start.20 = (bf16[128,1152]{1,0:T(8,128)(2,1)S(1)}, bf16[128,1152]{1,0:T(8,128)(2,1)S(1)}, u32[]{:S(2)}, u32[]{:S(2)}) collective-permute-start(bf16[128,1152]{1,0:T(8,128)(2,1)S(1)} %get-tuple-element.77), channel_id=1, source_target_pairs={{0,8},{8,16},{16,24},{24,0},{1,9},{9,17},{17,25},{25,1},{2,10},{10... | collective-permute-start | bytes 884744 | tf_op jit(solution)/shard_map/ppermute | solution.py:43
  58.3 17.0 %collective-permute-start.21 = (bf16[128,1152]{1,0:T(8,128)(2,1)S(1)}, bf16[128,1152]{1,0:T(8,128)(2,1)S(1)}, u32[]{:S(2)}, u32[]{:S(2)}) collective-permute-start(bf16[128,1152]{1,0:T(8,128)(2,1)S(1)} %get-tuple-element.77), channel_id=1, source_target_pairs={{0,16},{8,24},{16,0},{24,8},{1,17},{9,25},{17,1},{25,9},{2,18},{10... | collective-permute-start | bytes 884744 | tf_op jit(solution)/shard_map/ppermute | solution.py:43
  61.2 32.0 %collective-permute-start.22 = (bf16[128,1152]{1,0:T(8,128)(2,1)S(1)}, bf16[128,1152]{1,0:T(8,128)(2,1)S(1)}, u32[]{:S(2)}, u32[]{:S(2)}) collective-permute-start(bf16[128,1152]{1,0:T(8,128)(2,1)S(1)} %get-tuple-element.77), channel_id=1, source_target_pairs={{0,24},{8,0},{16,8},{24,16},{1,25},{9,1},{17,9},{25,17},{2,26},{10... | collective-permute-start | bytes 884744 | tf_op jit(solution)/shard_map/ppermute | solution.py:43
  64.9 60.6 %collective-permute-start.24 = (bf16[128,1152]{1,0:T(8,128)(2,1)}, bf16[128,1152]{1,0:T(8,128)(2,1)}, u32[]{:S(2)}, u32[]{:S(2)}) collective-permute-start(bf16[128,1152]{1,0:T(8,128)(2,1)} %get-tuple-element.78), channel_id=1, source_target_pairs={{0,8},{8,16},{16,24},{24,0},{1,9},{9,17},{17,25},{25,1},{2,10},{10... | collective-permute-start | bytes 884744 | tf_op jit(solution)/shard_map/ppermute | solution.py:43
  75.3 15.8 %collective-permute-start.7 = (bf16[4,2,32,1152]{3,2,0,1:T(8,128)(2,1)S(1)}, bf16[4,2,32,1152]{3,2,0,1:T(8,128)(2,1)S(1)}, u32[]{:S(2)}, u32[]{:S(2)}) collective-permute-start(bf16[4,2,32,1152]{3,2,0,1:T(8,128)(2,1)S(1)} %maximum_select_fusion.17), channel_id=1, source_target_pairs={{0,4},{4,0},{1,5},{5,1},{2,6},{6,2},{3,7},{7,3},{8,12},{12,8},{9,1... | collective-permute-start | bytes 1769480 | tf_op jit(solution)/shard_map/ppermute | solution.py:28
  81.5 47.1 %collective-permute-start.25 = (bf16[128,1152]{1,0:T(8,128)(2,1)}, bf16[128,1152]{1,0:T(8,128)(2,1)}, u32[]{:S(2)}, u32[]{:S(2)}) collective-permute-start(bf16[128,1152]{1,0:T(8,128)(2,1)} %get-tuple-element.78), channel_id=1, source_target_pairs={{0,16},{8,24},{16,0},{24,8},{1,17},{9,25},{17,1},{25,9},{2,18},{10... | collective-permute-start | bytes 884744 | tf_op jit(solution)/shard_map/ppermute | solution.py:43
  93.2 15.3 %collective-permute-start.8 = (bf16[4,2,2,32,1152]{4,3,0,2,1:T(8,128)(2,1)}, bf16[4,2,2,32,1152]{4,3,0,2,1:T(8,128)(2,1)}, u32[]{:S(2)}, u32[]{:S(2)}) collective-permute-start(bf16[4,2,2,32,1152]{4,3,0,2,1:T(8,128)(2,1)} %maximum_select_fusion.9), channel_id=1, source_target_pairs={{0,1},{1,0},{2,3},{3,2},{4,5},{5,4},{6,7},{7,6},{8,9},{9,8},{10,11... | collective-permute-start | bytes 3538952 | tf_op jit(solution)/shard_map/ppermute | solution.py:28
  94.5 40.5 %collective-permute-start.26 = (bf16[128,1152]{1,0:T(8,128)(2,1)}, bf16[128,1152]{1,0:T(8,128)(2,1)}, u32[]{:S(2)}, u32[]{:S(2)}) collective-permute-start(bf16[128,1152]{1,0:T(8,128)(2,1)} %get-tuple-element.78), channel_id=1, source_target_pairs={{0,24},{8,0},{16,8},{24,16},{1,25},{9,1},{17,9},{25,17},{2,26},{10... | collective-permute-start | bytes 884744 | tf_op jit(solution)/shard_map/ppermute | solution.py:43
  108.4 37.3 %collective-permute-start.31 = (bf16[4,144,1024]{2,1,0:T(8,128)(2,1)}, bf16[4,144,1024]{2,1,0:T(8,128)(2,1)}, u32[]{:S(2)}, u32[]{:S(2)}) collective-permute-start(bf16[4,144,1024]{2,1,0:T(8,128)(2,1)} %copy-done.17), channel_id=1, source_target_pairs={{0,4},{4,0},{1,5},{5,1},{2,6},{6,2},{3,7},{7,3},{8,12},{12,8},{9,1... | collective-permute-start | bytes 3538952 | tf_op jit(solution)/shard_map/ppermute | solution.py:28
  122.0 29.6 %all-to-all-start = ((bf16[8,256,256]{2,1,0:T(8,128)(2,1)}), bf16[8,256,256]{2,1,0:T(8,128)(2,1)S(1)}, u32[]{:S(2)}, u32[]{:S(2)}) async-start(bf16[8,256,256]{2,1,0:T(8,128)(2,1)} %pad_maximum_fusion.4), calls=%async_computation | async-start | bytes 2097152 | tf_op jit(solution)/shard_map/all_to_all | solution.py:244
  128.6 79.1 %collective-permute-start.23 = (bf16[4,128,1152]{2,1,0:T(8,128)(2,1)}, bf16[4,128,1152]{2,1,0:T(8,128)(2,1)}, u32[]{:S(2)}, u32[]{:S(2)}) collective-permute-start(bf16[4,128,1152]{2,1,0:T(8,128)(2,1)} %bitcast_dynamic-update-slice_fusion.8), channel_id=1, source_target_pairs={{0,4},{4,0},{1,5},{5,1},{2,6},{6,2},{3,7},{7,3},{8,12},{12,8},{9,1... | collective-permute-start | bytes 3538952 | tf_op jit(solution)/shard_map/ppermute | solution.py:28
  135.0 35.9 %collective-permute-start.35 = (bf16[2,256,1024]{2,1,0:T(8,128)(2,1)}, bf16[2,256,1024]{2,1,0:T(8,128)(2,1)}, u32[]{:S(2)}, u32[]{:S(2)}) collective-permute-start(bf16[2,256,1024]{2,1,0:T(8,128)(2,1)} %maximum_select_fusion.15), channel_id=1, source_target_pairs={{0,1},{1,0},{2,3},{3,2},{4,5},{5,4},{6,7},{7,6},{8,9},{9,8},{10,11... | collective-permute-start | bytes 3145736 | tf_op jit(solution)/shard_map/ppermute | solution.py:28
  136.7 84.6 %collective-permute-start.27 = (bf16[4,128,1152]{2,1,0:T(8,128)(2,1)}, bf16[4,128,1152]{2,1,0:T(8,128)(2,1)}, u32[]{:S(2)}, u32[]{:S(2)}) collective-permute-start(bf16[4,128,1152]{2,1,0:T(8,128)(2,1)} %bitcast_dynamic-update-slice_fusion.4), channel_id=1, source_target_pairs={{0,4},{4,0},{1,5},{5,1},{2,6},{6,2},{3,7},{7,3},{8,12},{12,8},{9,1... | collective-permute-start | bytes 3538952 | tf_op jit(solution)/shard_map/ppermute | solution.py:28
  140.7 39.7 %collective-permute-start.14 = (bf16[4,2,2,32,1024]{4,3,1,0,2:T(8,128)(2,1)}, bf16[4,2,2,32,1024]{4,3,1,0,2:T(8,128)(2,1)}, u32[]{:S(2)}, u32[]{:S(2)}) collective-permute-start(bf16[4,2,2,32,1024]{4,3,1,0,2:T(8,128)(2,1)} %maximum_select_fusion.12), channel_id=1, source_target_pairs={{0,1},{1,0},{2,3},{3,2},{4,5},{5,4},{6,7},{7,6},{8,9},{9,8},{10,11... | collective-permute-start | bytes 3145736 | tf_op jit(solution)/shard_map/ppermute | solution.py:28
  166.8 37.3 %all-to-all-start.1 = ((bf16[8,128,256]{2,1,0:T(8,128)(2,1)}), bf16[8,128,256]{2,1,0:T(8,128)(2,1)S(1)}, u32[]{:S(2)}, u32[]{:S(2)}) async-start(bf16[8,128,256]{2,1,0:T(8,128)(2,1)} %get-tuple-element.18), calls=%async_computation.1 | async-start | bytes 1048576 | tf_op jit(solution)/shard_map/all_to_all | solution.py:244
  261.4 48.3 %collective-permute-start.71 = (bf16[576,1024]{1,0:T(8,128)(2,1)}, bf16[576,1024]{1,0:T(8,128)(2,1)}, u32[]{:S(2)}, u32[]{:S(2)}) collective-permute-start(bf16[576,1024]{1,0:T(8,128)(2,1)} %convolution_convert_fusion.3), channel_id=1, source_target_pairs={{0,4},{4,0},{1,5},{5,1},{2,6},{6,2},{3,7},{7,3},{8,12},{12,8},{9,1... | collective-permute-start | bytes 3538952 | tf_op jit(solution)/shard_map/ppermute | solution.py:28
  279.6 36.1 %collective-permute-start.60 = (bf16[512,1152]{1,0:T(8,128)(2,1)}, bf16[512,1152]{1,0:T(8,128)(2,1)}, u32[]{:S(2)}, u32[]{:S(2)}) collective-permute-start(bf16[512,1152]{1,0:T(8,128)(2,1)} %convolution_convert_fusion.2), channel_id=1, source_target_pairs={{0,4},{4,0},{1,5},{5,1},{2,6},{6,2},{3,7},{7,3},{8,12},{12,8},{9,1... | collective-permute-start | bytes 3538952 | tf_op jit(solution)/shard_map/ppermute | solution.py:28
  289.8 50.7 %collective-permute-start.64 = (bf16[512,1152]{1,0:T(8,128)(2,1)S(1)}, bf16[512,1152]{1,0:T(8,128)(2,1)S(1)}, u32[]{:S(2)}, u32[]{:S(2)}) collective-permute-start(bf16[512,1152]{1,0:T(8,128)(2,1)S(1)} %convolution_convert_fusion.1), channel_id=1, source_target_pairs={{0,4},{4,0},{1,5},{5,1},{2,6},{6,2},{3,7},{7,3},{8,12},{12,8},{9,1... | collective-permute-start | bytes 3538952 | tf_op jit(solution)/shard_map/ppermute | solution.py:28
  306.6 73.8 %collective-permute-start.33 = (bf16[256,1024]{1,0:T(8,128)(2,1)S(1)}, bf16[256,1024]{1,0:T(8,128)(2,1)S(1)}, u32[]{:S(2)}, u32[]{:S(2)}) collective-permute-start(bf16[256,1024]{1,0:T(8,128)(2,1)S(1)} %fusion.35), channel_id=1, source_target_pairs={{0,2},{2,0},{1,3},{3,1},{4,6},{6,4},{5,7},{7,5},{8,10},{10,8},{9,1... | collective-permute-start | bytes 1572872 | tf_op jit(solution)/shard_map/ppermute | solution.py:28
  307.8 71.5 %collective-permute-start.37 = (bf16[256,1024]{1,0:T(8,128)(2,1)S(1)}, bf16[256,1024]{1,0:T(8,128)(2,1)S(1)}, u32[]{:S(2)}, u32[]{:S(2)}) collective-permute-start(bf16[256,1024]{1,0:T(8,128)(2,1)S(1)} %fusion.36), channel_id=1, source_target_pairs={{0,2},{2,0},{1,3},{3,1},{4,6},{6,4},{5,7},{7,5},{8,10},{10,8},{9,1... | collective-permute-start | bytes 1572872 | tf_op jit(solution)/shard_map/ppermute | solution.py:28
  318.8 25.2 %collective-permute-start.61 = (bf16[128,1152]{1,0:T(8,128)(2,1)S(1)}, bf16[128,1152]{1,0:T(8,128)(2,1)S(1)}, u32[]{:S(2)}, u32[]{:S(2)}) collective-permute-start(bf16[128,1152]{1,0:T(8,128)(2,1)S(1)} %get-tuple-element.57), channel_id=1, source_target_pairs={{0,8},{8,16},{16,24},{24,0},{1,9},{9,17},{17,25},{25,1},{2,10},{10... | collective-permute-start | bytes 884744 | tf_op jit(solution)/shard_map/ppermute | solution.py:43
  318.8 26.7 %collective-permute-start.62 = (bf16[128,1152]{1,0:T(8,128)(2,1)S(1)}, bf16[128,1152]{1,0:T(8,128)(2,1)S(1)}, u32[]{:S(2)}, u32[]{:S(2)}) collective-permute-start(bf16[128,1152]{1,0:T(8,128)(2,1)S(1)} %get-tuple-element.59), channel_id=1, source_target_pairs={{0,16},{8,24},{16,0},{24,8},{1,17},{9,25},{17,1},{25,9},{2,18},{10... | collective-permute-start | bytes 884744 | tf_op jit(solution)/shard_map/ppermute | solution.py:43
  340.5 16.4 %collective-permute-start.63 = (bf16[128,1152]{1,0:T(8,128)(2,1)S(1)}, bf16[128,1152]{1,0:T(8,128)(2,1)S(1)}, u32[]{:S(2)}, u32[]{:S(2)}) collective-permute-start(bf16[128,1152]{1,0:T(8,128)(2,1)S(1)} %get-tuple-element.58), channel_id=1, source_target_pairs={{0,24},{8,0},{16,8},{24,16},{1,25},{9,1},{17,9},{25,17},{2,26},{10... | collective-permute-start | bytes 884744 | tf_op jit(solution)/shard_map/ppermute | solution.py:43
  345.5 23.0 %collective-permute-start.66 = (bf16[128,1152]{1,0:T(8,128)(2,1)S(1)}, bf16[128,1152]{1,0:T(8,128)(2,1)S(1)}, u32[]{:S(2)}, u32[]{:S(2)}) collective-permute-start(bf16[128,1152]{1,0:T(8,128)(2,1)S(1)} %get-tuple-element.62), channel_id=1, source_target_pairs={{0,16},{8,24},{16,0},{24,8},{1,17},{9,25},{17,1},{25,9},{2,18},{10... | collective-permute-start | bytes 884744 | tf_op jit(solution)/shard_map/ppermute | solution.py:43
  356.9 18.8 %collective-permute-start.67 = (bf16[128,1152]{1,0:T(8,128)(2,1)S(1)}, bf16[128,1152]{1,0:T(8,128)(2,1)S(1)}, u32[]{:S(2)}, u32[]{:S(2)}) collective-permute-start(bf16[128,1152]{1,0:T(8,128)(2,1)S(1)} %get-tuple-element.61), channel_id=1, source_target_pairs={{0,24},{8,0},{16,8},{24,16},{1,25},{9,1},{17,9},{25,17},{2,26},{10... | collective-permute-start | bytes 884744 | tf_op jit(solution)/shard_map/ppermute | solution.py:43
  357.1 62.5 %collective-permute-start.72 = (bf16[144,1024]{1,0:T(8,128)(2,1)}, bf16[144,1024]{1,0:T(8,128)(2,1)}, u32[]{:S(2)}, u32[]{:S(2)}) collective-permute-start(bf16[144,1024]{1,0:T(8,128)(2,1)} %get-tuple-element.54), channel_id=1, source_target_pairs={{0,8},{8,16},{16,24},{24,0},{1,9},{9,17},{17,25},{25,1},{2,10},{10... | collective-permute-start | bytes 884744 | tf_op jit(solution)/shard_map/ppermute | solution.py:43
  368.6 51.2 %collective-permute-start.73 = (bf16[144,1024]{1,0:T(8,128)(2,1)}, bf16[144,1024]{1,0:T(8,128)(2,1)}, u32[]{:S(2)}, u32[]{:S(2)}) collective-permute-start(bf16[144,1024]{1,0:T(8,128)(2,1)} %get-tuple-element.56), channel_id=1, source_target_pairs={{0,16},{8,24},{16,0},{24,8},{1,17},{9,25},{17,1},{25,9},{2,18},{10... | collective-permute-start | bytes 884744 | tf_op jit(solution)/shard_map/ppermute | solution.py:43
  375.7 45.2 %collective-permute-start.74 = (bf16[144,1024]{1,0:T(8,128)(2,1)}, bf16[144,1024]{1,0:T(8,128)(2,1)}, u32[]{:S(2)}, u32[]{:S(2)}) collective-permute-start(bf16[144,1024]{1,0:T(8,128)(2,1)} %get-tuple-element.55), channel_id=1, source_target_pairs={{0,24},{8,0},{16,8},{24,16},{1,25},{9,1},{17,9},{25,17},{2,26},{10... | collective-permute-start | bytes 884744 | tf_op jit(solution)/shard_map/ppermute | solution.py:43
  384.4 83.2 %all-to-all-start.2 = ((bf16[8,128,256]{2,1,0:T(8,128)(2,1)}), bf16[8,128,256]{2,1,0:T(8,128)(2,1)S(1)}, u32[]{:S(2)}, u32[]{:S(2)}) async-start(bf16[8,128,256]{2,1,0:T(8,128)(2,1)} %bitcast.511), calls=%async_computation.2 | async-start | bytes 1048576 | tf_op jit(solution)/shard_map/all_to_all | solution.py:244
  398.8 95.4 %collective-permute-start.52 = (bf16[512,1024]{1,0:T(8,128)(2,1)}, bf16[512,1024]{1,0:T(8,128)(2,1)}, u32[]{:S(2)}, u32[]{:S(2)}) collective-permute-start(bf16[512,1024]{1,0:T(8,128)(2,1)} %convolution_convert_fusion.4), channel_id=1, source_target_pairs={{0,1},{1,0},{2,3},{3,2},{4,5},{5,4},{6,7},{7,6},{8,9},{9,8},{10,11... | collective-permute-start | bytes 3145736 | tf_op jit(solution)/shard_map/ppermute | solution.py:28
  406.4 16.9 %collective-permute-start.68 = (bf16[32,2,8,144]{3,2,1,0:T(8,128)(2,1)}, bf16[32,2,8,144]{3,2,1,0:T(8,128)(2,1)}, u32[]{:S(2)}, u32[]{:S(2)}) collective-permute-start(bf16[32,2,8,144]{3,2,1,0:T(8,128)(2,1)} %get-tuple-element.69), channel_id=1, source_target_pairs={{0,1},{1,0},{2,3},{3,2},{4,5},{5,4},{6,7},{7,6},{8,9},{9,8},{10,11... | collective-permute-start | bytes 442376 | tf_op jit(solution)/shard_map/ppermute | solution.py:398
  487.9 33.0 %all-to-all-start.3 = ((bf16[8,256,256]{2,1,0:T(8,128)(2,1)}), bf16[8,256,256]{2,1,0:T(8,128)(2,1)S(1)}, u32[]{:S(2)}, u32[]{:S(2)}) async-start(bf16[8,256,256]{2,1,0:T(8,128)(2,1)} %pad_maximum_fusion.5), calls=%async_computation.3 | async-start | bytes 2097152 | tf_op jit(solution)/shard_map/all_to_all | solution.py:244
  498.9 16.3 %collective-permute-start.53 = (bf16[4,2,32,512]{3,2,0,1:T(8,128)(2,1)S(1)}, bf16[4,2,32,512]{3,2,0,1:T(8,128)(2,1)S(1)}, u32[]{:S(2)}, u32[]{:S(2)}) collective-permute-start(bf16[4,2,32,512]{3,2,0,1:T(8,128)(2,1)S(1)} %fusion.54), channel_id=1, source_target_pairs={{0,4},{4,0},{1,5},{5,1},{2,6},{6,2},{3,7},{7,3},{8,12},{12,8},{9,1... | collective-permute-start | bytes 786440 | tf_op jit(solution)/shard_map/ppermute | solution.py:28
  516.0 19.0 %collective-permute-start.54 = (bf16[4,32,512]{2,1,0:T(8,128)(2,1)}, bf16[4,32,512]{2,1,0:T(8,128)(2,1)}, u32[]{:S(2)}, u32[]{:S(2)}) collective-permute-start(bf16[4,32,512]{2,1,0:T(8,128)(2,1)} %fusion.60), channel_id=1, source_target_pairs={{0,2},{2,0},{1,3},{3,1},{4,6},{6,4},{5,7},{7,5},{8,10},{10,8},{9,1... | collective-permute-start | bytes 393224 | tf_op jit(solution)/shard_map/ppermute | solution.py:28
  535.0 20.6 %collective-permute-start.38 = (bf16[512,2176]{1,0:T(8,128)(2,1)}, bf16[512,2176]{1,0:T(8,128)(2,1)}, u32[]{:S(2)}, u32[]{:S(2)}) collective-permute-start(bf16[512,2176]{1,0:T(8,128)(2,1)} %pad_maximum_fusion), channel_id=1, source_target_pairs={{0,1},{1,0},{2,3},{3,2},{4,5},{5,4},{6,7},{7,6},{8,9},{9,8},{10,11... | collective-permute-start | bytes 6684680 | tf_op jit(solution)/shard_map/ppermute | solution.py:28
  560.8 15.8 %collective-permute-start.49 = (f32[2,64]{1,0:T(2,128)S(1)}, f32[2,64]{1,0:T(2,128)S(1)}, u32[]{:S(2)}, u32[]{:S(2)}) collective-permute-start(f32[2,64]{1,0:T(2,128)S(1)} %add.528), channel_id=1, source_target_pairs={{0,8},{8,16},{16,24},{24,0},{1,9},{9,17},{17,25},{25,1},{2,10},{10... | collective-permute-start | bytes 1544 | tf_op jit(solution)/shard_map/ppermute | solution.py:43
  (118 other events, 735.4 us)

commit v2 on v1

--- a/solution.py
+++ b/solution.py
@@ -18,6 +18,7 @@
 ZAXES = ("t", "z")
 SEQ = ("t", "z", "x")
 HEADS = ("z", "x")
+GROUP = ("x", "y", "c")
 
 
 def dot(left, right, contract):
@@ -61,6 +62,10 @@
     return total
 
 
+def after(array, *others):
+    return lax.optimization_barrier((array,) + others)[0]
+
+
 def scatter_two(array, axis, place):
     here = lax.axis_index(axis)
     other = swap(pick(array, 1 - here, place).astype(BF), axis)
@@ -75,14 +80,6 @@
     scaled = grad * gain
     mean = jnp.mean(scaled * values, axis=-1, keepdims=True)
     return factor * scaled - values * (factor * factor * factor * mean)
-
-
-def prepare(pre, gain, cosine, sine):
-    half = pre.shape[1] // 2
-    factor = lax.rsqrt(jnp.mean(pre * pre, axis=1, keepdims=True) + EPS)
-    normed = pre * factor * gain[None, :, None]
-    first, second = normed[:, :half], normed[:, half:]
-    return jnp.concatenate([first * cosine - second * sine, second * cosine + first * sine], axis=1)
 
 
 def attend_kernel(rate, base_ref, start_ref, q_ref, kv_ref, out_ref, exact_ref, mass_ref, key_ref):
@@ -186,6 +183,131 @@
         return 0
 
     lax.fori_loop(0, kv_ref.shape[0], turn_back, 0)
+
+
+def spread_kernel(strip, gate_ref, up_ref, out_ref):
+    members, _, width = out_ref.shape
+    local = width // 2
+    wholes = [gate_ref[...].astype(F32), up_ref[...].astype(F32)]
+    for d in range(members):
+        firsts = [(s * members + d) * strip for s in range(local // strip)]
+        out_ref[d] = jnp.concatenate(
+            [whole[:, first : first + strip] for whole in wholes for first in firsts], axis=1
+        ).astype(BF)
+
+
+def weave_kernel(strip, in_ref, gate_ref, up_ref):
+    members, _, width = in_ref.shape
+    local = width // 2
+    blocks = [in_ref[d].astype(F32) for d in range(members)]
+    for part, ref in enumerate((gate_ref, up_ref)):
+        firsts = [part * local + s * strip for s in range(local // strip)]
+        ref[...] = jnp.concatenate(
+            [block[:, first : first + strip] for first in firsts for block in blocks], axis=1
+        )
+
+
+def prepare_kernel(
+    token_ref, query_ref, rest_ref, q_gain_ref, k_gain_ref, cos_ref, sin_ref, unit_ref, pre_ref, normed_ref, gain_ref
+):
+    dim = q_gain_ref.shape[0]
+    half = dim // 2
+    rows, width = token_ref.shape
+    q_cols = query_ref.shape[1]
+    k_cols = (rest_ref.shape[1] - 128) // 2
+    kv_heads = k_cols // dim
+    gains = rest_ref[:, 2 * k_cols :].astype(F32).T[:8]
+    gain_ref[...] = gains
+    tokens = token_ref[...].astype(F32)
+    factor = lax.rsqrt(jnp.mean(tokens * tokens, axis=1, keepdims=True) + EPS)
+    normed = (tokens * factor * gains[:1]).astype(BF)
+    normed_ref[...] = normed
+    cosine, sine = cos_ref[...], sin_ref[...]
+
+    def turned(weight_ref, first):
+        return dot(normed, weight_ref[:, first : first + 4 * dim], (1, 0)).T
+
+    def head(pre, gain):
+        scaled = pre * lax.rsqrt(jnp.mean(pre * pre, axis=0, keepdims=True) + EPS) * gain
+        one, two = scaled[:half], scaled[half:]
+        return jnp.concatenate([one * cosine - two * sine, two * cosine + one * sine], axis=0).astype(BF)
+
+    for block in range(q_cols // (4 * dim)):
+        pre = turned(query_ref, 4 * dim * block)
+        pre_ref[4 * dim * block : 4 * dim * (block + 1), :] = pre
+        for j in range(4):
+            place = block * 4 + j
+            unit_ref[place // 2, place % 2 * dim : (place % 2 + 1) * dim, :] = head(
+                pre[j * dim : (j + 1) * dim], q_gain_ref[...]
+            )
+    for block in range(kv_heads // 4):
+        pre = turned(rest_ref, 4 * dim * block)
+        pre_ref[q_cols + 4 * dim * block : q_cols + 4 * dim * (block + 1), :] = pre
+        value = turned(rest_ref, k_cols + 4 * dim * block).astype(BF)
+        for j in range(4):
+            part = slice(j * dim, (j + 1) * dim)
+            unit_ref[block * 4 + j, 2 * dim : 3 * dim, :] = head(pre[part], k_gain_ref[...])
+            unit_ref[block * 4 + j, 3 * dim :, :] = value[part]
+
+
+def prepare_back_kernel(back_ref, pre_ref, q_gain_ref, k_gain_ref, cos_ref, sin_ref, out_ref, q_ref, k_ref):
+    dim = q_gain_ref.shape[0]
+    half = dim // 2
+    kv_heads = back_ref.shape[0]
+    q_cols, k_cols = 2 * kv_heads * dim, kv_heads * dim
+    cosine, sine = cos_ref[...], sin_ref[...]
+
+    def head(grad, pre, gain):
+        one, two = grad[:half], grad[half:]
+        scaled = jnp.concatenate([one * cosine + two * sine, two * cosine - one * sine], axis=0)
+        factor = lax.rsqrt(jnp.mean(pre * pre, axis=0, keepdims=True) + EPS)
+        with_gain = scaled * gain
+        mean = jnp.mean(with_gain * pre, axis=0, keepdims=True)
+        d_pre = factor * with_gain - pre * (factor * factor * factor * mean)
+        return d_pre.astype(BF), scaled * pre * factor
+
+    sums = [jnp.zeros(q_gain_ref.shape[:1] + back_ref.shape[2:], F32) for _ in range(2)]
+    for kv in range(kv_heads):
+        for g in range(3):
+            first = (2 * kv + g) * dim if g < 2 else q_cols + kv * dim
+            gain_ref = q_gain_ref if g < 2 else k_gain_ref
+            d_pre, part = head(
+                back_ref[kv, g * dim : (g + 1) * dim, :].astype(F32), pre_ref[first : first + dim, :], gain_ref[...]
+            )
+            out_ref[first : first + dim, :] = d_pre
+            sums[g // 2] = sums[g // 2] + part
+        out_ref[q_cols + k_cols + kv * dim : q_cols + k_cols + (kv + 1) * dim, :] = back_ref[kv, 3 * dim :, :]
+    q_ref[...] = jnp.sum(sums[0], axis=1, keepdims=True)
+    k_ref[...] = jnp.sum(sums[1], axis=1, keepdims=True)
+
+
+def ffn_kernel(count, *refs):
+    tokens, grads = refs[:count], refs[count : 2 * count]
+    wide_ref, down_ref, hn_ref, grad_ref, act_ref, d_both_ref, d_hn_ref = refs[2 * count :]
+    at = 0
+    for token_ref, one_ref in zip(tokens, grads):
+        size = token_ref.shape[0]
+        hn_ref[at : at + size, :] = token_ref[...]
+        grad_ref[at : at + size, :] = one_ref[...]
+        at += size
+    local = down_ref.shape[0]
+    step = 256 if at % 256 == 0 else at
+
+    def block(i, _):
+        cut = pl.ds(pl.multiple_of(i * step, step), step)
+        both = dot(hn_ref[cut, :], wide_ref[...], (1, 0))
+        d_act = dot(grad_ref[cut, :], down_ref[...], (1, 1))
+        gate, up = both[:, :local], both[:, local:]
+        sig = jax.nn.sigmoid(gate)
+        silu = gate * sig
+        act_ref[cut, :] = (silu * up).astype(BF)
+        d_gate = d_act * up * (sig * (1.0 + gate * (1.0 - sig)))
+        d_both = jnp.concatenate([d_gate, d_act * silu], axis=1).astype(BF)
+        d_both_ref[cut, :] = d_both
+        d_hn_ref[cut, :] = dot(d_both, wide_ref[...], (1, 1)).astype(BF)
+        return 0
+
+    lax.fori_loop(0, at // step, block, 0)
 
 
 VMEM = pl.BlockSpec(memory_space=pltpu.VMEM)
@@ -240,6 +362,93 @@
     )(base, start, queries, kv, exact, mass, grads)
 
 
+def spread(gate, up, members, strip):
+    rows, width = gate.shape
+    return pl.pallas_call(
+        functools.partial(spread_kernel, strip),
+        out_shape=jax.ShapeDtypeStruct((members, rows, 2 * width // members), BF),
+        in_specs=[VMEM, VMEM],
+        out_specs=VMEM,
+        compiler_params=PARAMS,
+        name="spread",
+    )(gate, up)
+
+
+def weave(parts, strip):
+    members, rows, width = parts.shape
+    whole = jax.ShapeDtypeStruct((rows, members * width // 2), F32)
+    return pl.pallas_call(
+        functools.partial(weave_kernel, strip),
+        out_shape=(whole, whole),
+        in_specs=[VMEM],
+        out_specs=(VMEM, VMEM),
+        compiler_params=PARAMS,
+        name="weave",
+    )(parts)
+
+
+def prepare_heads(tokens, w_query, w_rest, q_gain, k_gain, cosine, sine):
+    rows, width = tokens.shape
+    dim = q_gain.shape[0]
+    q_cols = w_query.shape[1]
+    k_cols = (w_rest.shape[1] - 128) // 2
+    return pl.pallas_call(
+        prepare_kernel,
+        out_shape=(
+            jax.ShapeDtypeStruct((k_cols // dim, 4 * dim, rows), BF),
+            jax.ShapeDtypeStruct((q_cols + k_cols, rows), F32),
+            jax.ShapeDtypeStruct((rows, width), BF),
+            jax.ShapeDtypeStruct((8, width), F32),
+        ),
+        in_specs=[VMEM] * 7,
+        out_specs=(VMEM,) * 4,
+        compiler_params=PARAMS,
+        cost_estimate=pl.CostEstimate(
+            flops=2 * rows * width * (q_cols + 2 * k_cols), bytes_accessed=8 * 1024 * 1024, transcendentals=0
+        ),
+        name="prepare",
+    )(tokens, w_query, w_rest, q_gain, k_gain, cosine, sine)
+
+
+def prepare_back(back, pre, q_gain, k_gain, cosine, sine):
+    dim, rows = q_gain.shape[0], back.shape[2]
+    return pl.pallas_call(
+        prepare_back_kernel,
+        out_shape=(
+            jax.ShapeDtypeStruct((pre.shape[0] + back.shape[0] * dim, rows), BF),
+            jax.ShapeDtypeStruct((dim, 1), F32),
+            jax.ShapeDtypeStruct((dim, 1), F32),
+        ),
+        in_specs=[VMEM] * 6,
+        out_specs=(VMEM,) * 3,
+        compiler_params=PARAMS,
+        cost_estimate=pl.CostEstimate(flops=20 * pre.size, bytes_accessed=6 * pre.size, transcendentals=0),
+        name="prepare_back",
+    )(back, pre, q_gain, k_gain, cosine, sine)
+
+
+def ffn(tokens, grads, wide, down):
+    total = sum(part.shape[0] for part in tokens)
+    width = wide.shape[0]
+    local = down.shape[0]
+    shapes = [(total, width), (total, width), (total, local), (total, 2 * local), (total, width)]
+    return pl.pallas_call(
+        functools.partial(ffn_kernel, len(tokens)),
+        out_shape=tuple(jax.ShapeDtypeStruct(shape, BF) for shape in shapes),
+        in_specs=[VMEM] * (2 * len(tokens) + 2),
+        out_specs=(VMEM,) * len(shapes),
+        compiler_params=PARAMS,
+        cost_estimate=pl.CostEstimate(
+            flops=10 * total * width * local, bytes_accessed=8 * total * width, transcendentals=total * local
+        ),
+        name="ffn",
+    )(*tokens, *grads, wide, down)
+
+
+def trade(blocks):
+    return lax.all_to_all(blocks, GROUP, 0, 0, tiled=True)
+
+
 def exchange(blocks):
     return lax.all_to_all(blocks, HEADS, 0, 0, tiled=True)
 
@@ -267,14 +476,16 @@
     seq, pairs = lax.axis_size(SEQ), lax.axis_size(("y", "c"))
     half_pairs = pairs // 2
     here = lax.axis_index(SEQ)
-    own = lax.axis_index(("y", "c"))
     side_x, side_y, side_c = lax.axis_index("x"), lax.axis_index("y"), lax.axis_index("c")
     piece = q_weight.shape[0]
     q_cols, k_cols = q_weight.shape[1], k_weight.shape[1]
     heads, kv_heads = q_cols // dim, k_cols // dim
     blocks = kv_heads
     strip = down_weight.shape[0]
-    hidden_local = seq * strip
+    members = lax.axis_size(GROUP)
+    depth = members * piece
+    local = line * strip
+    whole = local // 128 * 128
     pad = 128
 
     lengths = doc_lengths[0]
@@ -297,53 +508,57 @@
     base = base.astype(jnp.int32).reshape(1)
 
     gains = jnp.pad(jnp.stack([attn_gain, ffn_gain], axis=1), ((0, 0), (0, pad - 2)))
-
-    def gather_all(array, first, second):
+    index = lax.axis_index(SEQ) * pairs + lax.axis_index(("y", "c"))
+
+    def gather_all(array, first, second, *others):
         places = {"x": 1, "y": 2}
-        array = gather_two(array, first, 1)
+        array = after(gather_two(array, first, 1), *others)
         array = gather_two(array, second, places[second])
         return gather_two(array, "c", 3)
 
-    first_line = gather_line(jnp.concatenate([q_weight, k_weight, v_weight, gains], axis=1))
-    w_query = gather_all(first_line[..., :q_cols], "x", "y").reshape(width, q_cols)
-    w_rest = gather_all(first_line[..., q_cols:], "y", "x").reshape(width, -1)
+    spreaded = spread(gate_weight, up_weight, members, strip)
+    mixed = trade(spreaded).reshape(depth, 2 * local)
+    first_line = gather_line(after(jnp.concatenate([q_weight, k_weight, v_weight, gains], axis=1), spreaded))
+    w_query = gather_all(first_line[..., :q_cols], "x", "y", mixed).reshape(width, q_cols)
+    w_rest = gather_all(first_line[..., q_cols:], "y", "x", mixed).reshape(width, -1)
     w_key, w_value = w_rest[:, :k_cols], w_rest[:, k_cols : 2 * k_cols]
-    gain_rows = w_rest[:, 2 * k_cols : 2 * k_cols + 2].astype(F32).T
-    attn_gain_all, ffn_gain_all = gain_rows[0], gain_rows[1]
-
-    wide = jnp.stack([gate_weight, up_weight], axis=1).reshape(piece, 2, seq, pairs, strip)
-    wide = jnp.transpose(wide, (3, 0, 1, 2, 4)).reshape(pairs, piece, 2 * hidden_local)
-    mixed = jnp.zeros_like(wide)
-    mixed = lax.dynamic_update_index_in_dim(mixed, pick(wide, own, 0), own, 0)
-    for by in range(1, pairs):
-        moved = lax.ppermute(pick(wide, own ^ by, 0), ("y", "c"), [(i, i ^ by) for i in range(pairs)])
-        mixed = lax.dynamic_update_index_in_dim(mixed, moved, own ^ by, 0)
-    mixed = mixed.reshape(pairs * piece, 2 * hidden_local)
-
-    def gather_seq(array):
-        return gather_two(gather_line(array), "x", 1).reshape((-1,) + array.shape[1:])
-
-    w_out = gather_all(gather_line(o_weight), "x", "y").reshape(heads * dim, width)
-    w_gate = gather_seq(mixed[:, :hidden_local])
-    w_up = gather_seq(mixed[:, hidden_local:])
-    w_down = gather_seq(down_weight)
-
-    def gather_pairs(array):
-        return gather_two(gather_two(array, "y", 0), "c", 1).reshape(pairs * rows, -1)
+    w_wide = lax.all_gather(mixed, ZAXES, axis=0, tiled=True)
+
+    quarter = rows // 2
+
+    def plane_parts(array):
+        first, second = array[:quarter], array[quarter:]
+        first_x, second_y = swap(first, "x"), swap(second, "y")
+        far_first = swap(jnp.concatenate([first, first_x], axis=0), "y")
+        far_second = swap(jnp.concatenate([second, second_y], axis=0), "x")
+        parts = ((array,), (first_x, second_y), (far_first, far_second))
+        return [list(part) + [swap(piece, "c") for piece in part] for part in parts]
+
+    def plane_sum(parts):
+        def chip(part):
+            half = part.shape[0] // 2
+            return part[:half].astype(F32) + swap(part[half:].astype(BF), "c").astype(F32)
+
+        def moved(part, axis):
+            return swap(part.astype(BF), axis).astype(F32)
+
+        near, middle, far = [chip(part) for part in parts]
+        from_y, from_x = moved(far[:rows], "y"), moved(far[rows:], "x")
+        first = from_y[:quarter] + moved(middle[:quarter] + from_y[quarter:], "x")
+        second = from_x[:quarter] + moved(middle[quarter:] + from_x[quarter:], "y")
+        return near + jnp.concatenate([first, second], axis=0)
 
     grad_out = cotangent[0]
-    grad_all = gather_pairs(grad_out)
 
     inputs = tokens[0].astype(F32)
     in_factor = rms_factor(inputs)
-    normed = (inputs * in_factor * attn_gain_all).astype(BF)
-    q_pre = dot(w_query, normed, (0, 1)).reshape(heads, dim, rows)
-    k_pre = dot(w_key, normed, (0, 1)).reshape(kv_heads, dim, rows)
-    values = dot(w_value, normed, (0, 1)).astype(BF).reshape(kv_heads, dim, rows)
-    q_gain, k_gain = q_norm_gain.astype(F32), k_norm_gain.astype(F32)
-    queries = prepare(q_pre, q_gain, cosine, sine).astype(BF).reshape(kv_heads, 2 * dim, rows)
-    keys = prepare(k_pre, k_gain, cosine, sine).astype(BF)
-    unit = exchange(jnp.concatenate([queries, keys, values], axis=1))
+    q_gain, k_gain = q_norm_gain.astype(F32)[:, None], k_norm_gain.astype(F32)[:, None]
+    unit, pre, normed, gain_rows = prepare_heads(tokens[0], w_query, w_rest, q_gain, k_gain, cosine, sine)
+    attn_gain_all, ffn_gain_all = gain_rows[0], gain_rows[1]
+    unit = exchange(unit)
+    w_out = lax.all_gather(after(o_weight, mixed), SEQ + ("y", "c"), axis=0, tiled=True)
+    w_down = lax.all_gather(after(down_weight, unit), ZAXES, axis=0, tiled=True)
+    grad_parts = plane_parts(after(grad_out, unit))
     unit_q, unit_kv = unit[:, : 2 * dim], unit[:, 2 * dim :]
     if groups > 1:
         unit_kv = lax.all_gather(unit_kv, "t", axis=0, tiled=True)
@@ -353,57 +568,35 @@
 
     ffn_factor = rms_factor(hidden)
     hn = (hidden * ffn_factor * ffn_gain_all).astype(BF)
-    hn_all = gather_pairs(hn)
-    gate = dot(hn_all, w_gate, (1, 0))
-    up = dot(hn_all, w_up, (1, 0))
-    sig = jax.nn.sigmoid(gate)
-    silu = gate * sig
-    act = (silu * up).astype(BF)
-    d_act = dot(grad_all, w_down, (1, 1))
-    d_gate = (d_act * up * (sig * (1.0 + gate * (1.0 - sig)))).astype(BF)
-    d_up = (d_act * silu).astype(BF)
-
-    def split_rows(array, side):
-        return pick(array.reshape(half_pairs, 2, rows, -1), side, 1).reshape(half_pairs * rows, -1)
-
-    def scatter_pairs(product):
-        sent = swap(product(1 - side_c).astype(BF), "c")
-        kept = (product(side_c) + sent.astype(F32)).reshape(half_pairs, rows, -1)
-        return scatter_two(kept, "y", 0)
-
-    d_hn = scatter_pairs(
-        lambda side: dot(split_rows(d_gate, side), w_gate, (1, 1)) + dot(split_rows(d_up, side), w_up, (1, 1))
-    )
-    result = hidden + scatter_pairs(lambda side: dot(split_rows(act, side), w_down, (1, 0)))
-    output = result.astype(BF)[None]
-
-    def scatter_seq(left, right):
-        part = left.shape[1] // (line * 2)
-        cut = left.reshape(left.shape[0], line, 2, part)
-
-        def product(side):
-            return dot(pick(cut, side, 2).reshape(left.shape[0], line * part), right, (0, 0))
-
-        sent = swap(product(1 - side_x).astype(BF), "x")
-        kept = product(side_x) + sent.astype(F32)
-        return scatter_line(kept.reshape(line, part, -1))
-
-    down_grad = scatter_seq(act, grad_all)
-    gate_part = scatter_seq(hn_all, d_gate)
-    up_part = scatter_seq(hn_all, d_up)
-    parts = jnp.concatenate([gate_part, up_part], axis=1).astype(BF).reshape(pairs, piece, 2, seq, strip)
-    wide_grad = jnp.zeros_like(parts)
-    wide_grad = lax.dynamic_update_index_in_dim(wide_grad, pick(parts, own, 0), own, 0)
-    for by in range(1, pairs):
-        moved = lax.ppermute(pick(parts, own ^ by, 0), ("y", "c"), [(i, i ^ by) for i in range(pairs)])
-        wide_grad = lax.dynamic_update_index_in_dim(wide_grad, moved, own ^ by, 0)
-    wide_grad = jnp.transpose(wide_grad, (2, 1, 3, 0, 4)).astype(F32).reshape(2, piece, -1)
+    hn_parts = plane_parts(hn)
+
+    done = []
+    for part, grad in zip(hn_parts, grad_parts):
+        part = list(part)
+        if done:
+            part[0] = after(part[0], done[-1][4])
+        done.append(ffn(part, grad, w_wide, w_down))
+    hns, grad_alls, acts, d_boths, d_hn_parts = zip(*done)
+    d_hn = plane_sum(d_hn_parts)
 
     d_hidden = grad_out.astype(F32) + rms_back(hidden, ffn_factor, ffn_gain_all, d_hn)
     ffn_gain_part = jnp.sum(d_hn * hidden * ffn_factor, axis=0)
     d_branch = d_hidden.astype(BF)
     d_attn = dot(w_out, d_branch, (1, 1)).astype(BF).reshape(kv_heads, 2 * dim, rows)
     unit_grad = exchange(d_attn)
+
+    acts, d_boths, _ = lax.optimization_barrier((acts, d_boths, d_branch))
+
+    def over_parts(lefts, rights):
+        return sum(dot(left, right, (0, 0)) for left, right in zip(lefts, rights)).astype(BF)
+
+    wide_grad = over_parts(hns, d_boths)
+    down_grad = over_parts(acts, grad_alls)
+    unit_grad = after(unit_grad, wide_grad, down_grad)
+    wide_grad = lax.psum_scatter(wide_grad, ZAXES, scatter_dimension=0, tiled=True)
+    down_grad = lax.psum_scatter(down_grad, ZAXES, scatter_dimension=0, tiled=True).astype(F32)
+    gate_grad, up_grad = weave(trade(wide_grad.reshape(members, piece, -1)), strip)
+    output = (hidden + plane_sum([dot(act, w_down, (1, 0)) for act in acts])).astype(BF)[None]
 
     def scatter_rest(array, first, second):
         places = {"x": 1, "y": 2}
@@ -431,22 +624,8 @@
     unit_dq, unit_dkv = attend_back(base, start_rows, unit_q, unit_kv, exact, mass, unit_grad, dim)
     if groups > 1:
         unit_dkv = lax.psum_scatter(unit_dkv.astype(F32), "t", scatter_dimension=0, tiled=True).astype(BF)
-    back = exchange(jnp.concatenate([unit_dq, unit_dkv], axis=1)).astype(F32)
-    d_queries = back[:, : 2 * dim].reshape(heads, dim, rows)
-    d_keys = back[:, 2 * dim : 3 * dim]
-    d_values = back[:, 3 * dim :]
-    _, query_pull = jax.vjp(lambda pre, gain: prepare(pre, gain, cosine, sine), q_pre, q_gain)
-    _, key_pull = jax.vjp(lambda pre, gain: prepare(pre, gain, cosine, sine), k_pre, k_gain)
-    d_q_pre, q_gain_grad = query_pull(d_queries)
-    d_k_pre, k_gain_grad = key_pull(d_keys)
-    d_pre = jnp.concatenate(
-        [d_q_pre.reshape(q_cols, rows), d_k_pre.reshape(k_cols, rows), d_values.reshape(k_cols, rows)], axis=0
-    ).astype(BF)
-
-    small = jnp.stack([q_gain_grad, k_gain_grad])
-    for axis in ("c", "y", "x"):
-        small = small + swap(small, axis)
-    small = sum((shift(small, ZAXES, by) for by in range(1, line)), small)
+    back = exchange(jnp.concatenate([unit_dq, unit_dkv], axis=1))
+    d_pre, q_gain_grad, k_gain_grad = prepare_back(back, pre, q_gain, k_gain, cosine, sine)
 
     d_normed = (
         dot(d_pre[:q_cols], w_query, (0, 1))
@@ -456,12 +635,19 @@
     attn_gain_part = jnp.sum(d_normed * inputs * in_factor, axis=0)
     input_grad = (d_hidden + rms_back(inputs, in_factor, attn_gain_all, d_normed))[None]
 
-    gain_parts = jnp.pad(jnp.stack([attn_gain_part, ffn_gain_part], axis=1), ((0, 0), (0, pad - 2)))
+    small = jnp.concatenate([attn_gain_part, ffn_gain_part, q_gain_grad[:, 0], k_gain_grad[:, 0]])[None]
+    for axis in ("c", "y", "x"):
+        small = small + swap(small, axis)
+    small = sum((shift(small, ZAXES, by) for by in range(1, line)), small)[0]
+
+    def own_piece(vector):
+        return pick(vector.reshape(-1, piece), index, 0)
+
     normed_cut = normed.reshape(rows, line * 2 * half_pairs, 2, piece)
 
     def pre_product(side):
         left = pick(normed_cut, side, 2).reshape(rows, -1)
-        return jnp.concatenate([dot(left, d_pre, (0, 1)), cut_core(gain_parts, side)], axis=1)
+        return dot(left, d_pre, (0, 1))
 
     kept = pre_product(side_c) + swap(pre_product(1 - side_c).astype(BF), "c").astype(F32)
     kept = kept.reshape(line, 2, half_pairs, piece, -1)
@@ -474,16 +660,16 @@
     return (
         output,
         input_grad,
-        rest[:, 2 * k_cols],
+        own_piece(small[:width]),
         shares[:, :q_cols],
         rest[:, :k_cols],
-        rest[:, k_cols : 2 * k_cols],
-        small[0],
-        small[1],
+        rest[:, k_cols:],
+        small[2 * width : 2 * width + dim],
+        small[2 * width + dim :],
         out_grad,
-        rest[:, 2 * k_cols + 1],
-        wide_grad[0],
-        wide_grad[1],
+        own_piece(small[width : 2 * width]),
+        gate_grad,
+        up_grad,
         down_grad,
     )
 

time: 607 us -> 472 us (0.78)
  local copies, waits for them, and re-layouts: 146 us -> 50.1 us
  starting transfers between devices: 128 us -> 84.6 us
  Pallas kernels: 34.4 us -> 70.4 us
  other arithmetic: 66.4 us -> 34.9 us
  matrix products: 64.9 us -> 38 us
  waiting for transfers between devices: 152 us -> 170 us
  between operations: 3.11 us -> 15.7 us
    dynamic_update_slice x7 -> x0, local copies, waits for them, and re-layouts: 44.9 us -> none  [the longest x3 33.6 us: on_device(): wide_grad = lax.dynamic_update_index_in_dim(wide_grad, moved, own ^ by, 0)]
    ppermute x33 -> x12, starting transfers between devices: 65.6 us -> 20.9 us  [shift(): lax.ppermute(array, axes, [(i, (i + by) % count) for i in range(count)])]
    pallas_call x0 -> x7, Pallas kernels: none -> 35.7 us  [the longest x3 27.8 us: ffn(): pl.pallas_call(functools.partial(ffn_kernel, len(tokens)), out_shape=tupl...]
    ppermute x33 -> x12, waiting for transfers between devices: 39.1 us -> 4.09 us  [shift(): lax.ppermute(array, axes, [(i, (i + by) % count) for i in range(count)])]
    all_to_all x4, waiting for transfers between devices: 25.7 us -> 56.3 us  [exchange(): return lax.all_to_all(blocks, HEADS, 0, 0, tiled=True)]
    select_n x24 -> x8, other arithmetic: 32.5 us -> 2.89 us  [gather_two(): jnp.where(first, jnp.stack([array, other], place), jnp.stack([other, arra...]
    dot_general x27 -> x18, matrix products: 64.9 us -> 38 us  [dot(): lax.dot_general(left, right, ((contract[:1], contract[1:]), ((), ())), pr...]
    ppermute x36 -> x51, waiting for transfers between devices: 76.2 us -> 98.6 us  [swap(): return lax.ppermute(array, axis, [(0, 1), (1, 0)])]
  transfers between devices with their start and end apart: 79 -> 74, of which waited for: 28 -> 26; matrix products, arithmetic and copies ran while one was open for 39% -> 18% of each run, Pallas kernels for 6% -> 12%
where the time goes in v2:
time: 472 us; the launch traced here: 463 us
  waiting for transfers between devices  170 us (36%)
  starting transfers between devices  84.6 us (18%)
  Pallas kernels  70.4 us (15%)
  local copies, waits for them, and re-layouts  50.1 us (11%)
  matrix products  38 us (8%)
  other arithmetic  34.9 us (7%)
  between operations  15.7 us (3%)
    ppermute x51, waiting for transfers between devices, swap(): return lax.ppermute(array, axis, [(0, 1), (1, 0)])  98.6 us
    all_to_all x4, waiting for transfers between devices, exchange(): return lax.all_to_all(blocks, HEADS, 0, 0, tiled=True)  56.3 us
    dot_general x18, matrix products, dot(): lax.dot_general(left, right, ((contract[:1], contract[1:]), ((), ())), pr...  38 us
    ppermute x51, starting transfers between devices, swap(): return lax.ppermute(array, axis, [(0, 1), (1, 0)])  37.4 us
    unnamed x181, local copies, waits for them, and re-layouts  30 us
    pallas_call x3, Pallas kernels, ffn(): pl.pallas_call(functools.partial(ffn_kernel, len(tokens)), out_shape=tupl...  27.8 us
    ppermute x12, starting transfers between devices, shift(): lax.ppermute(array, axes, [(i, (i + by) % count) for i in range(count)])  20.9 us
    pallas_call x1, Pallas kernels, attend_back(): pl.pallas_call(functools.partial(attend_back_kernel, dim ** (-0.5) * LOG2...  20.4 us
  transfers between devices with their start and end apart: 74, of which 26 were waited for; matrix products, arithmetic and copies ran while one was open for 18% of the time, Pallas kernels for 12%

profile of v2, /device:TPU:0, one launch (start us, length us, event | category | flops | bytes accessed | tf_op | source)
XLA Modules:
  0.0 463.3 jit_solution(15631314617952645538)
XLA Ops:
  12.0 3.1 collective-permute-start
  15.0 2.6 collective-permute-start.1
  19.0 3.7 all-to-all-start
  23.0 9.2 %all-to-all-done = bf16[8,32,1152]{2,1,0:T(8,128)(2,1)S(1)} async-done(((bf16[8,32,1152]{2,1,0:T(8,128)(2,1)}), bf16[8,32,1152]{2,1,0:T(8,128)(2,1)S(1)}, u32[]{:S(2)}, u32[]{:S(2)}) %all-to-all-start) | async-done | bytes 589856 | tf_op jit(solution)/shard_map/all_to_all | solution.py:449
  34.9 5.7 %collective-permute-done.3 = bf16[4,32,1024]{2,1,0:T(8,128)(2,1)S(1)} collective-permute-done((bf16[4,32,1024]{2,1,0:T(8,128)(2,1)S(1)}, bf16[4,32,1024]{2,1,0:T(8,128)(2,1)S(1)}, u32[]{:S(2)}, u32[]{:S(2)}) %collective-permute-start.3) | collective-permute-done | bytes 262176 | tf_op jit(solution)/shard_map/ppermute | solution.py:29
  45.7 9.6 %collective-permute-done.4 = bf16[4,2,32,1024]{3,2,0,1:T(8,128)(2,1)S(1)} collective-permute-done((bf16[4,2,32,1024]{3,2,0,1:T(8,128)(2,1)S(1)}, bf16[4,2,32,1024]{3,2,0,1:T(8,128)(2,1)S(1)}, u32[]{:S(2)}, u32[]{:S(2)}) %collective-permute-start.4) | collective-permute-done | bytes 524320 | tf_op jit(solution)/shard_map/ppermute | solution.py:29
  61.6 3.3 prepare.1
  67.0 4.2 all-to-all-start.1
  71.5 31.1 %all-to-all-done.1 = bf16[8,256,256]{2,1,0:T(8,128)(2,1)} async-done(((bf16[8,256,256]{2,1,0:T(8,128)(2,1)}), bf16[8,256,256]{2,1,0:T(8,128)(2,1)}, u32[]{:S(2)}, u32[]{:S(2)}) %all-to-all-start.1) | async-done | bytes 1048608 | tf_op jit(solution)/shard_map/all_to_all | solution.py:453
  103.9 14.3 %attend.1 = (bf16[8,128,256]{2,1,0:T(8,128)(2,1)S(1)}, f32[8,128,256]{2,1,0:T(8,128)S(1)}, f32[8,1,512]{2,1,0:T(1,128)S(1)}) custom-call(s32[1]{0:T(128)} %constant.181.clone.1.base_ref, s32[8,1,256]{2,1,0:T(1,128)S(1)} %bitcast.182, bf16[8,128,256]{2,1,0:T(8,128)(2,1)S(1)} %get-tuple-element.125.q_ref, bf16[8,128,256]{2,1,0:T(8,128)(2,1)S(1)} %get-tuple-element.124.kv_ref), custom_call_target="tpu_custom_call" | custom-call | flops 1207959552 | bytes 4194304 | tf_op jit(solution)/shard_map/attend/pallas_call | solution.py:322
  120.6 4.1 all-to-all-start.2
  129.6 25.2 %all-to-all-done.2 = bf16[8,128,256]{2,1,0:T(8,128)(2,1)} async-done(((bf16[8,128,256]{2,1,0:T(8,128)(2,1)}), bf16[8,128,256]{2,1,0:T(8,128)(2,1)}, u32[]{:S(2)}, u32[]{:S(2)}) %all-to-all-start.2) | async-done | bytes 524320 | tf_op jit(solution)/shard_map/all_to_all | solution.py:453
  154.8 2.6 multiply_reduce_fusion.2
  162.6 3.6 collective-permute-done.12.refs_1_
  173.4 6.7 %collective-permute-done.24.refs_5_ = bf16[256,1024]{1,0:T(8,128)(2,1)} collective-permute-done((bf16[256,1024]{1,0:T(8,128)(2,1)S(1)}, bf16[256,1024]{1,0:T(8,128)(2,1)}, u32[]{:S(2)}, u32[]{:S(2)}) %collective-permute-start.24) | collective-permute-done | bytes 524320 | tf_op jit(solution)/shard_map/ppermute | solution.py:29
  180.0 3.1 collective-permute-done.23.refs_4_
  185.2 4.7 %collective-permute-done.20.refs_1_ = bf16[256,1024]{1,0:T(8,128)(2,1)} collective-permute-done((bf16[256,1024]{1,0:T(8,128)(2,1)S(1)}, bf16[256,1024]{1,0:T(8,128)(2,1)}, u32[]{:S(2)}, u32[]{:S(2)}) %collective-permute-start.20) | collective-permute-done | bytes 524320 | tf_op jit(solution)/shard_map/ppermute | solution.py:29
  189.9 4.1 collective-permute-done.19.refs_0_
  196.1 7.0 %ffn.3 = (bf16[512,1024]{1,0:T(8,128)(2,1)S(1)}, bf16[512,1024]{1,0:T(8,128)(2,1)S(1)}, bf16[512,576]{1,0:T(8,128)(2,1)S(1)}, bf16[512,1152]{1,0:T(8,128)(2,1)}, bf16[512,1024]{1,0:T(8,128)(2,1)S(1)}) custom-call(bf16[256,1024]{1,0:T(8,128)(2,1)S(1)} %copy-done.5, bf16[256,1024]{1,0:T(8,128)(2,1)S(1)} %copy-done.36, bf16[256,1024]{1,0:T(8,128)(2,1)S(1)} %bitcast.181, ...), custom_call_target="tpu_custom_call" | custom-call | flops 3019898880 | bytes 4194304 | tf_op jit(solution)/shard_map/ffn/pallas_call | solution.py:435
  206.9 6.9 %ffn.4 = (bf16[512,1024]{1,0:T(8,128)(2,1)S(1)}, bf16[512,1024]{1,0:T(8,128)(2,1)S(1)}, bf16[512,576]{1,0:T(8,128)(2,1)S(1)}, bf16[512,1152]{1,0:T(8,128)(2,1)}, bf16[512,1024]{1,0:T(8,128)(2,1)S(1)}) custom-call(bf16[128,1024]{1,0:T(8,128)(2,1)S(1)} %copy-done.31, bf16[128,1024]{1,0:T(8,128)(2,1)} %collective-permute-done.12.refs_1_, ...), custom_call_target="tpu_custom_call" | custom-call | flops 3019898880 | bytes 4194304 | tf_op jit(solution)/shard_map/ffn/pallas_call | solution.py:435
  216.6 14.0 %ffn.5 = (bf16[1024,1024]{1,0:T(8,128)(2,1)}, bf16[1024,1024]{1,0:T(8,128)(2,1)}, bf16[1024,576]{1,0:T(8,128)(2,1)}, bf16[1024,1152]{1,0:T(8,128)(2,1)}, bf16[1024,1024]{1,0:T(8,128)(2,1)}) custom-call(bf16[256,1024]{1,0:T(8,128)(2,1)} %collective-permute-done.19.refs_0_, bf16[256,1024]{1,0:T(8,128)(2,1)} %collective-permute-done.20.refs_1_, ...), custom_call_target="tpu_custom_call" | custom-call | flops 6039797760 | bytes 8388608 | tf_op jit(solution)/shard_map/ffn/pallas_call | solution.py:435
  232.7 2.2 collective-permute-done.28
  238.7 10.9 %collective-permute-done.29 = bf16[256,1024]{1,0:T(8,128)(2,1)S(1)} collective-permute-done((bf16[256,1024]{1,0:T(8,128)(2,1)S(1)}, bf16[256,1024]{1,0:T(8,128)(2,1)S(1)}, u32[]{:S(2)}, u32[]{:S(2)}) %collective-permute-start.29) | collective-permute-done | bytes 524320 | tf_op jit(solution)/shard_map/ppermute | solution.py:29
  263.6 5.5 %collective-permute-done.33 = bf16[128,1024]{1,0:T(8,128)(2,1)S(1)} collective-permute-done((bf16[128,1024]{1,0:T(8,128)(2,1)}, bf16[128,1024]{1,0:T(8,128)(2,1)S(1)}, u32[]{:S(2)}, u32[]{:S(2)}) %collective-permute-start.33) | collective-permute-done | bytes 262176 | tf_op jit(solution)/shard_map/ppermute | solution.py:29
  274.5 4.1 all-to-all-start.3
  278.9 2.3 fusion.67
  290.0 2.5 add_convert_fusion.1
  292.5 3.3 fusion.64
  295.8 3.0 fusion.65
  298.9 3.2 add_convert_fusion
  302.1 2.5 slice_add_fusion.1
  307.9 20.4 %attend_back.1 = (bf16[8,128,256]{2,1,0:T(8,128)(2,1)S(1)}, bf16[8,128,256]{2,1,0:T(8,128)(2,1)S(1)}) custom-call(s32[1]{0:T(128)} %constant.181.clone.1.base_ref, s32[8,1,256]{2,1,0:T(1,128)S(1)} %bitcast.183, bf16[8,128,256]{2,1,0:T(8,128)(2,1)S(1)} %copy-done.27, bf16[8,128,256]{2,1,0:T(8,128)(2,1)S(1)} %copy-done.25, f32[8,128,256]{2,1,0:T(8,128)S(1)} %copy-done.44, ...), custom_call_target="tpu_custom_call" | custom-call | flops 3019898880 | bytes 4194304 | tf_op jit(solution)/shard_map/attend_back/pallas_call | solution.py:344
  329.4 5.9 %all-to-all-start.4 = ((bf16[8,256,256]{2,1,0:T(8,128)(2,1)}), bf16[8,256,256]{2,1,0:T(8,128)(2,1)}, u32[]{:S(2)}, u32[]{:S(2)}) async-start(bf16[8,256,256]{2,1,0:T(8,128)(2,1)} %pad_maximum_fusion.3), calls=%async_computation.4 | async-start | bytes 2097152 | tf_op jit(solution)/shard_map/all_to_all | solution.py:453
  343.9 3.0 collective-permute-done.58
  349.1 6.6 %collective-permute-done.56 = bf16[4,2,32,512]{3,2,0,1:T(8,128)(2,1)S(1)} collective-permute-done((bf16[4,2,32,512]{3,2,0,1:T(8,128)(2,1)S(1)}, bf16[4,2,32,512]{3,2,0,1:T(8,128)(2,1)S(1)}, u32[]{:S(2)}, u32[]{:S(2)}) %collective-permute-start.56) | collective-permute-done | bytes 262176 | tf_op jit(solution)/shard_map/ppermute | solution.py:29
  356.0 13.2 %collective-permute-done.59 = bf16[4,32,512]{2,1,0:T(8,128)(2,1)S(1)} collective-permute-done((bf16[4,32,512]{2,1,0:T(8,128)(2,1)S(1)}, bf16[4,32,512]{2,1,0:T(8,128)(2,1)S(1)}, u32[]{:S(2)}, u32[]{:S(2)}) %collective-permute-start.59) | collective-permute-done | bytes 131104 | tf_op jit(solution)/shard_map/ppermute | solution.py:29
  371.5 2.4 collective-permute-start.61
  387.7 2.3 prepare_back.1
  392.1 2.2 convolution_convert_fusion
  396.3 3.3 fusion.8
  404.7 2.9 collective-permute-done.42
  408.1 4.2 fusion.6
  413.3 2.9 collective-permute-start.46
  416.2 2.3 convert_add_fusion
  421.7 9.8 %collective-permute-done.50 = bf16[4,2,32,1024]{3,2,1,0:T(8,128)(2,1)S(1)} collective-permute-done((bf16[4,2,32,1024]{3,2,1,0:T(8,128)(2,1)S(1)}, bf16[4,2,32,1024]{3,2,1,0:T(8,128)(2,1)S(1)}, u32[]{:S(2)}, u32[]{:S(2)}) %collective-permute-start.50) | collective-permute-done | bytes 524320 | tf_op jit(solution)/shard_map/ppermute | solution.py:29
  436.6 3.5 all-to-all-start.5
  444.8 2.8 collective-permute-start.54
  451.3 3.7 collective-permute-done.53
  (429 shorter events, 148.1 us)
Async XLA Ops:
  12.0 20.5 %collective-permute-start = (bf16[32,2176]{1,0:T(8,128)(2,1)S(1)}, bf16[32,2176]{1,0:T(8,128)(2,1)S(1)}, u32[]{:S(2)}, u32[]{:S(2)}) collective-permute-start(bf16[32,2176]{1,0:T(8,128)(2,1)S(1)} %fusion.38), channel_id=1, source_target_pairs={{0,8},{8,16},{16,24},{24,0},{1,9},{9,17},{17,25},{25,1},{2,10},{10... | collective-permute-start | bytes 417800 | tf_op jit(solution)/shard_map/ppermute | solution.py:44
  15.0 17.5 %collective-permute-start.1 = (bf16[32,2176]{1,0:T(8,128)(2,1)S(1)}, bf16[32,2176]{1,0:T(8,128)(2,1)S(1)}, u32[]{:S(2)}, u32[]{:S(2)}) collective-permute-start(bf16[32,2176]{1,0:T(8,128)(2,1)S(1)} %fusion.38), channel_id=1, source_target_pairs={{0,16},{8,24},{16,0},{24,8},{1,17},{9,25},{17,1},{25,9},{2,18},{10... | collective-permute-start | bytes 417800 | tf_op jit(solution)/shard_map/ppermute | solution.py:44
  17.6 14.9 %collective-permute-start.2 = (bf16[32,2176]{1,0:T(8,128)(2,1)S(1)}, bf16[32,2176]{1,0:T(8,128)(2,1)S(1)}, u32[]{:S(2)}, u32[]{:S(2)}) collective-permute-start(bf16[32,2176]{1,0:T(8,128)(2,1)S(1)} %fusion.38), channel_id=1, source_target_pairs={{0,24},{8,0},{16,8},{24,16},{1,25},{9,1},{17,9},{25,17},{2,26},{10... | collective-permute-start | bytes 417800 | tf_op jit(solution)/shard_map/ppermute | solution.py:44
  19.0 13.3 %all-to-all-start = ((bf16[8,32,1152]{2,1,0:T(8,128)(2,1)}), bf16[8,32,1152]{2,1,0:T(8,128)(2,1)S(1)}, u32[]{:S(2)}, u32[]{:S(2)}) async-start(bf16[8,32,1152]{2,1,0:T(8,128)(2,1)} %spread.1), calls=%async_computation | async-start | bytes 1179648 | tf_op jit(solution)/shard_map/all_to_all | solution.py:449
  22.7 106.9 %all-gather.4.cloned.1.call-start = ((), (), s32[]{:S(2)}) async-start(), calls=%async_computation.8 | async-start | bytes 2162688 | tf_op jit(solution)/shard_map/all_gather | solution.py:559
  32.3 161.7 %all-gather.6.cloned.1.call-start = ((), (), s32[]{:S(2)}) async-start(), calls=%async_computation.9 | async-start | bytes 2949120 | tf_op jit(solution)/shard_map/all_gather | solution.py:525
  42.5 13.0 %collective-permute-start.7 = (bf16[4,2,32,1152]{3,2,1,0:T(8,128)(2,1)S(1)}, bf16[4,2,32,1152]{3,2,1,0:T(8,128)(2,1)S(1)}, u32[]{:S(2)}, u32[]{:S(2)}) collective-permute-start(bf16[4,2,32,1152]{3,2,1,0:T(8,128)(2,1)S(1)} %maximum_select_fusion.5), channel_id=1, source_target_pairs={{0,4},{4,0},{1,5},{5,1},{2,6},{6,2},{3,7},{7,3},{8,12},{12,8},{9,1... | collective-permute-start | bytes 1769480 | tf_op jit(solution)/shard_map/ppermute | solution.py:29
  43.7 11.5 %collective-permute-start.4 = (bf16[4,2,32,1024]{3,2,0,1:T(8,128)(2,1)S(1)}, bf16[4,2,32,1024]{3,2,0,1:T(8,128)(2,1)S(1)}, u32[]{:S(2)}, u32[]{:S(2)}) collective-permute-start(bf16[4,2,32,1024]{3,2,0,1:T(8,128)(2,1)S(1)} %maximum_select_fusion.6), channel_id=1, source_target_pairs={{0,2},{2,0},{1,3},{3,1},{4,6},{6,4},{5,7},{7,5},{8,10},{10,8},{9,1... | collective-permute-start | bytes 1572872 | tf_op jit(solution)/shard_map/ppermute | solution.py:29
  67.0 35.5 %all-to-all-start.1 = ((bf16[8,256,256]{2,1,0:T(8,128)(2,1)}), bf16[8,256,256]{2,1,0:T(8,128)(2,1)}, u32[]{:S(2)}, u32[]{:S(2)}) async-start(bf16[8,256,256]{2,1,0:T(8,128)(2,1)} %copy-done.13), calls=%async_computation.1 | async-start | bytes 2097152 | tf_op jit(solution)/shard_map/all_to_all | solution.py:453
  120.6 34.2 %all-to-all-start.2 = ((bf16[8,128,256]{2,1,0:T(8,128)(2,1)}), bf16[8,128,256]{2,1,0:T(8,128)(2,1)}, u32[]{:S(2)}, u32[]{:S(2)}) async-start(bf16[8,128,256]{2,1,0:T(8,128)(2,1)} %copy-done.23), calls=%async_computation.2 | async-start | bytes 1048576 | tf_op jit(solution)/shard_map/all_to_all | solution.py:453
  124.7 69.2 %all-gather.8.cloned.1.call-start = ((), (), s32[]{:S(2)}) async-start(), calls=%async_computation.10 | async-start | bytes 1474560 | tf_op jit(solution)/shard_map/all_gather | solution.py:560
  125.4 42.8 %collective-permute-start.10 = (bf16[256,1024]{1,0:T(8,128)(2,1)S(1)}, bf16[256,1024]{1,0:T(8,128)(2,1)}, u32[]{:S(2)}, u32[]{:S(2)}) collective-permute-start(bf16[256,1024]{1,0:T(8,128)(2,1)S(1)} %bitcast.179), channel_id=1, source_target_pairs={{0,1},{1,0},{2,3},{3,2},{4,5},{5,4},{6,7},{7,6},{8,9},{9,8},{10,11... | collective-permute-start | bytes 1572872 | tf_op jit(solution)/shard_map/ppermute | solution.py:29
  126.2 36.4 %collective-permute-start.15 = (bf16[128,1024]{1,0:T(8,128)(2,1)}, bf16[128,1024]{1,0:T(8,128)(2,1)S(1)}, u32[]{:S(2)}, u32[]{:S(2)}) collective-permute-start(bf16[128,1024]{1,0:T(8,128)(2,1)} %get-tuple-element.138), channel_id=1, source_target_pairs={{0,4},{4,0},{1,5},{5,1},{2,6},{6,2},{3,7},{7,3},{8,12},{12,8},{9,1... | collective-permute-start | bytes 786440 | tf_op jit(solution)/shard_map/ppermute | solution.py:29
  128.1 32.8 %collective-permute-start.16 = (bf16[128,1024]{1,0:T(8,128)(2,1)}, bf16[128,1024]{1,0:T(8,128)(2,1)}, u32[]{:S(2)}, u32[]{:S(2)}) collective-permute-start(bf16[128,1024]{1,0:T(8,128)(2,1)} %get-tuple-element.137), channel_id=1, source_target_pairs={{0,2},{2,0},{1,3},{3,1},{4,6},{6,4},{5,7},{7,5},{8,10},{10,8},{9,1... | collective-permute-start | bytes 786440 | tf_op jit(solution)/shard_map/ppermute | solution.py:29
  159.5 10.2 %collective-permute-start.11 = (bf16[128,1024]{1,0:T(8,128)(2,1)S(1)}, bf16[128,1024]{1,0:T(8,128)(2,1)S(1)}, u32[]{:S(2)}, u32[]{:S(2)}) collective-permute-start(bf16[128,1024]{1,0:T(8,128)(2,1)S(1)} %get-tuple-element.140), channel_id=1, source_target_pairs={{0,4},{4,0},{1,5},{5,1},{2,6},{6,2},{3,7},{7,3},{8,12},{12,8},{9,1... | collective-permute-start | bytes 786440 | tf_op jit(solution)/shard_map/ppermute | solution.py:29
  162.0 18.1 %collective-permute-start.24 = (bf16[256,1024]{1,0:T(8,128)(2,1)S(1)}, bf16[256,1024]{1,0:T(8,128)(2,1)}, u32[]{:S(2)}, u32[]{:S(2)}) collective-permute-start(bf16[256,1024]{1,0:T(8,128)(2,1)S(1)} %pad_maximum_fusion.8), channel_id=1, source_target_pairs={{0,4},{4,0},{1,5},{5,1},{2,6},{6,2},{3,7},{7,3},{8,12},{12,8},{9,1... | collective-permute-start | bytes 1572872 | tf_op jit(solution)/shard_map/ppermute | solution.py:29
  168.2 14.9 %collective-permute-start.23 = (bf16[256,1024]{1,0:T(8,128)(2,1)S(1)}, bf16[256,1024]{1,0:T(8,128)(2,1)}, u32[]{:S(2)}, u32[]{:S(2)}) collective-permute-start(bf16[256,1024]{1,0:T(8,128)(2,1)S(1)} %pad_maximum_fusion.7), channel_id=1, source_target_pairs={{0,2},{2,0},{1,3},{3,1},{4,6},{6,4},{5,7},{7,5},{8,10},{10,8},{9,1... | collective-permute-start | bytes 1572872 | tf_op jit(solution)/shard_map/ppermute | solution.py:29
  169.7 13.4 %collective-permute-start.9 = (bf16[256,1024]{1,0:T(8,128)(2,1)S(1)}, bf16[256,1024]{1,0:T(8,128)(2,1)S(1)}, u32[]{:S(2)}, u32[]{:S(2)}) collective-permute-start(bf16[256,1024]{1,0:T(8,128)(2,1)S(1)} %multiply_convert_fusion.refs_0_), channel_id=1, source_target_pairs={{0,1},{1,0},{2,3},{3,2},{4,5},{5,4},{6,7},{7,6},{8,9},{9,8},{10,11... | collective-permute-start | bytes 1572872 | tf_op jit(solution)/shard_map/ppermute | solution.py:29
  170.8 19.1 %collective-permute-start.20 = (bf16[256,1024]{1,0:T(8,128)(2,1)S(1)}, bf16[256,1024]{1,0:T(8,128)(2,1)}, u32[]{:S(2)}, u32[]{:S(2)}) collective-permute-start(bf16[256,1024]{1,0:T(8,128)(2,1)S(1)} %pad_maximum_fusion.6), channel_id=1, source_target_pairs={{0,4},{4,0},{1,5},{5,1},{2,6},{6,2},{3,7},{7,3},{8,12},{12,8},{9,1... | collective-permute-start | bytes 1572872 | tf_op jit(solution)/shard_map/ppermute | solution.py:29
  172.9 21.0 %collective-permute-start.19 = (bf16[256,1024]{1,0:T(8,128)(2,1)S(1)}, bf16[256,1024]{1,0:T(8,128)(2,1)}, u32[]{:S(2)}, u32[]{:S(2)}) collective-permute-start(bf16[256,1024]{1,0:T(8,128)(2,1)S(1)} %pad_maximum_fusion.5), channel_id=1, source_target_pairs={{0,2},{2,0},{1,3},{3,1},{4,6},{6,4},{5,7},{7,5},{8,10},{10,8},{9,1... | collective-permute-start | bytes 1572872 | tf_op jit(solution)/shard_map/ppermute | solution.py:29
  183.1 33.4 %collective-permute-start.26 = (bf16[256,1024]{1,0:T(8,128)(2,1)}, bf16[256,1024]{1,0:T(8,128)(2,1)}, u32[]{:S(2)}, u32[]{:S(2)}) collective-permute-start(bf16[256,1024]{1,0:T(8,128)(2,1)} %collective-permute-done.24.refs_5_), channel_id=1, source_target_pairs={{0,1},{1,0},{2,3},{3,2},{4,5},{5,4},{6,7},{7,6},{8,9},{9,8},{10,11... | collective-permute-start | bytes 1572872 | tf_op jit(solution)/shard_map/ppermute | solution.py:29
  183.9 32.6 %collective-permute-start.25 = (bf16[256,1024]{1,0:T(8,128)(2,1)}, bf16[256,1024]{1,0:T(8,128)(2,1)}, u32[]{:S(2)}, u32[]{:S(2)}) collective-permute-start(bf16[256,1024]{1,0:T(8,128)(2,1)} %collective-permute-done.23.refs_4_), channel_id=1, source_target_pairs={{0,1},{1,0},{2,3},{3,2},{4,5},{5,4},{6,7},{7,6},{8,9},{9,8},{10,11... | collective-permute-start | bytes 1572872 | tf_op jit(solution)/shard_map/ppermute | solution.py:29
  185.2 21.7 %collective-permute-start.14 = (bf16[128,1024]{1,0:T(8,128)(2,1)}, bf16[128,1024]{1,0:T(8,128)(2,1)}, u32[]{:S(2)}, u32[]{:S(2)}) collective-permute-start(bf16[128,1024]{1,0:T(8,128)(2,1)} %collective-permute-done.12.refs_1_), channel_id=1, source_target_pairs={{0,1},{1,0},{2,3},{3,2},{4,5},{5,4},{6,7},{7,6},{8,9},{9,8},{10,11... | collective-permute-start | bytes 786440 | tf_op jit(solution)/shard_map/ppermute | solution.py:29
  189.9 26.7 %collective-permute-start.22 = (bf16[256,1024]{1,0:T(8,128)(2,1)}, bf16[256,1024]{1,0:T(8,128)(2,1)}, u32[]{:S(2)}, u32[]{:S(2)}) collective-permute-start(bf16[256,1024]{1,0:T(8,128)(2,1)} %collective-permute-done.20.refs_1_), channel_id=1, source_target_pairs={{0,1},{1,0},{2,3},{3,2},{4,5},{5,4},{6,7},{7,6},{8,9},{9,8},{10,11... | collective-permute-start | bytes 1572872 | tf_op jit(solution)/shard_map/ppermute | solution.py:29
  194.0 22.6 %collective-permute-start.21 = (bf16[256,1024]{1,0:T(8,128)(2,1)}, bf16[256,1024]{1,0:T(8,128)(2,1)}, u32[]{:S(2)}, u32[]{:S(2)}) collective-permute-start(bf16[256,1024]{1,0:T(8,128)(2,1)} %collective-permute-done.19.refs_0_), channel_id=1, source_target_pairs={{0,1},{1,0},{2,3},{3,2},{4,5},{5,4},{6,7},{7,6},{8,9},{9,8},{10,11... | collective-permute-start | bytes 1572872 | tf_op jit(solution)/shard_map/ppermute | solution.py:29
  235.4 14.3 %collective-permute-start.29 = (bf16[256,1024]{1,0:T(8,128)(2,1)S(1)}, bf16[256,1024]{1,0:T(8,128)(2,1)S(1)}, u32[]{:S(2)}, u32[]{:S(2)}) collective-permute-start(bf16[256,1024]{1,0:T(8,128)(2,1)S(1)} %get-tuple-element.122), channel_id=1, source_target_pairs={{0,2},{2,0},{1,3},{3,1},{4,6},{6,4},{5,7},{7,5},{8,10},{10,8},{9,1... | collective-permute-start | bytes 1572872 | tf_op jit(solution)/shard_map/ppermute | solution.py:29
  236.9 13.9 %collective-permute-start.32 = (bf16[256,1024]{1,0:T(8,128)(2,1)S(1)}, bf16[256,1024]{1,0:T(8,128)(2,1)S(1)}, u32[]{:S(2)}, u32[]{:S(2)}) collective-permute-start(bf16[256,1024]{1,0:T(8,128)(2,1)S(1)} %get-tuple-element.123), channel_id=1, source_target_pairs={{0,4},{4,0},{1,5},{5,1},{2,6},{6,2},{3,7},{7,3},{8,12},{12,8},{9,1... | collective-permute-start | bytes 1572872 | tf_op jit(solution)/shard_map/ppermute | solution.py:29
  272.2 63.3 %collective-permute-start.55 = (bf16[512,1024]{1,0:T(8,128)(2,1)}, bf16[512,1024]{1,0:T(8,128)(2,1)}, u32[]{:S(2)}, u32[]{:S(2)}) collective-permute-start(bf16[512,1024]{1,0:T(8,128)(2,1)} %convolution_convert_fusion.1), channel_id=1, source_target_pairs={{0,1},{1,0},{2,3},{3,2},{4,5},{5,4},{6,7},{7,6},{8,9},{9,8},{10,11... | collective-permute-start | bytes 3145736 | tf_op jit(solution)/shard_map/ppermute | solution.py:29
  274.5 30.1 %all-to-all-start.3 = ((bf16[8,128,256]{2,1,0:T(8,128)(2,1)}), bf16[8,128,256]{2,1,0:T(8,128)(2,1)}, u32[]{:S(2)}, u32[]{:S(2)}) async-start(bf16[8,128,256]{2,1,0:T(8,128)(2,1)} %bitcast.206), calls=%async_computation.3 | async-start | bytes 1048576 | tf_op jit(solution)/shard_map/all_to_all | solution.py:453
  278.6 123.4 %reduce-scatter.5.cloned.1.call-start = ((), (), s32[]{:S(2)}) async-start(), calls=%async_computation.12 | async-start | bytes 1474560 | tf_op jit(solution)/shard_map/reduce_scatter | solution.py:597
  283.9 18.2 %collective-permute-start.37 = (bf16[256,1024]{1,0:T(8,128)(2,1)}, bf16[256,1024]{1,0:T(8,128)(2,1)}, u32[]{:S(2)}, u32[]{:S(2)}) collective-permute-start(bf16[256,1024]{1,0:T(8,128)(2,1)} %slice.333), channel_id=1, source_target_pairs={{0,1},{1,0},{2,3},{3,2},{4,5},{5,4},{6,7},{7,6},{8,9},{9,8},{10,11... | collective-permute-start | bytes 1572872 | tf_op jit(solution)/shard_map/ppermute | solution.py:29
  286.8 53.5 %collective-permute-start.35 = (bf16[512,1024]{1,0:T(8,128)(2,1)}, bf16[512,1024]{1,0:T(8,128)(2,1)}, u32[]{:S(2)}, u32[]{:S(2)}) collective-permute-start(bf16[512,1024]{1,0:T(8,128)(2,1)} %slice.332), channel_id=1, source_target_pairs={{0,1},{1,0},{2,3},{3,2},{4,5},{5,4},{6,7},{7,6},{8,9},{9,8},{10,11... | collective-permute-start | bytes 3145736 | tf_op jit(solution)/shard_map/ppermute | solution.py:29
  329.4 57.0 %all-to-all-start.4 = ((bf16[8,256,256]{2,1,0:T(8,128)(2,1)}), bf16[8,256,256]{2,1,0:T(8,128)(2,1)}, u32[]{:S(2)}, u32[]{:S(2)}) async-start(bf16[8,256,256]{2,1,0:T(8,128)(2,1)} %pad_maximum_fusion.3), calls=%async_computation.4 | async-start | bytes 2097152 | tf_op jit(solution)/shard_map/all_to_all | solution.py:453
  335.2 101.3 %reduce-scatter.3.cloned.1.call-start = ((), (), s32[]{:S(2)}) async-start(), calls=%async_computation.11 | async-start | bytes 2949120 | tf_op jit(solution)/shard_map/reduce_scatter | solution.py:596
  338.3 17.4 %collective-permute-start.56 = (bf16[4,2,32,512]{3,2,0,1:T(8,128)(2,1)S(1)}, bf16[4,2,32,512]{3,2,0,1:T(8,128)(2,1)S(1)}, u32[]{:S(2)}, u32[]{:S(2)}) collective-permute-start(bf16[4,2,32,512]{3,2,0,1:T(8,128)(2,1)S(1)} %fusion.30), channel_id=1, source_target_pairs={{0,4},{4,0},{1,5},{5,1},{2,6},{6,2},{3,7},{7,3},{8,12},{12,8},{9,1... | collective-permute-start | bytes 786440 | tf_op jit(solution)/shard_map/ppermute | solution.py:29
  342.1 33.2 %collective-permute-start.36 = (bf16[256,1024]{1,0:T(8,128)(2,1)S(1)}, bf16[256,1024]{1,0:T(8,128)(2,1)S(1)}, u32[]{:S(2)}, u32[]{:S(2)}) collective-permute-start(bf16[256,1024]{1,0:T(8,128)(2,1)S(1)} %get-tuple-element.118), channel_id=1, source_target_pairs={{0,2},{2,0},{1,3},{3,1},{4,6},{6,4},{5,7},{7,5},{8,10},{10,8},{9,1... | collective-permute-start | bytes 1572872 | tf_op jit(solution)/shard_map/ppermute | solution.py:29
  343.6 31.8 %collective-permute-start.39 = (bf16[256,1024]{1,0:T(8,128)(2,1)S(1)}, bf16[256,1024]{1,0:T(8,128)(2,1)S(1)}, u32[]{:S(2)}, u32[]{:S(2)}) collective-permute-start(bf16[256,1024]{1,0:T(8,128)(2,1)S(1)} %get-tuple-element.119), channel_id=1, source_target_pairs={{0,4},{4,0},{1,5},{5,1},{2,6},{6,2},{3,7},{7,3},{8,12},{12,8},{9,1... | collective-permute-start | bytes 1572872 | tf_op jit(solution)/shard_map/ppermute | solution.py:29
  347.0 22.2 %collective-permute-start.59 = (bf16[4,32,512]{2,1,0:T(8,128)(2,1)S(1)}, bf16[4,32,512]{2,1,0:T(8,128)(2,1)S(1)}, u32[]{:S(2)}, u32[]{:S(2)}) collective-permute-start(bf16[4,32,512]{2,1,0:T(8,128)(2,1)S(1)} %fusion.40), channel_id=1, source_target_pairs={{0,4},{4,0},{1,5},{5,1},{2,6},{6,2},{3,7},{7,3},{8,12},{12,8},{9,1... | collective-permute-start | bytes 393224 | tf_op jit(solution)/shard_map/ppermute | solution.py:29
  355.8 13.4 %collective-permute-start.57 = (bf16[4,32,512]{2,1,0:T(8,128)(2,1)S(1)}, bf16[4,32,512]{2,1,0:T(8,128)(2,1)S(1)}, u32[]{:S(2)}, u32[]{:S(2)}) collective-permute-start(bf16[4,32,512]{2,1,0:T(8,128)(2,1)S(1)} %fusion.39), channel_id=1, source_target_pairs={{0,2},{2,0},{1,3},{3,1},{4,6},{6,4},{5,7},{7,5},{8,10},{10,8},{9,1... | collective-permute-start | bytes 393224 | tf_op jit(solution)/shard_map/ppermute | solution.py:29
  370.0 10.4 %collective-permute-start.60 = (bf16[32,1024]{1,0:T(8,128)(2,1)}, bf16[32,1024]{1,0:T(8,128)(2,1)}, u32[]{:S(2)}, u32[]{:S(2)}) collective-permute-start(bf16[32,1024]{1,0:T(8,128)(2,1)} %get-tuple-element.141), channel_id=1, source_target_pairs={{0,8},{8,16},{16,24},{24,0},{1,9},{9,17},{17,25},{25,1},{2,10},{10... | collective-permute-start | bytes 196616 | tf_op jit(solution)/shard_map/ppermute | solution.py:44
  380.4 27.7 %collective-permute-start.34 = (bf16[256,1024]{1,0:T(8,128)(2,1)}, bf16[256,1024]{1,0:T(8,128)(2,1)}, u32[]{:S(2)}, u32[]{:S(2)}) collective-permute-start(bf16[256,1024]{1,0:T(8,128)(2,1)} %slice.334), channel_id=1, source_target_pairs={{0,1},{1,0},{2,3},{3,2},{4,5},{5,4},{6,7},{7,6},{8,9},{9,8},{10,11... | collective-permute-start | bytes 1572872 | tf_op jit(solution)/shard_map/ppermute | solution.py:29
  382.0 18.2 %collective-permute-start.40 = (bf16[128,1024]{1,0:T(8,128)(2,1)}, bf16[128,1024]{1,0:T(8,128)(2,1)}, u32[]{:S(2)}, u32[]{:S(2)}) collective-permute-start(bf16[128,1024]{1,0:T(8,128)(2,1)} %get-tuple-element.117), channel_id=1, source_target_pairs={{0,2},{2,0},{1,3},{3,1},{4,6},{6,4},{5,7},{7,5},{8,10},{10,8},{9,1... | collective-permute-start | bytes 786440 | tf_op jit(solution)/shard_map/ppermute | solution.py:29
  394.3 21.9 %collective-permute-start.47 = (bf16[512,2048]{1,0:T(8,128)(2,1)}, bf16[512,2048]{1,0:T(8,128)(2,1)}, u32[]{:S(2)}, u32[]{:S(2)}) collective-permute-start(bf16[512,2048]{1,0:T(8,128)(2,1)} %convolution_convert_fusion), channel_id=1, source_target_pairs={{0,1},{1,0},{2,3},{3,2},{4,5},{5,4},{6,7},{7,6},{8,9},{9,8},{10,11... | collective-permute-start | bytes 6291464 | tf_op jit(solution)/shard_map/ppermute | solution.py:29
  419.1 12.4 %collective-permute-start.50 = (bf16[4,2,32,1024]{3,2,1,0:T(8,128)(2,1)S(1)}, bf16[4,2,32,1024]{3,2,1,0:T(8,128)(2,1)S(1)}, u32[]{:S(2)}, u32[]{:S(2)}) collective-permute-start(bf16[4,2,32,1024]{3,2,1,0:T(8,128)(2,1)S(1)} %fusion.17), channel_id=1, source_target_pairs={{0,2},{2,0},{1,3},{3,1},{4,6},{6,4},{5,7},{7,5},{8,10},{10,8},{9,1... | collective-permute-start | bytes 1572872 | tf_op jit(solution)/shard_map/ppermute | solution.py:29
  419.7 14.4 %collective-permute-start.48 = (bf16[4,2,32,1024]{3,2,0,1:T(8,128)(2,1)S(1)}, bf16[4,2,32,1024]{3,2,0,1:T(8,128)(2,1)S(1)}, u32[]{:S(2)}, u32[]{:S(2)}) collective-permute-start(bf16[4,2,32,1024]{3,2,0,1:T(8,128)(2,1)S(1)} %fusion.18), channel_id=1, source_target_pairs={{0,4},{4,0},{1,5},{5,1},{2,6},{6,2},{3,7},{7,3},{8,12},{12,8},{9,1... | collective-permute-start | bytes 1572872 | tf_op jit(solution)/shard_map/ppermute | solution.py:29
  436.6 13.0 %all-to-all-start.5 = ((bf16[8,32,1152]{2,1,0:T(8,128)(2,1)}), bf16[8,32,1152]{2,1,0:T(8,128)(2,1)S(1)}, u32[]{:S(2)}, u32[]{:S(2)}) async-start(bf16[8,32,1152]{2,1,0:T(8,128)(2,1)} %bitcast.205), calls=%async_computation.6 | async-start | bytes 1179648 | tf_op jit(solution)/shard_map/all_to_all | solution.py:449
  443.5 11.4 %collective-permute-start.53 = (bf16[32,2048]{1,0:T(8,128)(2,1)S(1)}, bf16[32,2048]{1,0:T(8,128)(2,1)S(1)}, u32[]{:S(2)}, u32[]{:S(2)}) collective-permute-start(bf16[32,2048]{1,0:T(8,128)(2,1)S(1)} %get-tuple-element.134), channel_id=1, source_target_pairs={{0,16},{8,24},{16,0},{24,8},{1,17},{9,25},{17,1},{25,9},{2,18},{10... | collective-permute-start | bytes 393224 | tf_op jit(solution)/shard_map/ppermute | solution.py:44
  444.8 10.2 %collective-permute-start.54 = (bf16[32,2048]{1,0:T(8,128)(2,1)S(1)}, bf16[32,2048]{1,0:T(8,128)(2,1)S(1)}, u32[]{:S(2)}, u32[]{:S(2)}) collective-permute-start(bf16[32,2048]{1,0:T(8,128)(2,1)S(1)} %get-tuple-element.133), channel_id=1, source_target_pairs={{0,24},{8,0},{16,8},{24,16},{1,25},{9,1},{17,9},{25,17},{2,26},{10... | collective-permute-start | bytes 393224 | tf_op jit(solution)/shard_map/ppermute | solution.py:44
  (116 other events, 637.3 us)
Sparse Core Ops, SparseCore 0:
  32.4 58.5 all-gather.3
  93.1 68.3 all-gather.5
  163.1 29.0 all-gather.7
  292.6 29.6 reduce-scatter.4
  380.5 45.8 reduce-scatter.2

commit v3 on v2

--- a/solution.py
+++ b/solution.py
@@ -82,7 +82,7 @@
     return factor * scaled - values * (factor * factor * factor * mean)
 
 
-def attend_kernel(rate, base_ref, start_ref, q_ref, kv_ref, out_ref, exact_ref, mass_ref, key_ref):
+def attend_kernel(rate, base_ref, start_ref, q_ref, kv_ref, out_ref, mass_ref, key_ref):
     blocks, width, rows = q_ref.shape
     dim = width // 2
     base = base_ref[0]
@@ -113,9 +113,7 @@
         state = lax.fori_loop(0, base + i, functools.partial(tile, last=False), state)
         mass, total = tile(base + i, state, True)
         total = total / mass
-        exact = jnp.concatenate([total[:, :rows], total[:, rows:]], axis=0)
-        exact_ref[i] = exact
-        out_ref[i] = exact.astype(BF)
+        out_ref[i] = jnp.concatenate([total[:, :rows], total[:, rows:]], axis=0).astype(BF)
         mass_ref[i] = mass
         return 0
 
@@ -123,7 +121,7 @@
 
 
 def attend_back_kernel(
-    rate, scale, base_ref, start_ref, q_ref, kv_ref, exact_ref, mass_ref, grad_ref,
+    rate, scale, base_ref, start_ref, q_ref, kv_ref, attn_ref, mass_ref, grad_ref,
     dq_ref, dkv_ref, key_ref, value_ref, qrow_ref, grow_ref, dk_ref, dv_ref,
 ):
     blocks, width, rows = q_ref.shape
@@ -153,9 +151,9 @@
     def row(i, _):
         queries = jnp.concatenate([q_ref[i, :dim, :], q_ref[i, dim:, :]], axis=1)
         grads = jnp.concatenate([grad_ref[i, :dim, :], grad_ref[i, dim:, :]], axis=1)
-        exact = jnp.concatenate([exact_ref[i, :dim, :], exact_ref[i, dim:, :]], axis=1)
+        attn = jnp.concatenate([attn_ref[i, :dim, :], attn_ref[i, dim:, :]], axis=1).astype(F32)
         begin = jnp.concatenate([start_ref[i], start_ref[i]], axis=1)
-        delta = jnp.sum(grads.astype(F32) * exact, axis=0, keepdims=True)
+        delta = jnp.sum(grads.astype(F32) * attn, axis=0, keepdims=True)
         level = jnp.log(mass_ref[i]) * LOG2E
 
         def tile(j, dq, last):
@@ -281,21 +279,33 @@
     k_ref[...] = jnp.sum(sums[1], axis=1, keepdims=True)
 
 
+def down_rows(every_ref, down_ref):
+    line, total, _ = every_ref.shape
+    strip = down_ref.shape[0] // line
+    for z in range(line):
+        down_ref[z * strip : (z + 1) * strip, :] = every_ref[z, total - strip :, : down_ref.shape[1]]
+
+
 def ffn_kernel(count, *refs):
     tokens, grads = refs[:count], refs[count : 2 * count]
-    wide_ref, down_ref, hn_ref, grad_ref, act_ref, d_both_ref, d_hn_ref = refs[2 * count :]
+    every_ref, hn_ref, grad_ref, act_ref, d_both_ref, own_ref, other_ref, down_ref = refs[2 * count :]
     at = 0
     for token_ref, one_ref in zip(tokens, grads):
         size = token_ref.shape[0]
         hn_ref[at : at + size, :] = token_ref[...]
         grad_ref[at : at + size, :] = one_ref[...]
         at += size
+    down_rows(every_ref, down_ref)
+    line = every_ref.shape[0]
+    depth = hn_ref.shape[1] // line
     local = down_ref.shape[0]
-    step = 256 if at % 256 == 0 else at
-
-    def block(i, _):
-        cut = pl.ds(pl.multiple_of(i * step, step), step)
-        both = dot(hn_ref[cut, :], wide_ref[...], (1, 0))
+    half = own_ref.shape[0]
+    step = 256 if half % 256 == 0 else half
+    for first in reversed(range(0, at, step)):
+        cut = slice(first, first + step)
+        both = sum(
+            dot(hn_ref[cut, z * depth : (z + 1) * depth], every_ref[z, :depth, :], (1, 0)) for z in range(line)
+        )
         d_act = dot(grad_ref[cut, :], down_ref[...], (1, 1))
         gate, up = both[:, :local], both[:, local:]
         sig = jax.nn.sigmoid(gate)
@@ -304,14 +314,41 @@
         d_gate = d_act * up * (sig * (1.0 + gate * (1.0 - sig)))
         d_both = jnp.concatenate([d_gate, d_act * silu], axis=1).astype(BF)
         d_both_ref[cut, :] = d_both
-        d_hn_ref[cut, :] = dot(d_both, wide_ref[...], (1, 1)).astype(BF)
-        return 0
-
-    lax.fori_loop(0, at // step, block, 0)
+        ref, place = (own_ref, first) if first < half else (other_ref, first - half)
+        d_hn = [dot(d_both, every_ref[z, :depth, :], (1, 1)).astype(BF) for z in range(line)]
+        ref[place : place + step, :] = jnp.concatenate(d_hn, axis=1)
+
+
+def ffn_out_kernel(count, *refs):
+    acts, every_ref, outs, down_ref = refs[:count], refs[count], refs[count + 1 : -1], refs[-1]
+    down_rows(every_ref, down_ref)
+    for i, act_ref in enumerate(acts):
+        half = act_ref.shape[0] // 2
+        for side in range(2):
+            outs[2 * i + side][...] = dot(
+                act_ref[side * half : (side + 1) * half, :], down_ref[...], (1, 0)
+            ).astype(BF)
+
+
+def ffn_weights_kernel(count, *refs):
+    hns, d_boths, acts, grads = [refs[i * count : (i + 1) * count] for i in range(4)]
+    out_ref = refs[4 * count]
+    line, _, columns = out_ref.shape
+    width, local = hns[0].shape[1], acts[0].shape[1]
+    depth, strip = width // line, local // line
+    for z in range(line):
+        for lefts, rights, size, first in ((hns, d_boths, depth, 0), (acts, grads, strip, depth)):
+            total = sum(
+                dot(left[:, z * size : (z + 1) * size], right[...], (0, 0)) for left, right in zip(lefts, rights)
+            )
+            if total.shape[1] < columns:
+                total = jnp.concatenate([total, jnp.zeros((size, columns - total.shape[1]), F32)], axis=1)
+            out_ref[z, first : first + size, :] = total.astype(BF)
 
 
 VMEM = pl.BlockSpec(memory_space=pltpu.VMEM)
 SMEM = pl.BlockSpec(memory_space=pltpu.SMEM)
+LITTLE = pl.CostEstimate(flops=1, bytes_accessed=1, transcendentals=0)
 PARAMS = pltpu.CompilerParams(vmem_limit_bytes=48 * 1024 * 1024)
 
 
@@ -323,21 +360,18 @@
         functools.partial(attend_kernel, dim ** -0.5 * LOG2E),
         out_shape=(
             jax.ShapeDtypeStruct(queries.shape, BF),
-            jax.ShapeDtypeStruct(queries.shape, F32),
             jax.ShapeDtypeStruct((blocks, 1, 2 * rows), F32),
         ),
         in_specs=[SMEM, VMEM, VMEM, VMEM],
-        out_specs=(VMEM, VMEM, VMEM),
+        out_specs=(VMEM, VMEM),
         scratch_shapes=[pltpu.VMEM((tiles, rows, dim), BF)],
         compiler_params=PARAMS,
-        cost_estimate=pl.CostEstimate(
-            flops=pairs * 8 * rows * rows * dim, bytes_accessed=4 * 1024 * 1024, transcendentals=pairs * 2 * rows * rows
-        ),
+        cost_estimate=LITTLE,
         name="attend",
     )(base, start, queries, kv)
 
 
-def attend_back(base, start, queries, kv, exact, mass, grads, dim):
+def attend_back(base, start, queries, kv, attn, mass, grads, dim):
     blocks, width, rows = queries.shape
     tiles = kv.shape[0]
     pairs = blocks * (blocks + 1) // 2
@@ -355,11 +389,9 @@
             pltpu.VMEM((tiles, rows, dim), F32),
         ],
         compiler_params=PARAMS,
-        cost_estimate=pl.CostEstimate(
-            flops=pairs * 20 * rows * rows * dim, bytes_accessed=4 * 1024 * 1024, transcendentals=pairs * 2 * rows * rows
-        ),
+        cost_estimate=pl.CostEstimate(flops=int(6e9), bytes_accessed=8 << 20, transcendentals=0),
         name="attend_back",
-    )(base, start, queries, kv, exact, mass, grads)
+    )(base, start, queries, kv, attn, mass, grads)
 
 
 def spread(gate, up, members, strip):
@@ -403,9 +435,7 @@
         in_specs=[VMEM] * 7,
         out_specs=(VMEM,) * 4,
         compiler_params=PARAMS,
-        cost_estimate=pl.CostEstimate(
-            flops=2 * rows * width * (q_cols + 2 * k_cols), bytes_accessed=8 * 1024 * 1024, transcendentals=0
-        ),
+        cost_estimate=LITTLE,
         name="prepare",
     )(tokens, w_query, w_rest, q_gain, k_gain, cosine, sine)
 
@@ -422,27 +452,54 @@
         in_specs=[VMEM] * 6,
         out_specs=(VMEM,) * 3,
         compiler_params=PARAMS,
-        cost_estimate=pl.CostEstimate(flops=20 * pre.size, bytes_accessed=6 * pre.size, transcendentals=0),
+        cost_estimate=LITTLE,
         name="prepare_back",
     )(back, pre, q_gain, k_gain, cosine, sine)
 
 
-def ffn(tokens, grads, wide, down):
+def ffn(tokens, grads, every, strip):
     total = sum(part.shape[0] for part in tokens)
-    width = wide.shape[0]
-    local = down.shape[0]
-    shapes = [(total, width), (total, width), (total, local), (total, 2 * local), (total, width)]
+    line, _, columns = every.shape
+    width, local = tokens[0].shape[1], line * strip
+    shapes = [(total, width), (total, width), (total, local), (total, 2 * local), (total // 2, width), (total // 2, width)]
     return pl.pallas_call(
         functools.partial(ffn_kernel, len(tokens)),
         out_shape=tuple(jax.ShapeDtypeStruct(shape, BF) for shape in shapes),
-        in_specs=[VMEM] * (2 * len(tokens) + 2),
+        in_specs=[VMEM] * (2 * len(tokens) + 1),
         out_specs=(VMEM,) * len(shapes),
-        compiler_params=PARAMS,
-        cost_estimate=pl.CostEstimate(
-            flops=10 * total * width * local, bytes_accessed=8 * total * width, transcendentals=total * local
-        ),
+        scratch_shapes=[pltpu.VMEM((local, width), BF)],
+        compiler_params=PARAMS,
+        cost_estimate=LITTLE,
         name="ffn",
-    )(*tokens, *grads, wide, down)
+    )(*tokens, *grads, every)
+
+
+def ffn_out(acts, every, width):
+    local = acts[0].shape[1]
+    shapes = [(act.shape[0] // 2, width) for act in acts for _ in range(2)]
+    outs = pl.pallas_call(
+        functools.partial(ffn_out_kernel, len(acts)),
+        out_shape=tuple(jax.ShapeDtypeStruct(shape, BF) for shape in shapes),
+        in_specs=[VMEM] * (len(acts) + 1),
+        out_specs=(VMEM,) * len(shapes),
+        scratch_shapes=[pltpu.VMEM((local, width), BF)],
+        compiler_params=PARAMS,
+        cost_estimate=pl.CostEstimate(flops=int(2.4e9), bytes_accessed=8 << 20, transcendentals=0),
+        name="ffn_out",
+    )(*acts, every)
+    return list(zip(outs[::2], outs[1::2]))
+
+
+def ffn_weights(hns, d_boths, acts, grads, every):
+    return pl.pallas_call(
+        functools.partial(ffn_weights_kernel, len(hns)),
+        out_shape=jax.ShapeDtypeStruct(every.shape, BF),
+        in_specs=[VMEM] * (4 * len(hns)),
+        out_specs=VMEM,
+        compiler_params=PARAMS,
+        cost_estimate=pl.CostEstimate(flops=int(7.2e9), bytes_accessed=8 << 20, transcendentals=0),
+        name="ffn_weights",
+    )(*hns, *d_boths, *acts, *grads)
 
 
 def trade(blocks):
@@ -508,7 +565,6 @@
     base = base.astype(jnp.int32).reshape(1)
 
     gains = jnp.pad(jnp.stack([attn_gain, ffn_gain], axis=1), ((0, 0), (0, pad - 2)))
-    index = lax.axis_index(SEQ) * pairs + lax.axis_index(("y", "c"))
 
     def gather_all(array, first, second, *others):
         places = {"x": 1, "y": 2}
@@ -518,12 +574,13 @@
 
     spreaded = spread(gate_weight, up_weight, members, strip)
     mixed = trade(spreaded).reshape(depth, 2 * local)
+    packed = jnp.concatenate([mixed, jnp.pad(down_weight, ((0, 0), (0, mixed.shape[1] - width)))], axis=0)
+    w_out = lax.all_gather(o_weight, SEQ + ("y", "c"), axis=0, tiled=True)
+    every = lax.all_gather(packed, ZAXES, axis=0)
     first_line = gather_line(after(jnp.concatenate([q_weight, k_weight, v_weight, gains], axis=1), spreaded))
-    w_query = gather_all(first_line[..., :q_cols], "x", "y", mixed).reshape(width, q_cols)
-    w_rest = gather_all(first_line[..., q_cols:], "y", "x", mixed).reshape(width, -1)
+    w_query = gather_all(first_line[..., :q_cols], "x", "y", packed).reshape(width, q_cols)
+    w_rest = gather_all(first_line[..., q_cols:], "y", "x", packed).reshape(width, -1)
     w_key, w_value = w_rest[:, :k_cols], w_rest[:, k_cols : 2 * k_cols]
-    w_wide = lax.all_gather(mixed, ZAXES, axis=0, tiled=True)
-
     quarter = rows // 2
 
     def plane_parts(array):
@@ -534,15 +591,17 @@
         parts = ((array,), (first_x, second_y), (far_first, far_second))
         return [list(part) + [swap(piece, "c") for piece in part] for part in parts]
 
-    def plane_sum(parts):
-        def chip(part):
-            half = part.shape[0] // 2
-            return part[:half].astype(F32) + swap(part[half:].astype(BF), "c").astype(F32)
-
-        def moved(part, axis):
-            return swap(part.astype(BF), axis).astype(F32)
-
-        near, middle, far = [chip(part) for part in parts]
+    def plane_chip(part):
+        own, other = part
+        return own.astype(F32) + swap(other.astype(BF), "c").astype(F32)
+
+    def moved(part, axis):
+        return swap(part.astype(BF), axis).astype(F32)
+
+    def plane_sum(parts, start=None):
+        near, middle, far = [plane_chip(part) for part in parts]
+        if start is not None:
+            start(far)
         from_y, from_x = moved(far[:rows], "y"), moved(far[rows:], "x")
         first = from_y[:quarter] + moved(middle[:quarter] + from_y[quarter:], "x")
         second = from_x[:quarter] + moved(middle[quarter:] + from_x[quarter:], "y")
@@ -556,28 +615,36 @@
     unit, pre, normed, gain_rows = prepare_heads(tokens[0], w_query, w_rest, q_gain, k_gain, cosine, sine)
     attn_gain_all, ffn_gain_all = gain_rows[0], gain_rows[1]
     unit = exchange(unit)
-    w_out = lax.all_gather(after(o_weight, mixed), SEQ + ("y", "c"), axis=0, tiled=True)
-    w_down = lax.all_gather(after(down_weight, unit), ZAXES, axis=0, tiled=True)
     grad_parts = plane_parts(after(grad_out, unit))
     unit_q, unit_kv = unit[:, : 2 * dim], unit[:, 2 * dim :]
     if groups > 1:
         unit_kv = lax.all_gather(unit_kv, "t", axis=0, tiled=True)
-    unit_out, exact, mass = attend(base, start_rows, unit_q, unit_kv, dim)
+    unit_out, mass = attend(base, start_rows, unit_q, unit_kv, dim)
     attn_b = exchange(unit_out).reshape(heads * dim, rows)
     hidden = inputs + dot(attn_b, w_out, (0, 0))
 
     ffn_factor = rms_factor(hidden)
     hn = (hidden * ffn_factor * ffn_gain_all).astype(BF)
-    hn_parts = plane_parts(hn)
-
-    done = []
-    for part, grad in zip(hn_parts, grad_parts):
-        part = list(part)
-        if done:
-            part[0] = after(part[0], done[-1][4])
-        done.append(ffn(part, grad, w_wide, w_down))
-    hns, grad_alls, acts, d_boths, d_hn_parts = zip(*done)
-    d_hn = plane_sum(d_hn_parts)
+    first, second = hn[:quarter], hn[quarter:]
+    first_x, second_y = swap(first, "x"), swap(second, "y")
+    done = [ffn([hn, swap(hn, "c")], grad_parts[0], every, strip)]
+    first_x, second_y = lax.optimization_barrier((first_x, second_y, done[0][5]))[:2]
+    far_first = swap(jnp.concatenate([first, first_x], axis=0), "y")
+    far_second = swap(jnp.concatenate([second, second_y], axis=0), "x")
+    done.append(ffn([first_x, second_y, swap(first_x, "c"), swap(second_y, "c")], grad_parts[1], every, strip))
+    far_first, far_second = lax.optimization_barrier((far_first, far_second, done[1][5]))[:2]
+    done.append(ffn([far_first, far_second, swap(far_first, "c"), swap(far_second, "c")], grad_parts[2], every, strip))
+    hns, grad_alls, acts, d_boths = list(zip(*done))[:4]
+    packed_grads = []
+
+    def weights_after(far):
+        later, boths, _ = lax.optimization_barrier((acts, d_boths, far))
+        packed_grads.append(ffn_weights(hns, boths, later, grad_alls, every))
+
+    d_hn = plane_sum([part[4:] for part in done], weights_after)
+    packed_grad = packed_grads[0]
+    d_hn = after(d_hn, packed_grad)
+
 
     d_hidden = grad_out.astype(F32) + rms_back(hidden, ffn_factor, ffn_gain_all, d_hn)
     ffn_gain_part = jnp.sum(d_hn * hidden * ffn_factor, axis=0)
@@ -585,23 +652,7 @@
     d_attn = dot(w_out, d_branch, (1, 1)).astype(BF).reshape(kv_heads, 2 * dim, rows)
     unit_grad = exchange(d_attn)
 
-    acts, d_boths, _ = lax.optimization_barrier((acts, d_boths, d_branch))
-
-    def over_parts(lefts, rights):
-        return sum(dot(left, right, (0, 0)) for left, right in zip(lefts, rights)).astype(BF)
-
-    wide_grad = over_parts(hns, d_boths)
-    down_grad = over_parts(acts, grad_alls)
-    unit_grad = after(unit_grad, wide_grad, down_grad)
-    wide_grad = lax.psum_scatter(wide_grad, ZAXES, scatter_dimension=0, tiled=True)
-    down_grad = lax.psum_scatter(down_grad, ZAXES, scatter_dimension=0, tiled=True).astype(F32)
-    gate_grad, up_grad = weave(trade(wide_grad.reshape(members, piece, -1)), strip)
-    output = (hidden + plane_sum([dot(act, w_down, (1, 0)) for act in acts])).astype(BF)[None]
-
-    def scatter_rest(array, first, second):
-        places = {"x": 1, "y": 2}
-        array = scatter_two(array, first, places[first])
-        return scatter_two(array, second, 1)
+    near, middle, far = [plane_chip(part) for part in ffn_out(after(acts, d_attn), every, width)]
 
     def cut_core(array, side):
         return pick(array.reshape(line * 2 * half_pairs, 2, piece, -1), side, 1).reshape(line * 2 * half_pairs * piece, -1)
@@ -610,64 +661,70 @@
         return dot(cut_core(attn_b, side), d_branch, (1, 0))
 
     out_kept = out_product(side_c) + swap(out_product(1 - side_c).astype(BF), "c").astype(F32)
+    unit_grad = after(unit_grad, packed_grad, near, middle, far, out_kept)
+    packed_grad = lax.psum_scatter(packed_grad, ZAXES, scatter_dimension=0, tiled=True)[0]
+    wide_grad, down_grad = packed_grad[:depth], packed_grad[depth:, :width].astype(F32)
+
+    from_y, from_x = moved(far[:rows], "y"), moved(far[rows:], "x")
     out_kept = out_kept.reshape(line, 2, half_pairs, piece, width)
-    out_grad = scatter_line(
-        jnp.concatenate(
-            [
-                scatter_rest(out_kept[..., : width // 2], "x", "y"),
-                scatter_rest(out_kept[..., width // 2 :], "y", "x"),
-            ],
-            axis=-1,
-        )
-    )
-
-    unit_dq, unit_dkv = attend_back(base, start_rows, unit_q, unit_kv, exact, mass, unit_grad, dim)
+    out_sent = swap(pick(out_kept, 1 - side_y, 2).astype(BF), "y")
+    unit_dq, unit_dkv = attend_back(base, start_rows, unit_q, unit_kv, unit_out, mass, unit_grad, dim)
     if groups > 1:
         unit_dkv = lax.psum_scatter(unit_dkv.astype(F32), "t", scatter_dimension=0, tiled=True).astype(BF)
     back = exchange(jnp.concatenate([unit_dq, unit_dkv], axis=1))
+    from_y, from_x, out_sent, _ = lax.optimization_barrier((from_y, from_x, out_sent, unit_dq))
+    first = from_y[:quarter] + moved(middle[:quarter] + from_y[quarter:], "x")
+    second = from_x[:quarter] + moved(middle[quarter:] + from_x[quarter:], "y")
+    output = (hidden + near + jnp.concatenate([first, second], axis=0)).astype(BF)[None]
+    out_kept = scatter_two(pick(out_kept, side_y, 2) + out_sent.astype(F32), "x", 1)
+    back = after(back, packed_grad, output, out_kept)
     d_pre, q_gain_grad, k_gain_grad = prepare_back(back, pre, q_gain, k_gain, cosine, sine)
 
+    normed_cut = normed.reshape(rows, line * 2 * half_pairs, 2, piece)
+
+    def pre_product(side):
+        left = pick(normed_cut, side, 2).reshape(rows, -1)
+        return dot(left, d_pre, (0, 1))
+
+    kept = pre_product(side_c) + swap(pre_product(1 - side_c).astype(BF), "c").astype(F32)
+    d_late, wide_grad = lax.optimization_barrier((d_pre, wide_grad, kept))[:2]
+    gate_grad, up_grad = weave(trade(wide_grad.reshape(members, piece, -1)), strip)
+    kept = kept.reshape(line, 2, half_pairs, piece, -1)
     d_normed = (
-        dot(d_pre[:q_cols], w_query, (0, 1))
-        + dot(d_pre[q_cols : q_cols + k_cols], w_key, (0, 1))
-        + dot(d_pre[q_cols + k_cols :], w_value, (0, 1))
+        dot(d_late[:q_cols], w_query, (0, 1))
+        + dot(d_late[q_cols : q_cols + k_cols], w_key, (0, 1))
+        + dot(d_late[q_cols + k_cols :], w_value, (0, 1))
     )
     attn_gain_part = jnp.sum(d_normed * inputs * in_factor, axis=0)
     input_grad = (d_hidden + rms_back(inputs, in_factor, attn_gain_all, d_normed))[None]
-
-    small = jnp.concatenate([attn_gain_part, ffn_gain_part, q_gain_grad[:, 0], k_gain_grad[:, 0]])[None]
-    for axis in ("c", "y", "x"):
-        small = small + swap(small, axis)
-    small = sum((shift(small, ZAXES, by) for by in range(1, line)), small)[0]
-
-    def own_piece(vector):
-        return pick(vector.reshape(-1, piece), index, 0)
-
-    normed_cut = normed.reshape(rows, line * 2 * half_pairs, 2, piece)
-
-    def pre_product(side):
-        left = pick(normed_cut, side, 2).reshape(rows, -1)
-        return dot(left, d_pre, (0, 1))
-
-    kept = pre_product(side_c) + swap(pre_product(1 - side_c).astype(BF), "c").astype(F32)
-    kept = kept.reshape(line, 2, half_pairs, piece, -1)
-    shares = scatter_line(
-        jnp.concatenate(
-            [scatter_rest(kept[..., :q_cols], "x", "y"), scatter_rest(kept[..., q_cols:], "y", "x")], axis=-1
-        )
+    q_half, rest_half = scatter_two(kept[..., :q_cols], "x", 1), scatter_two(kept[..., q_cols:], "y", 2)
+    q_half, rest_half = lax.optimization_barrier((q_half, rest_half, input_grad))[:2]
+    q_half, rest_half = scatter_two(q_half, "y", 1), scatter_two(rest_half, "x", 1)
+    last = jnp.concatenate([q_half, rest_half, out_kept], axis=-1)
+    shares = scatter_line(last)
+
+    count = seq * pairs
+    heads_part = jnp.concatenate([q_gain_grad, k_gain_grad], axis=0).reshape(1, -1)
+    small = jnp.concatenate(
+        [
+            attn_gain_part.reshape(count, piece), ffn_gain_part.reshape(count, piece),
+            jnp.broadcast_to(heads_part, (count, 2 * dim)),
+        ],
+        axis=1,
     )
-    rest = shares[:, q_cols:]
+    small = after(small, last)
+    small = jnp.sum(lax.all_to_all(small, SEQ + ("y", "c"), 0, 0, tiled=True), axis=0)
     return (
         output,
         input_grad,
-        own_piece(small[:width]),
+        small[:piece],
         shares[:, :q_cols],
-        rest[:, :k_cols],
-        rest[:, k_cols:],
-        small[2 * width : 2 * width + dim],
-        small[2 * width + dim :],
-        out_grad,
-        own_piece(small[width : 2 * width]),
+        shares[:, q_cols : q_cols + k_cols],
+        shares[:, q_cols + k_cols : q_cols + 2 * k_cols],
+        small[2 * piece : 2 * piece + dim],
+        small[2 * piece + dim :],
+        shares[:, q_cols + 2 * k_cols :],
+        small[piece : 2 * piece],
         gate_grad,
         up_grad,
         down_grad,

time: 472 us -> 448 us (0.949)
  matrix products: 38 us -> 15.9 us
  Pallas kernels: 70.4 us -> 89.7 us
  starting transfers between devices: 84.6 us -> 73.9 us
  waiting for transfers between devices: 170 us -> 161 us
  local copies, waits for them, and re-layouts: 50.1 us -> 41.7 us
  other arithmetic: 34.9 us -> 41.7 us
    ppermute x51 -> x46, waiting for transfers between devices: 98.6 us -> 64.2 us  [swap(): return lax.ppermute(array, axis, [(0, 1), (1, 0)])]
    all_to_all x4, waiting for transfers between devices: 56.3 us -> 80.1 us  [exchange(): return lax.all_to_all(blocks, HEADS, 0, 0, tiled=True)]
    dot_general x18 -> x9, matrix products: 38 us -> 15.9 us  [dot(): lax.dot_general(left, right, ((contract[:1], contract[1:]), ((), ())), pr...]
    pallas_call x0 -> x2, Pallas kernels: none -> 21.1 us  [the longest x1 14.2 us: ffn_weights(): pl.pallas_call(functools.partial(ffn_weights_kernel, len(hns)), out_shape...]
    unnamed x181 -> x135, local copies, waits for them, and re-layouts: 30 us -> 20.9 us
    ppermute x12 -> x6, waiting for transfers between devices: 4.09 us -> 13.1 us  [shift(): lax.ppermute(array, axes, [(i, (i + by) % count) for i in range(count)])]
    ppermute x12 -> x6, starting transfers between devices: 20.9 us -> 12.7 us  [shift(): lax.ppermute(array, axes, [(i, (i + by) % count) for i in range(count)])]
    all_to_all x2, waiting for transfers between devices: 10.5 us -> 2.83 us  [trade(): return lax.all_to_all(blocks, GROUP, 0, 0, tiled=True)]
  transfers between devices with their start and end apart: 74 -> 62, of which waited for: 26 -> 30; matrix products, arithmetic and copies ran while one was open for 18% -> 15% of each run, Pallas kernels for 12% -> 17%
where the time goes in v3:
time: 448 us; the launch traced here: 440 us
  waiting for transfers between devices  161 us (36%)
  Pallas kernels  89.7 us (20%)
  starting transfers between devices  73.9 us (16%)
  local copies, waits for them, and re-layouts  41.7 us (9%)
  other arithmetic  41.7 us (9%)
  matrix products  15.9 us (4%)
  between operations  15.4 us (3%)
    all_to_all x4, waiting for transfers between devices, exchange(): return lax.all_to_all(blocks, HEADS, 0, 0, tiled=True)  80.1 us
    ppermute x46, waiting for transfers between devices, swap(): return lax.ppermute(array, axis, [(0, 1), (1, 0)])  64.2 us
    ppermute x46, starting transfers between devices, swap(): return lax.ppermute(array, axis, [(0, 1), (1, 0)])  31.4 us
    pallas_call x3, Pallas kernels, ffn(): pl.pallas_call(functools.partial(ffn_kernel, len(tokens)), out_shape=tupl...  26 us
    unnamed x135, local copies, waits for them, and re-layouts  20.9 us
    pallas_call x1, Pallas kernels, attend_back(): pl.pallas_call(functools.partial(attend_back_kernel, dim ** (-0.5) * LOG2...  20.4 us
    all_to_all x4, starting transfers between devices, exchange(): return lax.all_to_all(blocks, HEADS, 0, 0, tiled=True)  17.5 us
    dot_general x9, matrix products, dot(): lax.dot_general(left, right, ((contract[:1], contract[1:]), ((), ())), pr...  15.9 us
  transfers between devices with their start and end apart: 62, of which 30 were waited for; matrix products, arithmetic and copies ran while one was open for 15% of the time, Pallas kernels for 17%

profile of v3, /device:TPU:0, one launch (start us, length us, event | category | flops | bytes accessed | tf_op | source)
XLA Modules:
  0.0 439.6 jit_solution(7795736995070528122)
XLA Ops:
  12.0 3.1 collective-permute-start
  15.0 2.6 collective-permute-start.1
  19.0 3.7 all-to-all-start
  23.9 2.9 collective-permute-done.1
  30.3 8.1 %collective-permute-done.3 = bf16[4,32,1024]{2,1,0:T(8,128)(2,1)S(1)} collective-permute-done((bf16[4,32,1024]{2,1,0:T(8,128)(2,1)S(1)}, bf16[4,32,1024]{2,1,0:T(8,128)(2,1)S(1)}, u32[]{:S(2)}, u32[]{:S(2)}) %collective-permute-start.3) | collective-permute-done | bytes 262176 | tf_op jit(solution)/shard_map/ppermute | solution.py:29
  42.6 13.3 %collective-permute-done.4 = bf16[4,2,32,1024]{3,2,0,1:T(8,128)(2,1)S(1)} collective-permute-done((bf16[4,2,32,1024]{3,2,0,1:T(8,128)(2,1)S(1)}, bf16[4,2,32,1024]{3,2,0,1:T(8,128)(2,1)S(1)}, u32[]{:S(2)}, u32[]{:S(2)}) %collective-permute-start.4) | collective-permute-done | bytes 524320 | tf_op jit(solution)/shard_map/ppermute | solution.py:29
  62.2 3.3 prepare.1
  67.6 4.2 all-to-all-start.1
  72.0 31.3 %all-to-all-done.1 = bf16[8,256,256]{2,1,0:T(8,128)(2,1)} async-done(((bf16[8,256,256]{2,1,0:T(8,128)(2,1)}), bf16[8,256,256]{2,1,0:T(8,128)(2,1)}, u32[]{:S(2)}, u32[]{:S(2)}) %all-to-all-start.1) | async-done | bytes 1048608 | tf_op jit(solution)/shard_map/all_to_all | solution.py:510
  104.6 14.3 %attend.1 = (bf16[8,128,256]{2,1,0:T(8,128)(2,1)S(1)}, f32[8,1,512]{2,1,0:T(1,128)S(1)}) custom-call(s32[1]{0:T(128)} %constant.143.clone.1.base_ref, s32[8,1,256]{2,1,0:T(1,128)S(1)} %bitcast.133, bf16[8,128,256]{2,1,0:T(8,128)(2,1)S(1)} %get-tuple-element.160.q_ref, bf16[8,128,256]{2,1,0:T(8,128)(2,1)S(1)} %get-tuple-element.159.kv_ref), custom_call_target="tpu_custom_call" | custom-call | flops 1 | bytes 1 | tf_op jit(solution)/shard_map/attend/pallas_call | solution.py:359
  121.1 4.2 all-to-all-start.2
  126.4 27.3 %all-to-all-done.2 = bf16[8,128,256]{2,1,0:T(8,128)(2,1)} async-done(((bf16[8,128,256]{2,1,0:T(8,128)(2,1)}), bf16[8,128,256]{2,1,0:T(8,128)(2,1)}, u32[]{:S(2)}, u32[]{:S(2)}) %all-to-all-start.2) | async-done | bytes 524320 | tf_op jit(solution)/shard_map/all_to_all | solution.py:510
  153.7 2.6 multiply_reduce_fusion.2
  160.8 5.2 %collective-permute-done.16.refs_5_ = bf16[128,1024]{1,0:T(8,128)(2,1)S(1)} collective-permute-done((bf16[128,1024]{1,0:T(8,128)(2,1)S(1)}, bf16[128,1024]{1,0:T(8,128)(2,1)S(1)}, u32[]{:S(2)}, u32[]{:S(2)}) %collective-permute-start.16) | collective-permute-done | bytes 262176 | tf_op jit(solution)/shard_map/ppermute | solution.py:29
  174.8 6.7 %ffn.3 = (bf16[512,1024]{1,0:T(8,128)(2,1)S(1)}, bf16[512,1024]{1,0:T(8,128)(2,1)S(1)}, bf16[512,576]{1,0:T(8,128)(2,1)S(1)}, bf16[512,1152]{1,0:T(8,128)(2,1)},...) custom-call(bf16[256,1024]{1,0:T(8,128)(2,1)S(1)} %copy-done.5, bf16[256,1024]{1,0:T(8,128)(2,1)S(1)} %copy-done.24, ...), custom_call_target="tpu_custom_call" | custom-call | flops 1 | bytes 1 | tf_op jit(solution)/shard_map/ffn/pallas_call | solution.py:465
  188.0 6.9 %ffn.4 = (bf16[512,1024]{1,0:T(8,128)(2,1)S(1)}, bf16[512,1024]{1,0:T(8,128)(2,1)S(1)}, bf16[512,576]{1,0:T(8,128)(2,1)S(1)}, bf16[512,1152]{1,0:T(8,128)(2,1)},...) custom-call(bf16[128,1024]{1,0:T(8,128)(2,1)} %collective-permute-done.11.refs_0_, ...), custom_call_target="tpu_custom_call" | custom-call | flops 1 | bytes 1 | tf_op jit(solution)/shard_map/ffn/pallas_call | solution.py:465
  201.5 12.4 %ffn.5 = (bf16[1024,1024]{1,0:T(8,128)(2,1)}, bf16[1024,1024]{1,0:T(8,128)(2,1)}, bf16[1024,576]{1,0:T(8,128)(2,1)}, bf16[1024,1152]{1,0:T(8,128)(2,1)}, bf16[51...) custom-call(bf16[256,1024]{1,0:T(8,128)(2,1)S(1)} %collective-permute-done.19.refs_0_, ...), custom_call_target="tpu_custom_call" | custom-call | flops 1 | bytes 1 | tf_op jit(solution)/shard_map/ffn/pallas_call | solution.py:465
  214.5 2.7 collective-permute-done.28
  220.5 14.2 %ffn_weights.1 = bf16[4,400,1152]{2,1,0:T(8,128)(2,1)} custom-call(bf16[512,1024]{1,0:T(8,128)(2,1)S(1)} %get-tuple-element.98.refs_0_, bf16[512,1024]{1,0:T(8,128)(2,1)S(1)} %get-tuple-element.99.refs_1_, bf16[1024,1024]{1,0:T(8,128)(2,1)} %get-tuple-element.100.refs_2_, bf16[512,1152]{1,0:T(8,128)(2,1)} %get-tuple-element.104.refs_3_, ...), custom_call_target="tpu_custom_call" | custom-call | flops 7200000000 | bytes 8388608 | tf_op jit(solution)/shard_map/ffn_weights/pallas_call | solution.py:494
  243.9 4.9 %collective-permute-done.31 = bf16[128,1024]{1,0:T(8,128)(2,1)} collective-permute-done((bf16[128,1024]{1,0:T(8,128)(2,1)}, bf16[128,1024]{1,0:T(8,128)(2,1)}, u32[]{:S(2)}, u32[]{:S(2)}) %collective-permute-start.31) | collective-permute-done | bytes 262176 | tf_op jit(solution)/shard_map/ppermute | solution.py:29
  258.2 6.9 %ffn_out.1 = (bf16[256,1024]{1,0:T(8,128)(2,1)S(1)}, bf16[256,1024]{1,0:T(8,128)(2,1)S(1)}, bf16[256,1024]{1,0:T(8,128)(2,1)S(1)}, bf16[256,1024]{1,0:T(8,128)(2...) custom-call(bf16[512,576]{1,0:T(8,128)(2,1)S(1)} %copy-done.28, bf16[512,576]{1,0:T(8,128)(2,1)S(1)} %copy-done.30, ...), custom_call_target="tpu_custom_call" | custom-call | flops 2400000000 | bytes 8388608 | tf_op jit(solution)/shard_map/ffn_out/pallas_call | solution.py:480
  268.3 4.6 %all-to-all-start.3 = ((bf16[8,128,256]{2,1,0:T(8,128)(2,1)}), bf16[8,128,256]{2,1,0:T(8,128)(2,1)}, u32[]{:S(2)}, u32[]{:S(2)}) async-start(bf16[8,128,256]{2,1,0:T(8,128)(2,1)} %bitcast.155), calls=%async_computation.3 | async-start | bytes 1048576 | tf_op jit(solution)/shard_map/all_to_all | solution.py:510
  272.9 2.0 copy.73
  274.9 2.4 convert_add_fusion.5
  277.3 3.0 convert_add_fusion.1
  280.3 21.5 %all-to-all-done.3.grad_ref = bf16[8,128,256]{2,1,0:T(8,128)(2,1)} async-done(((bf16[8,128,256]{2,1,0:T(8,128)(2,1)}), bf16[8,128,256]{2,1,0:T(8,128)(2,1)}, u32[]{:S(2)}, u32[]{:S(2)}) %all-to-all-start.3) | async-done | bytes 524320 | tf_op jit(solution)/shard_map/all_to_all | solution.py:510
  301.9 2.1 fusion.16
  305.7 2.1 fusion.44
  310.6 20.4 %attend_back.1 = (bf16[8,128,256]{2,1,0:T(8,128)(2,1)S(1)}, bf16[8,128,256]{2,1,0:T(8,128)(2,1)S(1)}) custom-call(s32[1]{0:T(128)} %constant.143.clone.1.base_ref, s32[8,1,256]{2,1,0:T(1,128)S(1)} %bitcast.134, bf16[8,128,256]{2,1,0:T(8,128)(2,1)S(1)} %copy-done.9, bf16[8,128,256]{2,1,0:T(8,128)(2,1)S(1)} %copy-done.7, bf16[8,128,256]{2,1,0:T(8,128)(2,1)S(1)} %copy-done.17, ...), custom_call_target="tpu_custom_call" | custom-call | flops 6000000000 | bytes 8388608 | tf_op jit(solution)/shard_map/attend_back/pallas_call | solution.py:378
  332.0 4.5 %all-to-all-start.4 = ((bf16[8,256,256]{2,1,0:T(8,128)(2,1)}), bf16[8,256,256]{2,1,0:T(8,128)(2,1)}, u32[]{:S(2)}, u32[]{:S(2)}) async-start(bf16[8,256,256]{2,1,0:T(8,128)(2,1)} %pad_maximum_fusion.3), calls=%async_computation.4 | async-start | bytes 2097152 | tf_op jit(solution)/shard_map/all_to_all | solution.py:510
  340.4 2.0 collective-permute-start.43
  345.4 9.6 %collective-permute-done.43 = bf16[4,32,1024]{2,1,0:T(8,128)(2,1)S(1)} collective-permute-done((bf16[4,32,1024]{2,1,0:T(8,128)(2,1)S(1)}, bf16[4,32,1024]{2,1,0:T(8,128)(2,1)S(1)}, u32[]{:S(2)}, u32[]{:S(2)}) %collective-permute-start.43) | collective-permute-done | bytes 262176 | tf_op jit(solution)/shard_map/ppermute | solution.py:29
  355.8 5.4 %collective-permute-done.41 = bf16[128,1024]{1,0:T(8,128)(2,1)S(1)} collective-permute-done((bf16[128,1024]{1,0:T(8,128)(2,1)S(1)}, bf16[128,1024]{1,0:T(8,128)(2,1)S(1)}, u32[]{:S(2)}, u32[]{:S(2)}) %collective-permute-start.41) | collective-permute-done | bytes 262176 | tf_op jit(solution)/shard_map/ppermute | solution.py:29
  363.9 2.2 prepare_back.1
  367.1 3.0 convolution_convert_fusion
  370.7 1.9 slice_convert_fusion
  372.7 1.9 slice_bitcast_fusion
  374.7 2.3 convert_add_fusion
  383.8 3.5 all-to-all-start.6
  387.4 2.6 fusion.6
  390.0 3.6 collective-permute-done.46
  398.5 2.8 all-to-all-done.6.in_ref
  402.6 2.4 collective-permute-done.47
  408.0 4.5 %all-to-all-start.5 = ((f32[32,1,192]{2,1,0:T(1,128)}), f32[32,1,192]{2,1,0:T(1,128)S(1)}, u32[]{:S(2)}, u32[]{:S(2)}) async-start(f32[32,1,192]{2,1,0:T(1,128)} %all_to_all.29), calls=%async_computation.6 | async-start | bytes 65536 | tf_op jit(solution)/shard_map/all_to_all | solution.py:716
  413.7 1.8 collective-permute-start.49
  415.5 2.4 collective-permute-start.50
  421.0 2.4 collective-permute-done.49
  423.4 7.7 %collective-permute-done.50 = bf16[32,3072]{1,0:T(8,128)(2,1)S(1)} collective-permute-done((bf16[32,3072]{1,0:T(8,128)(2,1)S(1)}, bf16[32,3072]{1,0:T(8,128)(2,1)S(1)}, u32[]{:S(2)}, u32[]{:S(2)}) %collective-permute-start.50) | collective-permute-done | bytes 196640 | tf_op jit(solution)/shard_map/ppermute | solution.py:44
  (340 shorter events, 118.7 us)
Async XLA Ops:
  12.0 11.9 %collective-permute-start = (bf16[32,2176]{1,0:T(8,128)(2,1)S(1)}, bf16[32,2176]{1,0:T(8,128)(2,1)S(1)}, u32[]{:S(2)}, u32[]{:S(2)}) collective-permute-start(bf16[32,2176]{1,0:T(8,128)(2,1)S(1)} %fusion.33), channel_id=1, source_target_pairs={{0,8},{8,16},{16,24},{24,0},{1,9},{9,17},{17,25},{25,1},{2,10},{10... | collective-permute-start | bytes 417800 | tf_op jit(solution)/shard_map/ppermute | solution.py:44
  15.0 11.8 %collective-permute-start.1 = (bf16[32,2176]{1,0:T(8,128)(2,1)S(1)}, bf16[32,2176]{1,0:T(8,128)(2,1)S(1)}, u32[]{:S(2)}, u32[]{:S(2)}) collective-permute-start(bf16[32,2176]{1,0:T(8,128)(2,1)S(1)} %fusion.33), channel_id=1, source_target_pairs={{0,16},{8,24},{16,0},{24,8},{1,17},{9,25},{17,1},{25,9},{2,18},{10... | collective-permute-start | bytes 417800 | tf_op jit(solution)/shard_map/ppermute | solution.py:44
  17.6 9.2 %collective-permute-start.2 = (bf16[32,2176]{1,0:T(8,128)(2,1)S(1)}, bf16[32,2176]{1,0:T(8,128)(2,1)S(1)}, u32[]{:S(2)}, u32[]{:S(2)}) collective-permute-start(bf16[32,2176]{1,0:T(8,128)(2,1)S(1)} %fusion.33), channel_id=1, source_target_pairs={{0,24},{8,0},{16,8},{24,16},{1,25},{9,1},{17,9},{25,17},{2,26},{10... | collective-permute-start | bytes 417800 | tf_op jit(solution)/shard_map/ppermute | solution.py:44
  19.0 20.1 %all-to-all-start = ((bf16[8,32,1152]{2,1,0:T(8,128)(2,1)}), bf16[8,32,1152]{2,1,0:T(8,128)(2,1)S(1)}, u32[]{:S(2)}, u32[]{:S(2)}) async-start(bf16[8,32,1152]{2,1,0:T(8,128)(2,1)} %spread.1), calls=%async_computation | async-start | bytes 1179648 | tf_op jit(solution)/shard_map/all_to_all | solution.py:506
  22.7 103.7 %all-gather.4.cloned.1.call-start = ((), (), s32[]{:S(2)}) async-start(), calls=%async_computation.8 | async-start | bytes 2162688 | tf_op jit(solution)/shard_map/all_gather | solution.py:578
  23.4 149.2 %all-gather.6.cloned.1.call-start = ((), (), s32[]{:S(2)}) async-start(), calls=%async_computation.10 | async-start | bytes 4608000 | tf_op jit(solution)/shard_map/all_gather | solution.py:579
  26.9 11.4 %collective-permute-start.3 = (bf16[4,32,1024]{2,1,0:T(8,128)(2,1)S(1)}, bf16[4,32,1024]{2,1,0:T(8,128)(2,1)S(1)}, u32[]{:S(2)}, u32[]{:S(2)}) collective-permute-start(bf16[4,32,1024]{2,1,0:T(8,128)(2,1)S(1)} %get-tuple-element.167), channel_id=1, source_target_pairs={{0,4},{4,0},{1,5},{5,1},{2,6},{6,2},{3,7},{7,3},{8,12},{12,8},{9,1... | collective-permute-start | bytes 786440 | tf_op jit(solution)/shard_map/ppermute | solution.py:29
  28.5 10.5 %collective-permute-start.6 = (bf16[4,32,1152]{2,1,0:T(8,128)(2,1)S(1)}, bf16[4,32,1152]{2,1,0:T(8,128)(2,1)S(1)}, u32[]{:S(2)}, u32[]{:S(2)}) collective-permute-start(bf16[4,32,1152]{2,1,0:T(8,128)(2,1)S(1)} %get-tuple-element.165), channel_id=1, source_target_pairs={{0,2},{2,0},{1,3},{3,1},{4,6},{6,4},{5,7},{7,5},{8,10},{10,8},{9,1... | collective-permute-start | bytes 884744 | tf_op jit(solution)/shard_map/ppermute | solution.py:29
  40.2 16.8 %collective-permute-start.7 = (bf16[4,2,32,1152]{3,2,1,0:T(8,128)(2,1)S(1)}, bf16[4,2,32,1152]{3,2,1,0:T(8,128)(2,1)S(1)}, u32[]{:S(2)}, u32[]{:S(2)}) collective-permute-start(bf16[4,2,32,1152]{3,2,1,0:T(8,128)(2,1)S(1)} %maximum_select_fusion.5), channel_id=1, source_target_pairs={{0,4},{4,0},{1,5},{5,1},{2,6},{6,2},{3,7},{7,3},{8,12},{12,8},{9,1... | collective-permute-start | bytes 1769480 | tf_op jit(solution)/shard_map/ppermute | solution.py:29
  41.6 14.2 %collective-permute-start.4 = (bf16[4,2,32,1024]{3,2,0,1:T(8,128)(2,1)S(1)}, bf16[4,2,32,1024]{3,2,0,1:T(8,128)(2,1)S(1)}, u32[]{:S(2)}, u32[]{:S(2)}) collective-permute-start(bf16[4,2,32,1024]{3,2,0,1:T(8,128)(2,1)S(1)} %maximum_select_fusion.6), channel_id=1, source_target_pairs={{0,2},{2,0},{1,3},{3,1},{4,6},{6,4},{5,7},{7,5},{8,10},{10,8},{9,1... | collective-permute-start | bytes 1572872 | tf_op jit(solution)/shard_map/ppermute | solution.py:29
  67.6 35.7 %all-to-all-start.1 = ((bf16[8,256,256]{2,1,0:T(8,128)(2,1)}), bf16[8,256,256]{2,1,0:T(8,128)(2,1)}, u32[]{:S(2)}, u32[]{:S(2)}) async-start(bf16[8,256,256]{2,1,0:T(8,128)(2,1)} %copy-done.13), calls=%async_computation.1 | async-start | bytes 2097152 | tf_op jit(solution)/shard_map/all_to_all | solution.py:510
  121.1 32.6 %all-to-all-start.2 = ((bf16[8,128,256]{2,1,0:T(8,128)(2,1)}), bf16[8,128,256]{2,1,0:T(8,128)(2,1)}, u32[]{:S(2)}, u32[]{:S(2)}) async-start(bf16[8,128,256]{2,1,0:T(8,128)(2,1)} %copy-done.16), calls=%async_computation.2 | async-start | bytes 1048576 | tf_op jit(solution)/shard_map/all_to_all | solution.py:510
  125.2 237.3 %reduce-scatter.2.cloned.1.call-start = ((), (), s32[]{:S(2)}) async-start(), calls=%async_computation.9 | async-start | bytes 4608000 | tf_op jit(solution)/shard_map/reduce_scatter | solution.py:665
  126.4 42.4 %collective-permute-start.10 = (bf16[256,1024]{1,0:T(8,128)(2,1)S(1)}, bf16[256,1024]{1,0:T(8,128)(2,1)}, u32[]{:S(2)}, u32[]{:S(2)}) collective-permute-start(bf16[256,1024]{1,0:T(8,128)(2,1)S(1)} %bitcast.130), channel_id=1, source_target_pairs={{0,1},{1,0},{2,3},{3,2},{4,5},{5,4},{6,7},{7,6},{8,9},{9,8},{10,11... | collective-permute-start | bytes 1572872 | tf_op jit(solution)/shard_map/ppermute | solution.py:29
  157.1 13.5 %collective-permute-start.9 = (bf16[256,1024]{1,0:T(8,128)(2,1)S(1)}, bf16[256,1024]{1,0:T(8,128)(2,1)S(1)}, u32[]{:S(2)}, u32[]{:S(2)}) collective-permute-start(bf16[256,1024]{1,0:T(8,128)(2,1)S(1)} %multiply_convert_fusion.refs_0_), channel_id=1, source_target_pairs={{0,1},{1,0},{2,3},{3,2},{4,5},{5,4},{6,7},{7,6},{8,9},{9,8},{10,11... | collective-permute-start | bytes 1572872 | tf_op jit(solution)/shard_map/ppermute | solution.py:29
  157.9 9.5 %collective-permute-start.15 = (bf16[128,1024]{1,0:T(8,128)(2,1)S(1)}, bf16[128,1024]{1,0:T(8,128)(2,1)}, u32[]{:S(2)}, u32[]{:S(2)}) collective-permute-start(bf16[128,1024]{1,0:T(8,128)(2,1)S(1)} %get-tuple-element.173), channel_id=1, source_target_pairs={{0,4},{4,0},{1,5},{5,1},{2,6},{6,2},{3,7},{7,3},{8,12},{12,8},{9,1... | collective-permute-start | bytes 786440 | tf_op jit(solution)/shard_map/ppermute | solution.py:29
  160.1 21.3 %collective-permute-start.11 = (bf16[128,1024]{1,0:T(8,128)(2,1)}, bf16[128,1024]{1,0:T(8,128)(2,1)}, u32[]{:S(2)}, u32[]{:S(2)}) collective-permute-start(bf16[128,1024]{1,0:T(8,128)(2,1)} %get-tuple-element.175), channel_id=1, source_target_pairs={{0,4},{4,0},{1,5},{5,1},{2,6},{6,2},{3,7},{7,3},{8,12},{12,8},{9,1... | collective-permute-start | bytes 786440 | tf_op jit(solution)/shard_map/ppermute | solution.py:29
  166.0 15.8 %collective-permute-start.12 = (bf16[128,1024]{1,0:T(8,128)(2,1)}, bf16[128,1024]{1,0:T(8,128)(2,1)}, u32[]{:S(2)}, u32[]{:S(2)}) collective-permute-start(bf16[128,1024]{1,0:T(8,128)(2,1)} %get-tuple-element.174), channel_id=1, source_target_pairs={{0,2},{2,0},{1,3},{3,1},{4,6},{6,4},{5,7},{7,5},{8,10},{10,8},{9,1... | collective-permute-start | bytes 786440 | tf_op jit(solution)/shard_map/ppermute | solution.py:29
  167.4 18.5 %collective-permute-start.24 = (bf16[256,1024]{1,0:T(8,128)(2,1)}, bf16[256,1024]{1,0:T(8,128)(2,1)}, u32[]{:S(2)}, u32[]{:S(2)}) collective-permute-start(bf16[256,1024]{1,0:T(8,128)(2,1)} %pad_maximum_fusion.7), channel_id=1, source_target_pairs={{0,4},{4,0},{1,5},{5,1},{2,6},{6,2},{3,7},{7,3},{8,12},{12,8},{9,1... | collective-permute-start | bytes 1572872 | tf_op jit(solution)/shard_map/ppermute | solution.py:29
  168.8 16.2 %collective-permute-start.17 = (bf16[128,1024]{1,0:T(8,128)(2,1)}, bf16[128,1024]{1,0:T(8,128)(2,1)}, u32[]{:S(2)}, u32[]{:S(2)}) collective-permute-start(bf16[128,1024]{1,0:T(8,128)(2,1)} %collective-permute-done.15.refs_4_), channel_id=1, source_target_pairs={{0,1},{1,0},{2,3},{3,2},{4,5},{5,4},{6,7},{7,6},{8,9},{9,8},{10,11... | collective-permute-start | bytes 786440 | tf_op jit(solution)/shard_map/ppermute | solution.py:29
  171.4 15.0 %collective-permute-start.23 = (bf16[256,1024]{1,0:T(8,128)(2,1)}, bf16[256,1024]{1,0:T(8,128)(2,1)}, u32[]{:S(2)}, u32[]{:S(2)}) collective-permute-start(bf16[256,1024]{1,0:T(8,128)(2,1)} %pad_maximum_fusion.6), channel_id=1, source_target_pairs={{0,2},{2,0},{1,3},{3,1},{4,6},{6,4},{5,7},{7,5},{8,10},{10,8},{9,1... | collective-permute-start | bytes 1572872 | tf_op jit(solution)/shard_map/ppermute | solution.py:29
  183.1 14.1 %collective-permute-start.20 = (bf16[256,1024]{1,0:T(8,128)(2,1)S(1)}, bf16[256,1024]{1,0:T(8,128)(2,1)S(1)}, u32[]{:S(2)}, u32[]{:S(2)}) collective-permute-start(bf16[256,1024]{1,0:T(8,128)(2,1)S(1)} %pad_maximum_fusion.5), channel_id=1, source_target_pairs={{0,4},{4,0},{1,5},{5,1},{2,6},{6,2},{3,7},{7,3},{8,12},{12,8},{9,1... | collective-permute-start | bytes 1572872 | tf_op jit(solution)/shard_map/ppermute | solution.py:29
  185.0 13.8 %collective-permute-start.19 = (bf16[256,1024]{1,0:T(8,128)(2,1)S(1)}, bf16[256,1024]{1,0:T(8,128)(2,1)S(1)}, u32[]{:S(2)}, u32[]{:S(2)}) collective-permute-start(bf16[256,1024]{1,0:T(8,128)(2,1)S(1)} %pad_maximum_fusion.4), channel_id=1, source_target_pairs={{0,2},{2,0},{1,3},{3,1},{4,6},{6,4},{5,7},{7,5},{8,10},{10,8},{9,1... | collective-permute-start | bytes 1572872 | tf_op jit(solution)/shard_map/ppermute | solution.py:29
  186.4 13.0 %collective-permute-start.26 = (bf16[256,1024]{1,0:T(8,128)(2,1)}, bf16[256,1024]{1,0:T(8,128)(2,1)S(1)}, u32[]{:S(2)}, u32[]{:S(2)}) collective-permute-start(bf16[256,1024]{1,0:T(8,128)(2,1)} %collective-permute-done.24.refs_5_), channel_id=1, source_target_pairs={{0,1},{1,0},{2,3},{3,2},{4,5},{5,4},{6,7},{7,6},{8,9},{9,8},{10,11... | collective-permute-start | bytes 1572872 | tf_op jit(solution)/shard_map/ppermute | solution.py:29
  187.6 11.7 %collective-permute-start.25 = (bf16[256,1024]{1,0:T(8,128)(2,1)}, bf16[256,1024]{1,0:T(8,128)(2,1)S(1)}, u32[]{:S(2)}, u32[]{:S(2)}) collective-permute-start(bf16[256,1024]{1,0:T(8,128)(2,1)} %collective-permute-done.23.refs_4_), channel_id=1, source_target_pairs={{0,1},{1,0},{2,3},{3,2},{4,5},{5,4},{6,7},{7,6},{8,9},{9,8},{10,11... | collective-permute-start | bytes 1572872 | tf_op jit(solution)/shard_map/ppermute | solution.py:29
  214.1 20.6 %collective-permute-start.30 = (bf16[256,1024]{1,0:T(8,128)(2,1)}, bf16[256,1024]{1,0:T(8,128)(2,1)}, u32[]{:S(2)}, u32[]{:S(2)}) collective-permute-start(bf16[256,1024]{1,0:T(8,128)(2,1)} %get-tuple-element.90), channel_id=1, source_target_pairs={{0,1},{1,0},{2,3},{3,2},{4,5},{5,4},{6,7},{7,6},{8,9},{9,8},{10,11... | collective-permute-start | bytes 1572872 | tf_op jit(solution)/shard_map/ppermute | solution.py:29
  218.6 17.5 %collective-permute-start.29 = (bf16[256,1024]{1,0:T(8,128)(2,1)}, bf16[256,1024]{1,0:T(8,128)(2,1)}, u32[]{:S(2)}, u32[]{:S(2)}) collective-permute-start(bf16[256,1024]{1,0:T(8,128)(2,1)} %get-tuple-element.157), channel_id=1, source_target_pairs={{0,2},{2,0},{1,3},{3,1},{4,6},{6,4},{5,7},{7,5},{8,10},{10,8},{9,1... | collective-permute-start | bytes 1572872 | tf_op jit(solution)/shard_map/ppermute | solution.py:29
  219.0 18.2 %collective-permute-start.32 = (bf16[256,1024]{1,0:T(8,128)(2,1)}, bf16[256,1024]{1,0:T(8,128)(2,1)}, u32[]{:S(2)}, u32[]{:S(2)}) collective-permute-start(bf16[256,1024]{1,0:T(8,128)(2,1)} %get-tuple-element.158), channel_id=1, source_target_pairs={{0,4},{4,0},{1,5},{5,1},{2,6},{6,2},{3,7},{7,3},{8,12},{12,8},{9,1... | collective-permute-start | bytes 1572872 | tf_op jit(solution)/shard_map/ppermute | solution.py:29
  241.3 9.0 %collective-permute-start.27 = (bf16[256,1024]{1,0:T(8,128)(2,1)}, bf16[256,1024]{1,0:T(8,128)(2,1)S(1)}, u32[]{:S(2)}, u32[]{:S(2)}) collective-permute-start(bf16[256,1024]{1,0:T(8,128)(2,1)} %copy-done.31), channel_id=1, source_target_pairs={{0,1},{1,0},{2,3},{3,2},{4,5},{5,4},{6,7},{7,6},{8,9},{9,8},{10,11... | collective-permute-start | bytes 1572872 | tf_op jit(solution)/shard_map/ppermute | solution.py:29
  241.3 8.9 %collective-permute-start.33 = (bf16[128,1024]{1,0:T(8,128)(2,1)}, bf16[128,1024]{1,0:T(8,128)(2,1)S(1)}, u32[]{:S(2)}, u32[]{:S(2)}) collective-permute-start(bf16[128,1024]{1,0:T(8,128)(2,1)} %get-tuple-element.156), channel_id=1, source_target_pairs={{0,2},{2,0},{1,3},{3,1},{4,6},{6,4},{5,7},{7,5},{8,10},{10,8},{9,1... | collective-permute-start | bytes 786440 | tf_op jit(solution)/shard_map/ppermute | solution.py:29
  253.4 24.0 %collective-permute-start.38 = (bf16[512,1024]{1,0:T(8,128)(2,1)}, bf16[512,1024]{1,0:T(8,128)(2,1)}, u32[]{:S(2)}, u32[]{:S(2)}) collective-permute-start(bf16[512,1024]{1,0:T(8,128)(2,1)} %convolution_convert_fusion.1), channel_id=1, source_target_pairs={{0,1},{1,0},{2,3},{3,2},{4,5},{5,4},{6,7},{7,6},{8,9},{9,8},{10,11... | collective-permute-start | bytes 3145736 | tf_op jit(solution)/shard_map/ppermute | solution.py:29
  267.7 37.9 %collective-permute-start.35 = (bf16[512,1024]{1,0:T(8,128)(2,1)}, bf16[512,1024]{1,0:T(8,128)(2,1)}, u32[]{:S(2)}, u32[]{:S(2)}) collective-permute-start(bf16[512,1024]{1,0:T(8,128)(2,1)} %get-tuple-element.120), channel_id=1, source_target_pairs={{0,1},{1,0},{2,3},{3,2},{4,5},{5,4},{6,7},{7,6},{8,9},{9,8},{10,11... | collective-permute-start | bytes 3145736 | tf_op jit(solution)/shard_map/ppermute | solution.py:29
  268.3 33.6 %all-to-all-start.3 = ((bf16[8,128,256]{2,1,0:T(8,128)(2,1)}), bf16[8,128,256]{2,1,0:T(8,128)(2,1)}, u32[]{:S(2)}, u32[]{:S(2)}) async-start(bf16[8,128,256]{2,1,0:T(8,128)(2,1)} %bitcast.155), calls=%async_computation.3 | async-start | bytes 1048576 | tf_op jit(solution)/shard_map/all_to_all | solution.py:510
  304.0 35.1 %collective-permute-start.39 = (bf16[4,2,32,1024]{3,2,1,0:T(8,128)(2,1)}, bf16[4,2,32,1024]{3,2,1,0:T(8,128)(2,1)}, u32[]{:S(2)}, u32[]{:S(2)}) collective-permute-start(bf16[4,2,32,1024]{3,2,1,0:T(8,128)(2,1)} %fusion.16), channel_id=1, source_target_pairs={{0,2},{2,0},{1,3},{3,1},{4,6},{6,4},{5,7},{7,5},{8,10},{10,8},{9,1... | collective-permute-start | bytes 1572872 | tf_op jit(solution)/shard_map/ppermute | solution.py:29
  308.8 27.8 %collective-permute-start.36 = (bf16[256,1024]{1,0:T(8,128)(2,1)}, bf16[256,1024]{1,0:T(8,128)(2,1)}, u32[]{:S(2)}, u32[]{:S(2)}) collective-permute-start(bf16[256,1024]{1,0:T(8,128)(2,1)} %get-tuple-element.154), channel_id=1, source_target_pairs={{0,2},{2,0},{1,3},{3,1},{4,6},{6,4},{5,7},{7,5},{8,10},{10,8},{9,1... | collective-permute-start | bytes 1572872 | tf_op jit(solution)/shard_map/ppermute | solution.py:29
  309.1 28.7 %collective-permute-start.37 = (bf16[256,1024]{1,0:T(8,128)(2,1)}, bf16[256,1024]{1,0:T(8,128)(2,1)}, u32[]{:S(2)}, u32[]{:S(2)}) collective-permute-start(bf16[256,1024]{1,0:T(8,128)(2,1)} %get-tuple-element.153), channel_id=1, source_target_pairs={{0,4},{4,0},{1,5},{5,1},{2,6},{6,2},{3,7},{7,3},{8,12},{12,8},{9,1... | collective-permute-start | bytes 1572872 | tf_op jit(solution)/shard_map/ppermute | solution.py:29
  332.0 30.5 %all-to-all-start.4 = ((bf16[8,256,256]{2,1,0:T(8,128)(2,1)}), bf16[8,256,256]{2,1,0:T(8,128)(2,1)}, u32[]{:S(2)}, u32[]{:S(2)}) async-start(bf16[8,256,256]{2,1,0:T(8,128)(2,1)} %pad_maximum_fusion.3), calls=%async_computation.4 | async-start | bytes 2097152 | tf_op jit(solution)/shard_map/all_to_all | solution.py:510
  340.4 14.5 %collective-permute-start.43 = (bf16[4,32,1024]{2,1,0:T(8,128)(2,1)S(1)}, bf16[4,32,1024]{2,1,0:T(8,128)(2,1)S(1)}, u32[]{:S(2)}, u32[]{:S(2)}) collective-permute-start(bf16[4,32,1024]{2,1,0:T(8,128)(2,1)S(1)} %fusion.28), channel_id=1, source_target_pairs={{0,4},{4,0},{1,5},{5,1},{2,6},{6,2},{3,7},{7,3},{8,12},{12,8},{9,1... | collective-permute-start | bytes 786440 | tf_op jit(solution)/shard_map/ppermute | solution.py:29
  342.6 18.6 %collective-permute-start.41 = (bf16[128,1024]{1,0:T(8,128)(2,1)S(1)}, bf16[128,1024]{1,0:T(8,128)(2,1)S(1)}, u32[]{:S(2)}, u32[]{:S(2)}) collective-permute-start(bf16[128,1024]{1,0:T(8,128)(2,1)S(1)} %get-tuple-element.151), channel_id=1, source_target_pairs={{0,4},{4,0},{1,5},{5,1},{2,6},{6,2},{3,7},{7,3},{8,12},{12,8},{9,1... | collective-permute-start | bytes 786440 | tf_op jit(solution)/shard_map/ppermute | solution.py:29
  343.6 17.8 %collective-permute-start.34 = (bf16[256,1024]{1,0:T(8,128)(2,1)S(1)}, bf16[256,1024]{1,0:T(8,128)(2,1)S(1)}, u32[]{:S(2)}, u32[]{:S(2)}) collective-permute-start(bf16[256,1024]{1,0:T(8,128)(2,1)S(1)} %copy-done.33), channel_id=1, source_target_pairs={{0,1},{1,0},{2,3},{3,2},{4,5},{5,4},{6,7},{7,6},{8,9},{9,8},{10,11... | collective-permute-start | bytes 1572872 | tf_op jit(solution)/shard_map/ppermute | solution.py:29
  343.6 17.7 %collective-permute-start.42 = (bf16[128,1024]{1,0:T(8,128)(2,1)S(1)}, bf16[128,1024]{1,0:T(8,128)(2,1)S(1)}, u32[]{:S(2)}, u32[]{:S(2)}) collective-permute-start(bf16[128,1024]{1,0:T(8,128)(2,1)S(1)} %get-tuple-element.152), channel_id=1, source_target_pairs={{0,2},{2,0},{1,3},{3,1},{4,6},{6,4},{5,7},{7,5},{8,10},{10,8},{9,1... | collective-permute-start | bytes 786440 | tf_op jit(solution)/shard_map/ppermute | solution.py:29
  378.5 15.0 %collective-permute-start.46 = (bf16[4,2,32,1024]{3,2,0,1:T(8,128)(2,1)}, bf16[4,2,32,1024]{3,2,0,1:T(8,128)(2,1)}, u32[]{:S(2)}, u32[]{:S(2)}) collective-permute-start(bf16[4,2,32,1024]{3,2,0,1:T(8,128)(2,1)} %fusion.18), channel_id=1, source_target_pairs={{0,2},{2,0},{1,3},{3,1},{4,6},{6,4},{5,7},{7,5},{8,10},{10,8},{9,1... | collective-permute-start | bytes 1572872 | tf_op jit(solution)/shard_map/ppermute | solution.py:29
  380.1 14.9 %collective-permute-start.45 = (bf16[4,2,32,1024]{3,2,0,1:T(8,128)(2,1)S(1)}, bf16[4,2,32,1024]{3,2,0,1:T(8,128)(2,1)}, u32[]{:S(2)}, u32[]{:S(2)}) collective-permute-start(bf16[4,2,32,1024]{3,2,0,1:T(8,128)(2,1)S(1)} %fusion.17), channel_id=1, source_target_pairs={{0,4},{4,0},{1,5},{5,1},{2,6},{6,2},{3,7},{7,3},{8,12},{12,8},{9,1... | collective-permute-start | bytes 1572872 | tf_op jit(solution)/shard_map/ppermute | solution.py:29
  383.8 17.5 %all-to-all-start.6 = ((bf16[8,32,1152]{2,1,0:T(8,128)(2,1)}), bf16[8,32,1152]{2,1,0:T(8,128)(2,1)S(1)}, u32[]{:S(2)}, u32[]{:S(2)}) async-start(bf16[8,32,1152]{2,1,0:T(8,128)(2,1)} %bitcast.69), calls=%async_computation.7 | async-start | bytes 1179648 | tf_op jit(solution)/shard_map/all_to_all | solution.py:506
  408.0 11.8 %all-to-all-start.5 = ((f32[32,1,192]{2,1,0:T(1,128)}), f32[32,1,192]{2,1,0:T(1,128)S(1)}, u32[]{:S(2)}, u32[]{:S(2)}) async-start(f32[32,1,192]{2,1,0:T(1,128)} %all_to_all.29), calls=%async_computation.6 | async-start | bytes 65536 | tf_op jit(solution)/shard_map/all_to_all | solution.py:716
  413.7 9.7 %collective-permute-start.49 = (bf16[32,3072]{1,0:T(8,128)(2,1)S(1)}, bf16[32,3072]{1,0:T(8,128)(2,1)S(1)}, u32[]{:S(2)}, u32[]{:S(2)}) collective-permute-start(bf16[32,3072]{1,0:T(8,128)(2,1)S(1)} %get-tuple-element.161), channel_id=1, source_target_pairs={{0,8},{8,16},{16,24},{24,0},{1,9},{9,17},{17,25},{25,1},{2,10},{10... | collective-permute-start | bytes 589832 | tf_op jit(solution)/shard_map/ppermute | solution.py:44
  415.5 15.6 %collective-permute-start.50 = (bf16[32,3072]{1,0:T(8,128)(2,1)S(1)}, bf16[32,3072]{1,0:T(8,128)(2,1)S(1)}, u32[]{:S(2)}, u32[]{:S(2)}) collective-permute-start(bf16[32,3072]{1,0:T(8,128)(2,1)S(1)} %get-tuple-element.163), channel_id=1, source_target_pairs={{0,16},{8,24},{16,0},{24,8},{1,17},{9,25},{17,1},{25,9},{2,18},{10... | collective-permute-start | bytes 589832 | tf_op jit(solution)/shard_map/ppermute | solution.py:44
  417.9 13.2 %collective-permute-start.51 = (bf16[32,3072]{1,0:T(8,128)(2,1)S(1)}, bf16[32,3072]{1,0:T(8,128)(2,1)S(1)}, u32[]{:S(2)}, u32[]{:S(2)}) collective-permute-start(bf16[32,3072]{1,0:T(8,128)(2,1)S(1)} %get-tuple-element.162), channel_id=1, source_target_pairs={{0,24},{8,0},{16,8},{24,16},{1,25},{9,1},{17,9},{25,17},{2,26},{10... | collective-permute-start | bytes 589832 | tf_op jit(solution)/shard_map/ppermute | solution.py:44
  (81 other events, 494.4 us)
Sparse Core Ops, SparseCore 0:
  26.4 55.9 all-gather.3
  84.0 87.5 all-gather.5
  234.8 77.3 reduce-scatter.1
